TPU v7x, 128 devices: a whole 4x4x4 slice. The times are simulated.
128 devices in a mesh: ia: 8 (over z, y_hi), ja: 8 (over x, y_lo), sa: 2 (over core).
Axes of the slice: x: 4, y: 4 (y_hi: 2, y_lo: 2; y = y_hi * 2 + y_lo), z: 4, core: 2. Of those that a mesh axis runs over, the one named last changes fastest.
Arguments:
- alignment_features: bfloat16 [128, 1024, 256], P('sa', 'ia'), may hold values from -90 to 90
- norm_gain_vector: float32 [256], replicated, may hold values from 0.25 to 1.75
- norm_offset_vector: float32 [256], replicated, may hold values from -1.8 to 1.8
- projection_weight: bfloat16 [256, 64], replicated, may hold values from -0.75 to 0.75
- output_weight: bfloat16 [1024, 128], replicated, may hold values from -0.1875 to 0.1875
- output_bias: float32 [128], replicated, may hold values from -1.8 to 1.8
- pair_update_cotangent: bfloat16 [1024, 1024, 128], P(('ia', 'sa'), 'ja'), may hold values from -6 to 6
Outputs:
- pair_update_result: bfloat16 [1024, 1024, 128], P(('ia', 'sa'), 'ja')
- alignment_gradient: bfloat16 [128, 1024, 256], P('sa', 'ia')
- projection_weight_gradient: float32 [256, 64], replicated
- out_weight_grad: float32 [1024, 128], replicated
- out_bias_grad: float32 [128], replicated
All inputs are finite; a program needn't handle non-finite values.
Results may differ from a plain program's by a relative error of at most 0.025.
Values may be sent and summed in bfloat16 or wider, within the bound.
No kernel may reach another device: no remote copies, remote signals or barrier semaphores. Data moves between devices by JAX's collectives and lax.ppermute only.
A program may use at most 128 MiB of HBM per device.

v0:
```python
import jax
import jax.numpy as jnp
from jax import lax
from jax.experimental import pallas as pl
from jax.experimental.pallas import tpu as pltpu
from jax.sharding import PartitionSpec as P

epsilon = 1e-05
AXES = ("ia", "ja", "sa")
RING = 4
SWAP_Y = (0, 2, 1, 3)
ROWS_AT_ONCE = 8
BF16 = jnp.bfloat16
F32 = jnp.float32
VMEM_LIMIT = 48 * 1024 * 1024


def dot(a, b, contract):
    return lax.dot_general(a, b, (contract, ((), ())), preferred_element_type=F32)


def params():
    return pltpu.CompilerParams(
        dimension_semantics=("arbitrary",), vmem_limit_bytes=VMEM_LIMIT
    )


def whole(shape):
    return pl.BlockSpec(shape, lambda *_: (0,) * len(shape))


def norm_rows(features):
    values = features.astype(F32)
    scale = 1.0 / values.shape[-1]
    centred = values - jnp.sum(values, axis=-1, keepdims=True) * scale
    variance = jnp.sum(centred * centred, axis=-1, keepdims=True) * scale
    inverse_deviation = lax.rsqrt(variance + epsilon)
    return centred * inverse_deviation, inverse_deviation


def project_kernel(features_ref, gain_ref, offset_ref, weight_ref, out_ref):
    seqs, residues, channels = features_ref.shape
    width = weight_ref.shape[0]
    for s in range(0, seqs, 2):
        rescaled, _ = norm_rows(features_ref[s : s + 2].reshape(2 * residues, channels))
        normed = (rescaled * gain_ref[...] + offset_ref[...]).astype(BF16)
        both = dot(weight_ref[...], normed, ((1,), (1,))).astype(BF16)
        out_ref[s] = both[:, :residues]
        out_ref[s + 1] = both[:, residues:]


def project(features, gain, offset, weight, seqs):
    count, residues, channels = features.shape
    width = weight.shape[0]
    return pl.pallas_call(
        project_kernel,
        grid=(count // seqs,),
        in_specs=[
            pl.BlockSpec((seqs, residues, channels), lambda n: (n, 0, 0)),
            whole((1, channels)),
            whole((1, channels)),
            whole((width, channels)),
        ],
        out_specs=pl.BlockSpec((seqs, width, residues), lambda n: (n, 0, 0)),
        out_shape=jax.ShapeDtypeStruct((count, width, residues), BF16),
        compiler_params=params(),
        cost_estimate=pl.CostEstimate(
            flops=2 * count * residues * channels * width,
            bytes_accessed=2 * count * residues * (channels + width),
            transcendentals=count * residues,
        ),
        name="project",
    )(features, gain.reshape(1, -1), offset.reshape(1, -1), weight)


def outer_grad_kernel(cot_ref, weight_ref, left_ref, grad_ref, right_ref, bias_ref, total_ref):
    step = pl.program_id(0)
    rows, cols, pair_channels = cot_ref.shape
    width = grad_ref.shape[1]

    @pl.when(step == 0)
    def _():
        total_ref[...] = jnp.zeros_like(total_ref)
        bias_ref[...] = jnp.zeros_like(bias_ref)

    bias_ref[...] += jnp.sum(
        cot_ref[...].astype(F32).reshape(rows * cols // 8, 8, pair_channels), axis=0
    )
    for i in range(0, rows, 2):
        cot = cot_ref[i : i + 2].reshape(2 * cols, pair_channels)
        grad = dot(weight_ref[...], cot, ((1,), (1,))).astype(BF16)
        grad = grad.reshape(width, width, 2 * cols)
        grad_ref[0, :, i * width : (i + 1) * width, :] = grad[:, :, :cols]
        grad_ref[0, :, (i + 1) * width : (i + 2) * width, :] = grad[:, :, cols:]
    left = left_ref[...].T
    for d in range(0, width, 2):
        both = jnp.concatenate([grad_ref[0, d], grad_ref[0, d + 1]], axis=1)
        total_ref[:, d * cols : (d + 2) * cols] += dot(left, both, ((1,), (0,)))

    @pl.when(step == pl.num_programs(0) - 1)
    def _():
        right_ref[...] = total_ref[...].astype(BF16)


def outer_grad_and_right(cotangent, weight, left):
    rows, cols, pair_channels = cotangent.shape
    seqs = left.shape[1]
    width = left.shape[0] // rows
    blocks = rows // ROWS_AT_ONCE
    block = ROWS_AT_ONCE * width
    return pl.pallas_call(
        outer_grad_kernel,
        grid=(blocks,),
        in_specs=[
            pl.BlockSpec((ROWS_AT_ONCE, cols, pair_channels), lambda n: (n, 0, 0)),
            whole((width * width, pair_channels)),
            pl.BlockSpec((block, seqs), lambda n: (n, 0)),
        ],
        out_specs=[
            pl.BlockSpec((1, width, block, cols), lambda n: (n, 0, 0, 0)),
            whole((seqs, width * cols)),
            whole((8, pair_channels)),
        ],
        out_shape=[
            jax.ShapeDtypeStruct((blocks, width, block, cols), BF16),
            jax.ShapeDtypeStruct((seqs, width * cols), BF16),
            jax.ShapeDtypeStruct((8, pair_channels), F32),
        ],
        scratch_shapes=[pltpu.VMEM((seqs, width * cols), F32)],
        compiler_params=params(),
        cost_estimate=pl.CostEstimate(
            flops=4 * rows * cols * width * width * pair_channels,
            bytes_accessed=2 * rows * cols * (pair_channels + width * width),
            transcendentals=0,
        ),
        name="outer_grad",
    )(cotangent, weight, left)


def fill(whole_ref, piece_refs):
    first = 0
    for piece in piece_refs:
        count = piece.shape[0]
        whole_ref[first : first + count, :] = piece[...]
        first += count


def left_grad_kernel(*refs):
    piece_refs, (grad_ref, out_ref, cols_ref) = refs[:-3], refs[-3:]
    _, width, _, cols = grad_ref.shape

    @pl.when(pl.program_id(0) == 0)
    def _():
        for d in range(width):
            here = slice(d * cols, (d + 1) * cols)
            part = jnp.concatenate([piece[:, here] for piece in piece_refs], axis=0)
            cols_ref[here, :] = part.T

    total = None
    for d in range(0, width, 2):
        both = jnp.concatenate([grad_ref[0, d], grad_ref[0, d + 1]], axis=1)
        term = dot(both, cols_ref[d * cols : (d + 2) * cols, :], ((1,), (0,)))
        total = term if total is None else total + term
    out_ref[...] = total.T.astype(BF16)


def left_grad_part(pieces, outer_grad):
    blocks, width, block, cols = outer_grad.shape
    seqs = sum(piece.shape[0] for piece in pieces)
    return pl.pallas_call(
        left_grad_kernel,
        grid=(blocks,),
        in_specs=[whole(piece.shape) for piece in pieces]
        + [pl.BlockSpec((1, width, block, cols), lambda n: (n, 0, 0, 0))],
        out_specs=pl.BlockSpec((seqs, block), lambda n: (0, n)),
        out_shape=jax.ShapeDtypeStruct((seqs, blocks * block), BF16),
        scratch_shapes=[pltpu.VMEM((width * cols, seqs), BF16)],
        compiler_params=params(),
        cost_estimate=pl.CostEstimate(
            flops=2 * blocks * width * block * cols * seqs,
            bytes_accessed=2 * blocks * width * block * cols,
            transcendentals=0,
        ),
        name="left_grad",
    )(*pieces, outer_grad)


def pair_kernel(*refs):
    piece_refs, refs = refs[:-9], refs[-9:]
    left_ref, weight_ref, bias_ref, cot_ref, pair_ref, grad_ref = refs[:6]
    cols_ref, outer_ref, total_ref = refs[6:]
    step = pl.program_id(0)
    rows, cols, pair_channels = cot_ref.shape
    width = outer_ref.shape[0]
    inv_seqs = 1.0 / cols_ref.shape[0]

    @pl.when(step == 0)
    def _():
        fill(cols_ref, piece_refs)
        total_ref[...] = jnp.zeros_like(total_ref)

    for d in range(0, width, 2):
        both = dot(left_ref[...], cols_ref[:, d * cols : (d + 2) * cols], ((1,), (0,)))
        both = (both * inv_seqs).astype(BF16)
        outer_ref[d] = both[:, :cols]
        outer_ref[d + 1] = both[:, cols:]
    for i in range(0, rows, 2):
        outer = jnp.concatenate(
            [
                outer_ref[:, n * width : (n + 1) * width, :].reshape(width * width, cols)
                for n in (i, i + 1)
            ],
            axis=1,
        )
        cot = cot_ref[i : i + 2].reshape(2 * cols, pair_channels)
        total_ref[...] += dot(outer, cot, ((1,), (0,)))
        pair = dot(weight_ref[...], outer, ((1,), (0,))).T + bias_ref[...]
        pair_ref[i : i + 2] = pair.astype(BF16).reshape(2, cols, pair_channels)

    @pl.when(step == pl.num_programs(0) - 1)
    def _():
        grad_ref[...] = total_ref[...].astype(BF16)


def pair_and_weight_grad(pieces, left, weight, bias, cotangent):
    rows, cols, pair_channels = cotangent.shape
    seqs = left.shape[1]
    width = left.shape[0] // rows
    blocks = rows // ROWS_AT_ONCE
    block = ROWS_AT_ONCE * width
    return pl.pallas_call(
        pair_kernel,
        grid=(blocks,),
        in_specs=[whole(piece.shape) for piece in pieces]
        + [
            pl.BlockSpec((block, seqs), lambda n: (n, 0)),
            whole((pair_channels, width * width)),
            whole((1, pair_channels)),
            pl.BlockSpec((ROWS_AT_ONCE, cols, pair_channels), lambda n: (n, 0, 0)),
        ],
        out_specs=[
            pl.BlockSpec((ROWS_AT_ONCE, cols, pair_channels), lambda n: (n, 0, 0)),
            whole((width * width, pair_channels)),
        ],
        out_shape=[
            jax.ShapeDtypeStruct((rows, cols, pair_channels), BF16),
            jax.ShapeDtypeStruct((width * width, pair_channels), BF16),
        ],
        scratch_shapes=[
            pltpu.VMEM((seqs, width * cols), BF16),
            pltpu.VMEM((width, block, cols), BF16),
            pltpu.VMEM((width * width, pair_channels), F32),
        ],
        compiler_params=params(),
        cost_estimate=pl.CostEstimate(
            flops=2 * rows * cols * width * width * (2 * pair_channels + seqs),
            bytes_accessed=4 * rows * cols * pair_channels,
            transcendentals=0,
        ),
        name="pair_update",
    )(*pieces, left, weight, bias.reshape(1, -1), cotangent)


def projection_grad_kernel(features_ref, gain_ref, offset_ref, left_ref, right_ref, out_ref):
    seqs = features_ref.shape[0]
    total = None
    for s in range(seqs):
        rescaled, _ = norm_rows(features_ref[s])
        normed = (rescaled * gain_ref[...] + offset_ref[...]).astype(BF16)
        grads = jnp.concatenate([left_ref[s], right_ref[s]], axis=0)
        term = dot(grads, normed, ((1,), (0,)))
        total = term if total is None else total + term
    out_ref[...] = total


def projection_grad_part(features, gain, offset, left, right):
    channels = features.shape[2]
    return pl.pallas_call(
        projection_grad_kernel,
        out_shape=jax.ShapeDtypeStruct((2 * left.shape[1], channels), F32),
        compiler_params=pltpu.CompilerParams(vmem_limit_bytes=VMEM_LIMIT),
        name="projection_grad",
    )(features, gain.reshape(1, -1), offset.reshape(1, -1), left, right)


def norm_grad_kernel(x_ref, *refs):
    left_refs, right_refs = refs[:RING], refs[RING : 2 * RING]
    features_ref, gain_ref, weight_ref, out_ref, grads_ref = refs[2 * RING :]
    step = pl.program_id(0)
    seqs = features_ref.shape[0]
    width = left_refs[0].shape[1]
    steps = left_refs[0].shape[0] // seqs
    for t in range(RING):

        @pl.when(step // steps == t)
        def _(t=t):
            here = pl.ds(lax.rem(step, steps) * seqs, seqs)
            grads_ref[:, :width, :] = left_refs[t][here]
            grads_ref[:, width:, :] = right_refs[t][here]

    channels = features_ref.shape[2]
    for s in range(seqs):
        rescaled, inverse_deviation = norm_rows(features_ref[s])
        grad = dot(grads_ref[s], weight_ref[...], ((0,), (0,))) * gain_ref[...]
        first = jnp.sum(grad, axis=-1, keepdims=True) * (1.0 / channels)
        cross = jnp.sum(grad * rescaled, axis=-1, keepdims=True) * (1.0 / channels)
        out_ref[s] = (inverse_deviation * (grad - first - rescaled * cross)).astype(BF16)


def norm_grad(x, left_pieces, right_pieces, features, gain, weight, seqs=8):
    count, residues, channels = features.shape
    quarter, width, _ = left_pieces[0].shape
    steps = quarter // seqs

    def place(n, x_ref):
        return (lax.rem(n // steps + x_ref[0], RING) * steps + lax.rem(n, steps), 0, 0)

    def all_of(shape):
        return pl.BlockSpec(shape, lambda n, x_ref: (0,) * len(shape))

    return pl.pallas_call(
        norm_grad_kernel,
        grid_spec=pltpu.PrefetchScalarGridSpec(
            num_scalar_prefetch=1,
            grid=(count // seqs,),
            in_specs=[all_of(left_pieces[0].shape)] * (2 * RING)
            + [
                pl.BlockSpec((seqs, residues, channels), place),
                all_of((1, channels)),
                all_of(weight.shape),
            ],
            out_specs=pl.BlockSpec((seqs, residues, channels), place),
            scratch_shapes=[pltpu.VMEM((seqs, 2 * width, residues), BF16)],
        ),
        out_shape=jax.ShapeDtypeStruct(features.shape, BF16),
        compiler_params=params(),
        cost_estimate=pl.CostEstimate(
            flops=4 * count * residues * channels * width,
            bytes_accessed=4 * count * residues * channels,
            transcendentals=count * residues,
        ),
        name="norm_grad",
    )(x.reshape(1), *left_pieces, *right_pieces, features, gain.reshape(1, -1), weight)


def torus_permute(value, move):
    pairs = []
    for z in range(RING):
        for y in range(RING):
            for x in range(RING):
                for s in range(2):
                    tx, ty, tz, ts = move(x, y, z, s)
                    tx, ty, tz = tx % RING, ty % RING, tz % RING
                    source = ((z * 2 + y // 2) * 8 + x * 2 + y % 2) * 2 + s
                    target = ((tz * 2 + ty // 2) * 8 + tx * 2 + ty % 2) * 2 + ts
                    pairs.append((source, target))
    return lax.ppermute(value, AXES, pairs)


def swap_cores(value):
    return torus_permute(value, lambda x, y, z, s: (x, y, z, 1 - s))


def swap_low_y(value):
    return torus_permute(value, lambda x, y, z, s: (x, y ^ 1, z, s))


def shift_z(value, steps):
    return torus_permute(value, lambda x, y, z, s: (x, y, z + steps, s))


def shift_x(value, steps):
    return torus_permute(value, lambda x, y, z, s: (x + steps, y, z, s))


def transpose_xz(value):
    return torus_permute(value, lambda x, y, z, s: (z, SWAP_Y[y], x, s))


def add_up(parts):
    total = parts[0].astype(F32)
    for part in parts[1:]:
        total = total + part.astype(F32)
    return total


def body(
    alignment_features,
    norm_gain_vector,
    norm_offset_vector,
    projection_weight,
    output_weight,
    output_bias,
    pair_update_cotangent,
):
    half, residues, channels = alignment_features.shape
    width = projection_weight.shape[1] // 2
    pair_channels = output_weight.shape[1]
    rows, cols, _ = pair_update_cotangent.shape
    rows_total = residues * lax.axis_size("ia")
    quarter = half // RING
    inv_seqs = 1.0 / (half * 2)
    x = lax.axis_index("ja") // 2
    low_y = lax.axis_index("ja") % 2
    z = lax.axis_index("ia") // 2
    core = lax.axis_index("sa")
    gain, offset = norm_gain_vector, norm_offset_vector
    weight_rows = projection_weight.T

    own_quarter = lax.dynamic_slice_in_dim(alignment_features, x * quarter, quarter, 0)
    right_piece = project(own_quarter, gain, offset, weight_rows[width:], quarter // 2)
    arrived = transpose_xz(right_piece.reshape(quarter, width * residues))
    right_pieces = [arrived] + [shift_z(arrived, -t) for t in range(1, RING)]
    right_cols = right_pieces + [swap_cores(piece) for piece in right_pieces]

    left = project(alignment_features, gain, offset, weight_rows[:width], 8)
    left = jnp.roll(left, -z * quarter, axis=0)
    left_kept = lax.dynamic_slice_in_dim(left, core * rows, rows, 2).transpose(2, 1, 0)
    left_sent = lax.dynamic_slice_in_dim(left, (1 - core) * rows, rows, 2)
    left_came = swap_cores(left_sent).transpose(2, 1, 0)
    own_left = jnp.concatenate([left_kept, left_came], axis=2).reshape(rows * width, 2 * half)

    weight_dc = (
        output_weight.reshape(width, width, pair_channels)
        .transpose(1, 0, 2)
        .reshape(width * width, pair_channels)
    )
    outer_grad, right_partial, bias_partial = outer_grad_and_right(
        pair_update_cotangent, weight_dc, own_left
    )

    right_sum = add_up([right_partial[:half], swap_cores(right_partial[half:])])
    pieces = [right_sum[t * quarter : (t + 1) * quarter].astype(BF16) for t in range(RING)]
    right_sum = add_up([pieces[0]] + [shift_z(pieces[t], t) for t in range(1, RING)])
    right_sum = transpose_xz(right_sum.astype(BF16))
    right_sum = add_up([right_sum, swap_low_y(right_sum)])
    right_grad = (right_sum * inv_seqs).astype(BF16).reshape(quarter, width, residues)
    right_grads = [right_grad] + [shift_x(right_grad, -t) for t in range(1, RING)]

    left_partial = left_grad_part(right_cols, outer_grad)
    left_all = jnp.concatenate([left_partial[:half], swap_cores(left_partial[half:])], axis=1)

    def left_quarter(t):
        place = lax.rem(x + t - z + RING, RING)
        return lax.dynamic_slice_in_dim(left_all, place * quarter, quarter, 0)

    left_sum = add_up([left_quarter(0)] + [shift_x(left_quarter(t), t) for t in range(1, RING)])
    left_sum = left_sum.astype(BF16)
    left_sum = add_up([left_sum, swap_low_y(left_sum)])
    left_sum = (left_sum * inv_seqs).astype(BF16).reshape(quarter, 2, rows, width)
    left_sum = jnp.where(core == 0, left_sum, left_sum[:, ::-1])
    left_grad = left_sum.reshape(quarter, residues, width).transpose(0, 2, 1)
    left_grads = [left_grad] + [shift_x(left_grad, -t) for t in range(1, RING)]

    pair_update_result, weight_partial = pair_and_weight_grad(
        right_cols, own_left, weight_dc.T, output_bias, pair_update_cotangent
    )
    devices = 128
    weight_share = jnp.sum(
        lax.all_to_all(
            weight_partial.reshape(devices, -1, pair_channels), AXES, 0, 0, tiled=True
        ).astype(F32),
        axis=0,
    )

    eighth = quarter // 2
    features_eighth = lax.dynamic_slice_in_dim(
        alignment_features, x * quarter + low_y * eighth, eighth, 0
    )
    projection_part = projection_grad_part(
        features_eighth,
        gain,
        offset,
        lax.dynamic_slice_in_dim(left_grad, low_y * eighth, eighth, 0),
        lax.dynamic_slice_in_dim(right_grad, low_y * eighth, eighth, 0),
    )
    small = jnp.concatenate(
        [
            projection_part.reshape(devices, -1),
            jnp.broadcast_to(jnp.sum(bias_partial, axis=0), (devices, pair_channels)),
        ],
        axis=1,
    ).reshape(devices, 2, pair_channels)
    small_share = jnp.sum(lax.all_to_all(small, AXES, 0, 0, tiled=True), axis=0)
    share = jnp.concatenate([weight_share, small_share], axis=0)
    everything = lax.all_to_all(
        jnp.broadcast_to(share, (devices, *share.shape)), AXES, 0, 0, tiled=True
    )
    weight_sum = (
        everything[:, :-2]
        .reshape(width, width, pair_channels)
        .transpose(1, 0, 2)
        .reshape(width * width, pair_channels)
    )
    projection_sum = everything[:, -2].reshape(2 * width, channels).T
    bias_sum = everything[0, -1]

    alignment_gradient = norm_grad(
        x, left_grads, right_grads, alignment_features, gain, weight_rows
    )
    return (
        pair_update_result,
        alignment_gradient,
        projection_sum / rows_total,
        weight_sum / rows_total,
        bias_sum / rows_total,
    )


def solution(mesh):
    in_specs = (P("sa", "ia", None), P(), P(), P(), P(), P(), P(("ia", "sa"), "ja", None))
    out_specs = (P(("ia", "sa"), "ja", None), P("sa", "ia", None), P(), P(), P())
    return jax.shard_map(body, mesh=mesh, in_specs=in_specs, out_specs=out_specs, check_vma=False)
```

profile of v0, /device:TPU:1, one launch (start us, length us, event | category | flops | bytes accessed | tf_op | source)
XLA Modules:
  0.0 197.2 jit_solution(9307220920853546222)
XLA Ops:
  1.4 2.2 %copy-done = bf16[64,128,256]{2,1,0:T(8,128)(2,1)S(1)} copy-done((bf16[64,128,256]{2,1,0:T(8,128)(2,1)S(1)}, bf16[64,128,256]{2,1,0:T(8,128)(2,1)}, u32[]{:S(2)}) %copy-start) | copy-done | bytes 4194328
  5.0 4.6 %project.3 = bf16[64,32,128]{2,1,0:T(8,128)(2,1)S(1)} custom-call(bf16[64,128,256]{2,1,0:T(8,128)(2,1)S(1)} %copy-done, f32[1,256]{1,0:T(1,128)S(1)} %bitcast.51, f32[1,256]{1,0:T(1,128)S(1)} %bitcast.55, bf16[32,256]{1,0:T(8,128)(2,1)S(1)} %get-tuple-element.25.weight_ref), custom_call_target="tpu_custom_call" | custom-call | flops 134217728 | bytes 4718592 | tf_op jit(solution)/shard_map/project/pallas_call | solution.py:55
  17.1 15.0 %collective-permute-start.1 = (bf16[16,4096]{1,0:T(8,128)(2,1)S(1)}, bf16[16,4096]{1,0:T(8,128)(2,1)S(1)}, u32[]{:S(2)}, u32[]{:S(2)}) collective-permute-start(bf16[16,4096]{1,0:T(8,128)(2,1)S(1)} %collective-permute-done.refs_0_), channel_id=1, source_target_pairs={{0,96},{1,97},{4,100},{5,101},{8,104},{9,105},{12,108},{13,109},{2... | collective-permute-start | bytes 393224 | tf_op jit(solution)/shard_map/ppermute | solution.py:357
  38.6 2.3 %collective-permute-start.6 = (bf16[16,4096]{1,0:T(8,128)(2,1)S(1)}, bf16[16,4096]{1,0:T(8,128)(2,1)S(1)}, u32[]{:S(2)}, u32[]{:S(2)}) collective-permute-start(bf16[16,4096]{1,0:T(8,128)(2,1)S(1)} %collective-permute-done.2.refs_2_), channel_id=1, source_target_pairs={{0,1},{1,0},{4,5},{5,4},{8,9},{9,8},{12,13},{13,12},{2,3},{3,2},{6... | collective-permute-start | bytes 393224 | tf_op jit(solution)/shard_map/ppermute | solution.py:357
  42.0 1.6 copy-done.7
  43.6 10.7 %outer_grad.1 = (bf16[8,32,256,128]{3,2,1,0:T(8,128)(2,1)}, bf16[128,4096]{1,0:T(8,128)(2,1)S(1)}, f32[8,128]{1,0:T(8,128)S(1)}) custom-call(bf16[64,128,128]{2,1,0:T(8,128)(2,1)S(1)} %copy-done.7, bf16[1024,128]{1,0:T(8,128)(2,1)S(1)} %bitcast.36, bf16[2048,128]{1,0:T(8,128)(2,1)S(1)} %bitcast.46), custom_call_target="tpu_custom_call" | custom-call | flops 4294967296 | bytes 18874368 | tf_op jit(solution)/shard_map/outer_grad/pallas_call | solution.py:111
  55.2 11.3 %left_grad.1 = bf16[128,2048]{1,0:T(8,128)(2,1)S(1)} custom-call(bf16[16,4096]{1,0:T(8,128)(2,1)S(1)} %collective-permute-done.refs_0_, bf16[16,4096]{1,0:T(8,128)(2,1)S(1)} %collective-permute-done.1.refs_1_, bf16[16,4096]{1,0:T(8,128)(2,1)S(1)} %collective-permute-done.2.refs_2_, bf16[16,4096]{1,0:T(8,128)(2,1)S(1)} %collective-permute-done.3.refs_3_, ...), custom_call_target="tpu_custom_call" | custom-call | flops 2147483648 | bytes 16777216 | tf_op jit(solution)/shard_map/left_grad/pallas_call | solution.py:170
  67.8 14.8 %pair_update.1 = (bf16[64,128,128]{2,1,0:T(8,128)(2,1)}, bf16[1024,128]{1,0:T(8,128)(2,1)}) custom-call(bf16[16,4096]{1,0:T(8,128)(2,1)S(1)} %collective-permute-done.refs_0_, bf16[16,4096]{1,0:T(8,128)(2,1)S(1)} %collective-permute-done.1.refs_1_, bf16[16,4096]{1,0:T(8,128)(2,1)S(1)} %collective-permute-done.2.refs_2_, ...), custom_call_target="tpu_custom_call" | custom-call | flops 6442450944 | bytes 4194304 | tf_op jit(solution)/shard_map/pair_update/pallas_call | solution.py:231
  82.7 8.8 %all-to-all-start = ((bf16[128,8,128]{2,1,0:T(8,128)(2,1)}), bf16[128,8,128]{2,1,0:T(8,128)(2,1)S(1)}, u32[]{:S(2)}, u32[]{:S(2)}) async-start(bf16[128,8,128]{2,1,0:T(8,128)(2,1)} %bitcast.15), calls=%async_computation | async-start | bytes 524288 | tf_op jit(solution)/shard_map/all_to_all | solution.py:460
  94.0 2.4 %collective-permute-start.11 = (bf16[16,4096]{1,0:T(8,128)(2,1)S(1)}, bf16[16,4096]{1,0:T(8,128)(2,1)S(1)}, u32[]{:S(2)}, u32[]{:S(2)}) collective-permute-start(bf16[16,4096]{1,0:T(8,128)(2,1)S(1)} %get-tuple-element.19), channel_id=1, source_target_pairs={{0,8},{1,9},{4,12},{5,13},{8,0},{9,1},{12,4},{13,5},{2,10},{3,11},... | collective-permute-start | bytes 393224 | tf_op jit(solution)/shard_map/ppermute | solution.py:357
  100.2 2.9 %collective-permute-start.19 = (bf16[16,4096]{1,0:T(8,128)(2,1)S(1)}, bf16[16,4096]{1,0:T(8,128)(2,1)S(1)}, u32[]{:S(2)}, u32[]{:S(2)}) collective-permute-start(bf16[16,4096]{1,0:T(8,128)(2,1)S(1)} %get-tuple-element.17), channel_id=1, source_target_pairs={{0,64},{1,65},{4,68},{5,69},{8,72},{9,73},{12,76},{13,77},{2,66},{... | collective-permute-start | bytes 393224 | tf_op jit(solution)/shard_map/ppermute | solution.py:357
  106.3 1.6 collective-permute-done.19
  109.7 5.8 %collective-permute-start.22 = (bf16[16,4096]{1,0:T(8,128)(2,1)S(1)}, bf16[16,4096]{1,0:T(8,128)(2,1)S(1)}, u32[]{:S(2)}, u32[]{:S(2)}) collective-permute-start(bf16[16,4096]{1,0:T(8,128)(2,1)S(1)} %collective-permute-done.21), channel_id=1, source_target_pairs={{0,2},{1,3},{4,6},{5,7},{8,10},{9,11},{12,14},{13,15},{2,0},{3,1},... | collective-permute-start | bytes 393224 | tf_op jit(solution)/shard_map/ppermute | solution.py:357
  116.0 2.0 collective-permute-done.22
  119.5 18.2 %all-to-all-start.1 = ((f32[128,2,128]{2,1,0:T(2,128)}), f32[128,2,128]{2,1,0:T(2,128)S(1)}, u32[]{:S(2)}, u32[]{:S(2)}) async-start(f32[128,2,128]{2,1,0:T(2,128)} %pad_maximum_fusion.1), calls=%async_computation.1 | async-start | bytes 262144 | tf_op jit(solution)/shard_map/all_to_all | solution.py:484
  137.8 10.1 %all-to-all-done.1 = f32[128,2,128]{2,1,0:T(2,128)S(1)} async-done(((f32[128,2,128]{2,1,0:T(2,128)}), f32[128,2,128]{2,1,0:T(2,128)S(1)}, u32[]{:S(2)}, u32[]{:S(2)}) %all-to-all-start.1) | async-done | bytes 131104 | tf_op jit(solution)/shard_map/all_to_all | solution.py:484
  149.1 3.9 %all-to-all-start.2 = ((f32[128,10,128]{2,1,0:T(8,128)}), f32[128,10,128]{2,1,0:T(8,128)S(1)}, u32[]{:S(2)}, u32[]{:S(2)}) async-start(f32[128,10,128]{2,1,0:T(8,128)} %broadcast_in_dim.7), calls=%async_computation.2 | async-start | bytes 2097152 | tf_op jit(solution)/shard_map/all_to_all | solution.py:486
  153.1 2.7 %collective-permute-start.14 = (bf16[16,32,128]{2,1,0:T(8,128)(2,1)S(1)}, bf16[16,32,128]{2,1,0:T(8,128)(2,1)S(1)}, u32[]{:S(2)}, u32[]{:S(2)}) collective-permute-start(bf16[16,32,128]{2,1,0:T(8,128)(2,1)S(1)} %bitcast.37), channel_id=1, source_target_pairs={{0,12},{1,13},{4,0},{5,1},{8,4},{9,5},{12,8},{13,9},{2,14},{3,15},... | collective-permute-start | bytes 393224 | tf_op jit(solution)/shard_map/ppermute | solution.py:357
  156.9 2.1 %collective-permute-start.23 = (bf16[16,32,128]{2,1,0:T(8,128)(2,1)S(1)}, bf16[16,32,128]{2,1,0:T(8,128)(2,1)S(1)}, u32[]{:S(2)}, u32[]{:S(2)}) collective-permute-start(bf16[16,32,128]{2,1,0:T(8,128)(2,1)S(1)} %bitcast.42), channel_id=1, source_target_pairs={{0,12},{1,13},{4,0},{5,1},{8,4},{9,5},{12,8},{13,9},{2,14},{3,15},... | collective-permute-start | bytes 393224 | tf_op jit(solution)/shard_map/ppermute | solution.py:357
  160.2 8.4 %collective-permute-done.14.refs_1_ = bf16[16,32,128]{2,1,0:T(8,128)(2,1)S(1)} collective-permute-done((bf16[16,32,128]{2,1,0:T(8,128)(2,1)S(1)}, bf16[16,32,128]{2,1,0:T(8,128)(2,1)S(1)}, u32[]{:S(2)}, u32[]{:S(2)}) %collective-permute-start.14) | collective-permute-done | bytes 131104 | tf_op jit(solution)/shard_map/ppermute | solution.py:357
  170.1 2.7 %collective-permute-done.16.refs_3_ = bf16[16,32,128]{2,1,0:T(8,128)(2,1)S(1)} collective-permute-done((bf16[16,32,128]{2,1,0:T(8,128)(2,1)S(1)}, bf16[16,32,128]{2,1,0:T(8,128)(2,1)S(1)}, u32[]{:S(2)}, u32[]{:S(2)}) %collective-permute-start.16) | collective-permute-done | bytes 131104 | tf_op jit(solution)/shard_map/ppermute | solution.py:357
  175.8 2.5 %collective-permute-done.25.refs_7_ = bf16[16,32,128]{2,1,0:T(8,128)(2,1)S(1)} collective-permute-done((bf16[16,32,128]{2,1,0:T(8,128)(2,1)S(1)}, bf16[16,32,128]{2,1,0:T(8,128)(2,1)S(1)}, u32[]{:S(2)}, u32[]{:S(2)}) %collective-permute-start.25) | collective-permute-done | bytes 131104 | tf_op jit(solution)/shard_map/ppermute | solution.py:357
  178.3 2.2 %copy-done.1 = bf16[64,128,256]{2,1,0:T(8,128)(2,1)S(1)} copy-done((bf16[64,128,256]{2,1,0:T(8,128)(2,1)S(1)}, bf16[64,128,256]{2,1,0:T(8,128)(2,1)}, u32[]{:S(2)}) %copy-start.1) | copy-done | bytes 4194328
  180.4 14.3 %norm_grad.1 = bf16[64,128,256]{2,1,0:T(8,128)(2,1)} custom-call(s32[1]{0:T(128)} %bitcast.11.x_ref, bf16[16,32,128]{2,1,0:T(8,128)(2,1)S(1)} %bitcast.40, bf16[16,32,128]{2,1,0:T(8,128)(2,1)S(1)} %collective-permute-done.14.refs_1_, bf16[16,32,128]{2,1,0:T(8,128)(2,1)S(1)} %collective-permute-done.15.refs_2_, ...), custom_call_target="tpu_custom_call" | custom-call | flops 268435456 | bytes 8388608 | tf_op jit(solution)/shard_map/norm_grad/pallas_call | solution.py:321
  (100 shorter events, 42.9 us)
Async XLA Ops:
  10.8 23.0 %collective-permute-start.8 = (bf16[64,32,64]{2,1,0:T(8,128)(2,1)S(1)}, bf16[64,32,64]{2,1,0:T(8,128)(2,1)}, u32[]{:S(2)}, u32[]{:S(2)}) collective-permute-start(bf16[64,32,64]{2,1,0:T(8,128)(2,1)S(1)} %get-tuple-element.24), channel_id=1, source_target_pairs={{0,1},{1,0},{4,5},{5,4},{8,9},{9,8},{12,13},{13,12},{2,3},{3,2},{6... | collective-permute-start | bytes 786440 | tf_op jit(solution)/shard_map/ppermute | solution.py:357
  17.1 20.7 %collective-permute-start.1 = (bf16[16,4096]{1,0:T(8,128)(2,1)S(1)}, bf16[16,4096]{1,0:T(8,128)(2,1)S(1)}, u32[]{:S(2)}, u32[]{:S(2)}) collective-permute-start(bf16[16,4096]{1,0:T(8,128)(2,1)S(1)} %collective-permute-done.refs_0_), channel_id=1, source_target_pairs={{0,96},{1,97},{4,100},{5,101},{8,104},{9,105},{12,108},{13,109},{2... | collective-permute-start | bytes 393224 | tf_op jit(solution)/shard_map/ppermute | solution.py:357
  32.0 9.1 %collective-permute-start.3 = (bf16[16,4096]{1,0:T(8,128)(2,1)S(1)}, bf16[16,4096]{1,0:T(8,128)(2,1)S(1)}, u32[]{:S(2)}, u32[]{:S(2)}) collective-permute-start(bf16[16,4096]{1,0:T(8,128)(2,1)S(1)} %collective-permute-done.refs_0_), channel_id=1, source_target_pairs={{0,32},{1,33},{4,36},{5,37},{8,40},{9,41},{12,44},{13,45},{2,34},{... | collective-permute-start | bytes 393224 | tf_op jit(solution)/shard_map/ppermute | solution.py:357
  32.6 22.5 %collective-permute-start.4 = (bf16[16,4096]{1,0:T(8,128)(2,1)S(1)}, bf16[16,4096]{1,0:T(8,128)(2,1)S(1)}, u32[]{:S(2)}, u32[]{:S(2)}) collective-permute-start(bf16[16,4096]{1,0:T(8,128)(2,1)S(1)} %collective-permute-done.refs_0_), channel_id=1, source_target_pairs={{0,1},{1,0},{4,5},{5,4},{8,9},{9,8},{12,13},{13,12},{2,3},{3,2},{6... | collective-permute-start | bytes 393224 | tf_op jit(solution)/shard_map/ppermute | solution.py:357
  37.7 17.4 %collective-permute-start.5 = (bf16[16,4096]{1,0:T(8,128)(2,1)S(1)}, bf16[16,4096]{1,0:T(8,128)(2,1)S(1)}, u32[]{:S(2)}, u32[]{:S(2)}) collective-permute-start(bf16[16,4096]{1,0:T(8,128)(2,1)S(1)} %collective-permute-done.1.refs_1_), channel_id=1, source_target_pairs={{0,1},{1,0},{4,5},{5,4},{8,9},{9,8},{12,13},{13,12},{2,3},{3,2},{6... | collective-permute-start | bytes 393224 | tf_op jit(solution)/shard_map/ppermute | solution.py:357
  38.6 16.6 %collective-permute-start.6 = (bf16[16,4096]{1,0:T(8,128)(2,1)S(1)}, bf16[16,4096]{1,0:T(8,128)(2,1)S(1)}, u32[]{:S(2)}, u32[]{:S(2)}) collective-permute-start(bf16[16,4096]{1,0:T(8,128)(2,1)S(1)} %collective-permute-done.2.refs_2_), channel_id=1, source_target_pairs={{0,1},{1,0},{4,5},{5,4},{8,9},{9,8},{12,13},{13,12},{2,3},{3,2},{6... | collective-permute-start | bytes 393224 | tf_op jit(solution)/shard_map/ppermute | solution.py:357
  41.1 14.0 %collective-permute-start.7 = (bf16[16,4096]{1,0:T(8,128)(2,1)S(1)}, bf16[16,4096]{1,0:T(8,128)(2,1)}, u32[]{:S(2)}, u32[]{:S(2)}) collective-permute-start(bf16[16,4096]{1,0:T(8,128)(2,1)S(1)} %collective-permute-done.3.refs_3_), channel_id=1, source_target_pairs={{0,1},{1,0},{4,5},{5,4},{8,9},{9,8},{12,13},{13,12},{2,3},{3,2},{6... | collective-permute-start | bytes 393224 | tf_op jit(solution)/shard_map/ppermute | solution.py:357
  55.1 42.4 %collective-permute-start.17 = (bf16[64,4096]{1,0:T(8,128)(2,1)}, bf16[64,4096]{1,0:T(8,128)(2,1)}, u32[]{:S(2)}, u32[]{:S(2)}) collective-permute-start(bf16[64,4096]{1,0:T(8,128)(2,1)} %slice.48), channel_id=1, source_target_pairs={{0,1},{1,0},{4,5},{5,4},{8,9},{9,8},{12,13},{13,12},{2,3},{3,2},{6... | collective-permute-start | bytes 1572872 | tf_op jit(solution)/shard_map/ppermute | solution.py:357
  67.3 24.1 %collective-permute-start.9 = (bf16[64,2048]{1,0:T(8,128)(2,1)}, bf16[64,2048]{1,0:T(8,128)(2,1)}, u32[]{:S(2)}, u32[]{:S(2)}) collective-permute-start(bf16[64,2048]{1,0:T(8,128)(2,1)} %get-tuple-element.21), channel_id=1, source_target_pairs={{0,1},{1,0},{4,5},{5,4},{8,9},{9,8},{12,13},{13,12},{2,3},{3,2},{6... | collective-permute-start | bytes 786440 | tf_op jit(solution)/shard_map/ppermute | solution.py:357
  82.7 36.8 %all-to-all-start = ((bf16[128,8,128]{2,1,0:T(8,128)(2,1)}), bf16[128,8,128]{2,1,0:T(8,128)(2,1)S(1)}, u32[]{:S(2)}, u32[]{:S(2)}) async-start(bf16[128,8,128]{2,1,0:T(8,128)(2,1)} %bitcast.15), calls=%async_computation | async-start | bytes 524288 | tf_op jit(solution)/shard_map/all_to_all | solution.py:460
  92.5 10.6 %collective-permute-start.10 = (bf16[16,4096]{1,0:T(8,128)(2,1)S(1)}, bf16[16,4096]{1,0:T(8,128)(2,1)S(1)}, u32[]{:S(2)}, u32[]{:S(2)}) collective-permute-start(bf16[16,4096]{1,0:T(8,128)(2,1)S(1)} %get-tuple-element.18), channel_id=1, source_target_pairs={{0,4},{1,5},{4,8},{5,9},{8,12},{9,13},{12,0},{13,1},{2,6},{3,7},{6... | collective-permute-start | bytes 393224 | tf_op jit(solution)/shard_map/ppermute | solution.py:357
  94.0 10.1 %collective-permute-start.11 = (bf16[16,4096]{1,0:T(8,128)(2,1)S(1)}, bf16[16,4096]{1,0:T(8,128)(2,1)S(1)}, u32[]{:S(2)}, u32[]{:S(2)}) collective-permute-start(bf16[16,4096]{1,0:T(8,128)(2,1)S(1)} %get-tuple-element.19), channel_id=1, source_target_pairs={{0,8},{1,9},{4,12},{5,13},{8,0},{9,1},{12,4},{13,5},{2,10},{3,11},... | collective-permute-start | bytes 393224 | tf_op jit(solution)/shard_map/ppermute | solution.py:357
  96.4 7.7 %collective-permute-start.12 = (bf16[16,4096]{1,0:T(8,128)(2,1)S(1)}, bf16[16,4096]{1,0:T(8,128)(2,1)S(1)}, u32[]{:S(2)}, u32[]{:S(2)}) collective-permute-start(bf16[16,4096]{1,0:T(8,128)(2,1)S(1)} %get-tuple-element.20), channel_id=1, source_target_pairs={{0,12},{1,13},{4,0},{5,1},{8,4},{9,5},{12,8},{13,9},{2,14},{3,15},... | collective-permute-start | bytes 393224 | tf_op jit(solution)/shard_map/ppermute | solution.py:357
  98.8 7.6 %collective-permute-start.18 = (bf16[16,4096]{1,0:T(8,128)(2,1)S(1)}, bf16[16,4096]{1,0:T(8,128)(2,1)S(1)}, u32[]{:S(2)}, u32[]{:S(2)}) collective-permute-start(bf16[16,4096]{1,0:T(8,128)(2,1)S(1)} %get-tuple-element.15), channel_id=1, source_target_pairs={{0,32},{1,33},{4,36},{5,37},{8,40},{9,41},{12,44},{13,45},{2,34},{... | collective-permute-start | bytes 393224 | tf_op jit(solution)/shard_map/ppermute | solution.py:357
  100.2 7.8 %collective-permute-start.19 = (bf16[16,4096]{1,0:T(8,128)(2,1)S(1)}, bf16[16,4096]{1,0:T(8,128)(2,1)S(1)}, u32[]{:S(2)}, u32[]{:S(2)}) collective-permute-start(bf16[16,4096]{1,0:T(8,128)(2,1)S(1)} %get-tuple-element.17), channel_id=1, source_target_pairs={{0,64},{1,65},{4,68},{5,69},{8,72},{9,73},{12,76},{13,77},{2,66},{... | collective-permute-start | bytes 393224 | tf_op jit(solution)/shard_map/ppermute | solution.py:357
  109.7 8.2 %collective-permute-start.22 = (bf16[16,4096]{1,0:T(8,128)(2,1)S(1)}, bf16[16,4096]{1,0:T(8,128)(2,1)S(1)}, u32[]{:S(2)}, u32[]{:S(2)}) collective-permute-start(bf16[16,4096]{1,0:T(8,128)(2,1)S(1)} %collective-permute-done.21), channel_id=1, source_target_pairs={{0,2},{1,3},{4,6},{5,7},{8,10},{9,11},{12,14},{13,15},{2,0},{3,1},... | collective-permute-start | bytes 393224 | tf_op jit(solution)/shard_map/ppermute | solution.py:357
  119.5 28.5 %all-to-all-start.1 = ((f32[128,2,128]{2,1,0:T(2,128)}), f32[128,2,128]{2,1,0:T(2,128)S(1)}, u32[]{:S(2)}, u32[]{:S(2)}) async-start(f32[128,2,128]{2,1,0:T(2,128)} %pad_maximum_fusion.1), calls=%async_computation.1 | async-start | bytes 262144 | tf_op jit(solution)/shard_map/all_to_all | solution.py:484
  149.1 45.6 %all-to-all-start.2 = ((f32[128,10,128]{2,1,0:T(8,128)}), f32[128,10,128]{2,1,0:T(8,128)S(1)}, u32[]{:S(2)}, u32[]{:S(2)}) async-start(f32[128,10,128]{2,1,0:T(8,128)} %broadcast_in_dim.7), calls=%async_computation.2 | async-start | bytes 2097152 | tf_op jit(solution)/shard_map/all_to_all | solution.py:486
  153.1 15.5 %collective-permute-start.14 = (bf16[16,32,128]{2,1,0:T(8,128)(2,1)S(1)}, bf16[16,32,128]{2,1,0:T(8,128)(2,1)S(1)}, u32[]{:S(2)}, u32[]{:S(2)}) collective-permute-start(bf16[16,32,128]{2,1,0:T(8,128)(2,1)S(1)} %bitcast.37), channel_id=1, source_target_pairs={{0,12},{1,13},{4,0},{5,1},{8,4},{9,5},{12,8},{13,9},{2,14},{3,15},... | collective-permute-start | bytes 393224 | tf_op jit(solution)/shard_map/ppermute | solution.py:357
  155.7 14.4 %collective-permute-start.15 = (bf16[16,32,128]{2,1,0:T(8,128)(2,1)S(1)}, bf16[16,32,128]{2,1,0:T(8,128)(2,1)S(1)}, u32[]{:S(2)}, u32[]{:S(2)}) collective-permute-start(bf16[16,32,128]{2,1,0:T(8,128)(2,1)S(1)} %bitcast.38), channel_id=1, source_target_pairs={{0,8},{1,9},{4,12},{5,13},{8,0},{9,1},{12,4},{13,5},{2,10},{3,11},... | collective-permute-start | bytes 393224 | tf_op jit(solution)/shard_map/ppermute | solution.py:357
  156.3 16.5 %collective-permute-start.16 = (bf16[16,32,128]{2,1,0:T(8,128)(2,1)S(1)}, bf16[16,32,128]{2,1,0:T(8,128)(2,1)S(1)}, u32[]{:S(2)}, u32[]{:S(2)}) collective-permute-start(bf16[16,32,128]{2,1,0:T(8,128)(2,1)S(1)} %bitcast.39), channel_id=1, source_target_pairs={{0,4},{1,5},{4,8},{5,9},{8,12},{9,13},{12,0},{13,1},{2,6},{3,7},{6... | collective-permute-start | bytes 393224 | tf_op jit(solution)/shard_map/ppermute | solution.py:357
  156.9 17.4 %collective-permute-start.23 = (bf16[16,32,128]{2,1,0:T(8,128)(2,1)S(1)}, bf16[16,32,128]{2,1,0:T(8,128)(2,1)S(1)}, u32[]{:S(2)}, u32[]{:S(2)}) collective-permute-start(bf16[16,32,128]{2,1,0:T(8,128)(2,1)S(1)} %bitcast.42), channel_id=1, source_target_pairs={{0,12},{1,13},{4,0},{5,1},{8,4},{9,5},{12,8},{13,9},{2,14},{3,15},... | collective-permute-start | bytes 393224 | tf_op jit(solution)/shard_map/ppermute | solution.py:357
  159.0 16.8 %collective-permute-start.24 = (bf16[16,32,128]{2,1,0:T(8,128)(2,1)S(1)}, bf16[16,32,128]{2,1,0:T(8,128)(2,1)S(1)}, u32[]{:S(2)}, u32[]{:S(2)}) collective-permute-start(bf16[16,32,128]{2,1,0:T(8,128)(2,1)S(1)} %bitcast.43), channel_id=1, source_target_pairs={{0,8},{1,9},{4,12},{5,13},{8,0},{9,1},{12,4},{13,5},{2,10},{3,11},... | collective-permute-start | bytes 393224 | tf_op jit(solution)/shard_map/ppermute | solution.py:357
  168.6 9.7 %collective-permute-start.25 = (bf16[16,32,128]{2,1,0:T(8,128)(2,1)S(1)}, bf16[16,32,128]{2,1,0:T(8,128)(2,1)S(1)}, u32[]{:S(2)}, u32[]{:S(2)}) collective-permute-start(bf16[16,32,128]{2,1,0:T(8,128)(2,1)S(1)} %bitcast.44), channel_id=1, source_target_pairs={{0,4},{1,5},{4,8},{5,9},{8,12},{9,13},{12,0},{13,1},{2,6},{3,7},{6... | collective-permute-start | bytes 393224 | tf_op jit(solution)/shard_map/ppermute | solution.py:357
  (16 other events, 166.9 us)
where the time goes:
time: 198 us; the launch traced here: 197 us
  starting transfers between devices  80.7 us (41%)
  Pallas kernels  57.5 us (29%)
  waiting for transfers between devices  32.6 us (16%)
  local copies, waits for them, and re-layouts  17.5 us (9%)
  other arithmetic  7.71 us (4%)
    ppermute x26, starting transfers between devices, torus_permute(): return lax.ppermute(value, AXES, pairs)  49.8 us
    ppermute x26, waiting for transfers between devices, torus_permute(): return lax.ppermute(value, AXES, pairs)  22.5 us
    all_to_all x1, starting transfers between devices, body(): small_share = jnp.sum(lax.all_to_all(small, AXES, 0, 0, tiled=True), axis=0)  18.2 us
    pallas_call x1, Pallas kernels, pair_and_weight_grad(): pl.pallas_call(pair_kernel, grid=(blocks,), in_specs=[whole(piece.shape)...  14.8 us
    pallas_call x1, Pallas kernels, norm_grad(): pl.pallas_call(norm_grad_kernel, grid_spec=pltpu.PrefetchScalarGridSpec(n...  14.3 us
    pallas_call x1, Pallas kernels, left_grad_part(): pl.pallas_call(left_grad_kernel, grid=(blocks,), in_specs=[whole(piece.sh...  11.3 us
    pallas_call x1, Pallas kernels, outer_grad_and_right(): pl.pallas_call(outer_grad_kernel, grid=(blocks,), in_specs=[pl.BlockSpec(...  10.7 us
    all_to_all x1, waiting for transfers between devices, body(): small_share = jnp.sum(lax.all_to_all(small, AXES, 0, 0, tiled=True), axis=0)  10.1 us
  transfers between devices with their start and end apart: 29, of which 12 were waited for; matrix products, arithmetic and copies ran while one was open for 6% of the time, Pallas kernels for 27%

commit v1 on v0

v1 whole, which is shorter than its diff:
```python
import functools

import jax
import jax.numpy as jnp
from jax import lax
from jax.experimental import pallas as pl
from jax.experimental.pallas import tpu as pltpu
from jax.sharding import PartitionSpec as P

epsilon = 1e-05
AXES = ("ia", "ja", "sa")
RING = 4
SWAP_Y = (0, 2, 1, 3)
ROWS_AT_ONCE = 8
BF16 = jnp.bfloat16
F32 = jnp.float32
VMEM_LIMIT = 12 * 1024 * 1024


def dot(a, b, contract):
    return lax.dot_general(a, b, (contract, ((), ())), preferred_element_type=F32)


def params(limit=VMEM_LIMIT):
    return pltpu.CompilerParams(dimension_semantics=("arbitrary",), vmem_limit_bytes=limit)


ANYWHERE = pl.BlockSpec(memory_space=pl.ANY)


def cost(flops, bytes_accessed, transcendentals):
    return pl.CostEstimate(
        flops=flops, bytes_accessed=bytes_accessed, transcendentals=transcendentals
    )


def whole(shape):
    return pl.BlockSpec(shape, lambda *_: (0,) * len(shape))


def row_mean(values):
    channels = values.shape[-1]
    ones = jnp.full((channels, 128), 1.0 / channels, BF16)
    mean = dot(values.astype(BF16), ones, ((1,), (0,)))
    return jnp.concatenate([mean] * (channels // 128), axis=1)


def norm_block(features):
    centred = features.astype(F32) - row_mean(features)
    inverse_deviation = lax.rsqrt(row_mean(centred * centred) + epsilon)
    return centred * inverse_deviation, inverse_deviation


def norm_rows(features):
    values = features.astype(F32)
    scale = 1.0 / values.shape[-1]
    centred = values - jnp.sum(values, axis=-1, keepdims=True) * scale
    variance = jnp.sum(centred * centred, axis=-1, keepdims=True) * scale
    return centred * lax.rsqrt(variance + epsilon)


def project_kernel(place_ref, features_ref, gain_ref, offset_ref, weight_ref, *refs):
    out_ref = refs[-1]
    seqs, residues, channels = features_ref.shape
    at_once = 256 // residues
    for s in range(0, seqs, at_once):
        rescaled = norm_rows(
            features_ref[s : s + at_once].reshape(at_once * residues, channels)
        )
        normed = (rescaled * gain_ref[...] + offset_ref[...]).astype(BF16)
        several = dot(weight_ref[...], normed, ((1,), (1,))).astype(BF16)
        for n in range(at_once):
            out_ref[s + n] = several[:, n * residues : (n + 1) * residues]


def project(first, count, part, residues, features, gain, offset, weight, after=()):
    total, _, channels = features.shape
    width = weight.shape[0]
    seqs = 1024 // residues
    steps = total // seqs

    def place(n, place_ref):
        return (lax.rem(place_ref[0] + n, steps), place_ref[1], 0)

    return pl.pallas_call(
        project_kernel,
        grid_spec=pltpu.PrefetchScalarGridSpec(
            num_scalar_prefetch=1,
            grid=(count // seqs,),
            in_specs=[
                pl.BlockSpec((seqs, residues, channels), place),
                whole((1, channels)),
                whole((1, channels)),
                whole((width, channels)),
            ]
            + [ANYWHERE] * len(after),
            out_specs=pl.BlockSpec((seqs, width, residues), lambda n, place_ref: (n, 0, 0)),
        ),
        out_shape=jax.ShapeDtypeStruct((count, width, residues), BF16),
        compiler_params=params(),
        cost_estimate=cost(
            flops=4 * count * residues * channels * width,
            bytes_accessed=2 * count * residues * (channels + width),
            transcendentals=count * residues,
        ),
        name="project",
    )(jnp.stack([first, part]), features, gain, offset, weight, *after)


def outer_grad_block(cot_ref, weight_ref, grad_ref):
    rows, cols, pair_channels = cot_ref.shape
    width = grad_ref.shape[0]
    for i in range(0, rows, 2):
        cot = cot_ref[i : i + 2].reshape(2 * cols, pair_channels)
        grad = dot(weight_ref[...], cot, ((1,), (1,))).astype(BF16)
        grad = grad.reshape(width, width, 2 * cols)
        grad_ref[:, i * width : (i + 1) * width, :] = grad[:, :, :cols]
        grad_ref[:, (i + 1) * width : (i + 2) * width, :] = grad[:, :, cols:]


def right_grad_kernel(fresh, cot_ref, weight_ref, left_ref, total_in_ref, bias_in_ref, *refs):
    right_ref, total_ref, bias_ref, grad_ref = refs[-4:]
    step = pl.program_id(0)
    rows, cols, pair_channels = cot_ref.shape
    width = grad_ref.shape[0]

    @pl.when(step == 0)
    def _():
        if fresh:
            total_ref[...] = jnp.zeros_like(total_ref)
            bias_ref[...] = jnp.zeros_like(bias_ref)
        else:
            total_ref[...] = total_in_ref[...]
            bias_ref[...] = bias_in_ref[...]

    bias_ref[...] += jnp.sum(
        cot_ref[...].astype(F32).reshape(rows * cols // 8, 8, pair_channels), axis=0
    )
    outer_grad_block(cot_ref, weight_ref, grad_ref)
    left = left_ref[...].T
    for d in range(0, width, 2):
        both = jnp.concatenate([grad_ref[d], grad_ref[d + 1]], axis=1)
        total_ref[:, d * cols : (d + 2) * cols] += dot(left, both, ((1,), (0,)))

    if not fresh:

        @pl.when(step == pl.num_programs(0) - 1)
        def _():
            right_ref[...] = total_ref[...].astype(BF16)


def right_grad_part(first, count, cotangent, weight, left, before, after=()):
    rows, cols, pair_channels = cotangent.shape
    seqs = left.shape[1]
    width = left.shape[0] // rows
    block = ROWS_AT_ONCE * width
    fresh = before is None
    if fresh:
        before = (None, jnp.zeros((8, pair_channels), F32), jnp.zeros((8, pair_channels), F32))
    right_shape = (8, pair_channels) if fresh else (seqs, width * cols)
    return pl.pallas_call(
        functools.partial(right_grad_kernel, fresh),
        grid=(count,),
        in_specs=[
            pl.BlockSpec((ROWS_AT_ONCE, cols, pair_channels), lambda n: (first + n, 0, 0)),
            whole((width * width, pair_channels)),
            pl.BlockSpec((block, seqs), lambda n: (first + n, 0)),
            whole(before[1].shape),
            whole(before[2].shape),
        ]
        + [ANYWHERE] * len(after),
        out_specs=[
            whole(right_shape),
            whole((seqs, width * cols)),
            whole((8, pair_channels)),
        ],
        out_shape=[
            jax.ShapeDtypeStruct(right_shape, BF16),
            jax.ShapeDtypeStruct((seqs, width * cols), F32),
            jax.ShapeDtypeStruct((8, pair_channels), F32),
        ],
        scratch_shapes=[pltpu.VMEM((width, block, cols), BF16)],
        compiler_params=params(),
        cost_estimate=cost(
            flops=4 * count * ROWS_AT_ONCE * cols * width * width * pair_channels,
            bytes_accessed=2 * count * ROWS_AT_ONCE * cols * pair_channels,
            transcendentals=0,
        ),
        name="right_grad",
    )(cotangent, weight, left, before[1], before[2], *after)


def left_grad_kernel(turn_ref, *refs):
    piece_refs, (cot_ref, weight_ref, out_ref, cols_ref, grad_ref) = refs[: 2 * RING], refs[-5:]
    width, _, cols = grad_ref.shape
    quarter = piece_refs[0].shape[0]

    @pl.when(pl.program_id(0) == 0)
    def _():
        for d in range(width):
            here = slice(d * cols, (d + 1) * cols)
            part = jnp.concatenate([piece[:, here] for piece in piece_refs], axis=0)
            cols_ref[here, :] = part.T

    outer_grad_block(cot_ref, weight_ref, grad_ref)
    total = None
    for d in range(0, width, 2):
        both = jnp.concatenate([grad_ref[d], grad_ref[d + 1]], axis=1)
        term = dot(both, cols_ref[d * cols : (d + 2) * cols, :], ((1,), (0,)))
        total = term if total is None else total + term
    total = total.T.astype(BF16)
    for p in range(RING):
        place = lax.rem(turn_ref[0] + p, RING)
        for h in range(2):
            first = (h * RING + p) * quarter
            out_ref[place, h * quarter : (h + 1) * quarter, :] = total[first : first + quarter]


def left_grad_part(turn, pieces, cotangent, weight, after=()):
    rows, cols, pair_channels = cotangent.shape
    quarter = pieces[0].shape[0]
    width = pieces[0].shape[1] // cols
    blocks, block = rows // ROWS_AT_ONCE, ROWS_AT_ONCE * width
    seqs = 2 * RING * quarter
    return pl.pallas_call(
        left_grad_kernel,
        grid_spec=pltpu.PrefetchScalarGridSpec(
            num_scalar_prefetch=1,
            grid=(blocks,),
            in_specs=[whole(piece.shape) for piece in pieces]
            + [ANYWHERE] * len(after)
            + [
                pl.BlockSpec((ROWS_AT_ONCE, cols, pair_channels), lambda n, turn_ref: (n, 0, 0)),
                whole((width * width, pair_channels)),
            ],
            out_specs=pl.BlockSpec((RING, 2 * quarter, block), lambda n, turn_ref: (0, 0, n)),
            scratch_shapes=[
                pltpu.VMEM((width * cols, seqs), BF16),
                pltpu.VMEM((width, block, cols), BF16),
            ],
        ),
        out_shape=jax.ShapeDtypeStruct((RING, 2 * quarter, blocks * block), BF16),
        compiler_params=params(),
        cost_estimate=cost(
            flops=4 * blocks * width * block * cols * (seqs + pair_channels),
            bytes_accessed=4 * seqs * width * cols,
            transcendentals=0,
        ),
        name="left_grad",
    )(
        turn.reshape(1),
        *pieces,
        *after,
        cotangent,
        weight,
    )


def add_kernel(count, scale, *refs):
    total = refs[0][...].astype(F32)
    for ref in refs[1:count]:
        total = total + ref[...].astype(F32)
    refs[-1][...] = (total * scale).astype(BF16)


def add_up(parts, scale=1.0, after=()):
    return pl.pallas_call(
        lambda *refs: add_kernel(len(parts), scale, *refs),
        in_specs=[pl.BlockSpec(memory_space=pltpu.VMEM)] * len(parts) + [ANYWHERE] * len(after),
        out_specs=pl.BlockSpec(memory_space=pltpu.VMEM),
        out_shape=jax.ShapeDtypeStruct(parts[0].shape, BF16),
        compiler_params=pltpu.CompilerParams(vmem_limit_bytes=VMEM_LIMIT),
        name="add_up",
    )(*parts, *after)


def pair_kernel(fresh, *refs):
    piece_refs, refs = refs[: 2 * RING], refs[2 * RING :]
    left_ref, weight_ref, bias_ref, cot_ref, before_ref = refs[:5]
    pair_ref, total_ref, cols_ref, outer_ref = refs[-4:]
    rows, cols, pair_channels = cot_ref.shape
    width = outer_ref.shape[0]
    inv_seqs = 1.0 / cols_ref.shape[0]

    @pl.when(pl.program_id(0) == 0)
    def _():
        first = 0
        for piece in piece_refs:
            cols_ref[first : first + piece.shape[0], :] = piece[...]
            first += piece.shape[0]
        total_ref[...] = jnp.zeros_like(total_ref) if fresh else before_ref[...]

    for d in range(0, width, 2):
        both = dot(left_ref[...], cols_ref[:, d * cols : (d + 2) * cols], ((1,), (0,)))
        both = (both * inv_seqs).astype(BF16)
        outer_ref[d] = both[:, :cols]
        outer_ref[d + 1] = both[:, cols:]
    for i in range(0, rows, 2):
        outer = jnp.concatenate(
            [
                outer_ref[:, n * width : (n + 1) * width, :].reshape(width * width, cols)
                for n in (i, i + 1)
            ],
            axis=1,
        )
        cot = cot_ref[i : i + 2].reshape(2 * cols, pair_channels)
        total_ref[...] += dot(outer, cot, ((1,), (0,)))
        pair = dot(weight_ref[...], outer, ((1,), (0,))).T + bias_ref[...]
        pair_ref[i : i + 2] = pair.astype(BF16).reshape(2, cols, pair_channels)


def pair_and_weight_grad(first, count, pieces, left, weight, bias, cotangent, before, after=()):
    rows, cols, pair_channels = cotangent.shape
    seqs = left.shape[1]
    width = left.shape[0] // rows
    block = ROWS_AT_ONCE * width
    fresh = before is None
    if fresh:
        before = (None, jnp.zeros((8, pair_channels), F32))
    operands = [*pieces, left, weight, bias.reshape(1, -1), cotangent, before[1], *after]
    in_specs = [whole(piece.shape) for piece in pieces] + [
        pl.BlockSpec((block, seqs), lambda n: (first + n, 0)),
        whole((pair_channels, width * width)),
        whole((1, pair_channels)),
        pl.BlockSpec((ROWS_AT_ONCE, cols, pair_channels), lambda n: (first + n, 0, 0)),
        whole(before[1].shape),
    ]
    in_specs += [ANYWHERE] * len(after)
    aliases = {}
    if not fresh:
        aliases = {len(operands): 0}
        operands.append(before[0])
        in_specs.append(ANYWHERE)
    return pl.pallas_call(
        functools.partial(pair_kernel, fresh),
        grid=(count,),
        in_specs=in_specs,
        out_specs=[
            pl.BlockSpec((ROWS_AT_ONCE, cols, pair_channels), lambda n: (first + n, 0, 0)),
            whole((width * width, pair_channels)),
        ],
        out_shape=[
            jax.ShapeDtypeStruct((rows, cols, pair_channels), BF16),
            jax.ShapeDtypeStruct((width * width, pair_channels), F32),
        ],
        scratch_shapes=[
            pltpu.VMEM((seqs, width * cols), BF16),
            pltpu.VMEM((width, block, cols), BF16),
        ],
        input_output_aliases=aliases,
        compiler_params=params(),
        cost_estimate=cost(
            flops=4 * count * ROWS_AT_ONCE * cols * width * width * (2 * pair_channels + seqs),
            bytes_accessed=4 * count * ROWS_AT_ONCE * cols * pair_channels,
            transcendentals=0,
        ),
        name="pair_update",
    )(*operands)


def projection_grad_kernel(place_ref, features_ref, gain_ref, offset_ref, grads_ref, out_ref):
    seqs = features_ref.shape[0]
    total = None
    for s in range(seqs):
        rescaled = norm_rows(features_ref[s])
        normed = (rescaled * gain_ref[...] + offset_ref[...]).astype(BF16)
        term = dot(grads_ref[s], normed, ((1,), (0,)))
        total = term if total is None else total + term
    out_ref[...] = total


def projection_grad_part(x, low_y, features, gain, offset, grads):
    _, residues, channels = features.shape
    quarter, both_widths, _ = grads.shape
    eighth = quarter // 2
    place = jnp.stack([x * 2 + low_y, low_y])
    return pl.pallas_call(
        projection_grad_kernel,
        grid_spec=pltpu.PrefetchScalarGridSpec(
            num_scalar_prefetch=1,
            grid=(1,),
            in_specs=[
                pl.BlockSpec((eighth, residues, channels), lambda n, ref: (ref[0], 0, 0)),
                whole((1, channels)),
                whole((1, channels)),
                pl.BlockSpec((eighth, both_widths, residues), lambda n, ref: (ref[1], 0, 0)),
            ],
            out_specs=whole((both_widths, channels)),
        ),
        out_shape=jax.ShapeDtypeStruct((both_widths, channels), F32),
        compiler_params=params(),
        name="projection_grad",
    )(place, features, gain, offset, grads)


def norm_grad_kernel(count, first_ref, features_ref, gain_ref, weight_ref, *refs):
    piece_refs, (out_ref, token_ref, grads_ref) = refs[:count], refs[-3:]
    token_ref[...] = jnp.zeros_like(token_ref)
    step = pl.program_id(0)
    seqs, residues, channels = features_ref.shape
    steps = piece_refs[0].shape[0] // seqs
    for t in range(len(piece_refs)):

        @pl.when(step // steps == t)
        def _(t=t):
            grads_ref[...] = piece_refs[t][pl.ds(lax.rem(step, steps) * seqs, seqs)]

    at_once = 4
    for s in range(0, seqs, at_once):
        features = features_ref[s : s + at_once].reshape(at_once * residues, channels)
        rescaled, inverse_deviation = norm_block(features)
        grad = [dot(grads_ref[s + n], weight_ref[...], ((0,), (0,))) for n in range(at_once)]
        grad = jnp.concatenate(grad, axis=0) * gain_ref[...]
        grad = inverse_deviation * (grad - row_mean(grad) - rescaled * row_mean(grad * rescaled))
        out_ref[s : s + at_once] = grad.astype(BF16).reshape(at_once, residues, channels)


def norm_grad(first, pieces, features, gain, weight, before=None, after=()):
    _, residues, channels = features.shape
    quarter, both_widths, _ = pieces[0].shape
    seqs = 8
    steps = quarter // seqs

    def place(n, first_ref):
        return (lax.rem(n // steps + first_ref[0], RING) * steps + lax.rem(n, steps), 0, 0)

    operands = [first.reshape(1), features, gain, weight, *pieces, *after]
    in_specs = [
        pl.BlockSpec((seqs, residues, channels), place),
        whole((1, channels)),
        whole(weight.shape),
    ]
    in_specs += [whole(piece.shape) for piece in pieces] + [ANYWHERE] * len(after)
    aliases = {}
    if before is not None:
        aliases = {len(operands): 0}
        operands.append(before)
        in_specs.append(ANYWHERE)
    return pl.pallas_call(
        functools.partial(norm_grad_kernel, len(pieces)),
        grid_spec=pltpu.PrefetchScalarGridSpec(
            num_scalar_prefetch=1,
            grid=(len(pieces) * steps,),
            in_specs=in_specs,
            out_specs=[pl.BlockSpec((seqs, residues, channels), place), whole((8, 128))],
            scratch_shapes=[pltpu.VMEM((seqs, both_widths, residues), BF16)],
        ),
        out_shape=[
            jax.ShapeDtypeStruct(features.shape, BF16),
            jax.ShapeDtypeStruct((8, 128), F32),
        ],
        input_output_aliases=aliases,
        compiler_params=params(),
        cost_estimate=cost(
            flops=4 * len(pieces) * quarter * residues * channels * both_widths,
            bytes_accessed=4 * len(pieces) * quarter * residues * channels,
            transcendentals=0,
        ),
        name="norm_grad",
    )(*operands)


def share_kernel(scale, terms_ref, *refs):
    share_ref, spread_ref = refs[-2:]
    total = terms_ref[0].astype(F32)
    for n in range(1, terms_ref.shape[0]):
        total = total + terms_ref[n].astype(F32)
    total = total * scale
    share_ref[...] = total
    spread_ref[...] = jnp.broadcast_to(total.astype(BF16), spread_ref.shape)


def add_terms(terms, scale, after=()):
    return pl.pallas_call(
        functools.partial(share_kernel, scale),
        in_specs=[pl.BlockSpec(memory_space=pltpu.VMEM)] + [ANYWHERE] * len(after),
        out_specs=[pl.BlockSpec(memory_space=pltpu.VMEM)] * 2,
        out_shape=[
            jax.ShapeDtypeStruct(terms.shape[1:], F32),
            jax.ShapeDtypeStruct(terms.shape, BF16),
        ],
        compiler_params=pltpu.CompilerParams(vmem_limit_bytes=VMEM_LIMIT),
        name="add_terms",
    )(terms, *after)


def terms_kernel(weight_ref, projection_ref, bias_ref, *refs):
    out_ref, token_ref = refs[-2:]
    token_ref[...] = jnp.zeros_like(token_ref)
    devices, rows, lanes = out_ref.shape
    weight_rows = weight_ref.shape[0] // devices
    bias = jnp.sum(bias_ref[...], axis=0, keepdims=True)
    bias_high = bias.astype(BF16).astype(F32)
    tail = jnp.concatenate(
        [bias_high, bias - bias_high, jnp.zeros((rows - weight_rows - 3, lanes), F32)], axis=0
    )
    for n in range(devices):
        block = [
            weight_ref[n * weight_rows : (n + 1) * weight_rows, :],
            projection_ref[n : n + 1, :],
            tail,
        ]
        out_ref[n] = jnp.concatenate(block, axis=0).astype(BF16)


def gather_terms(devices, weight_part, projection_part, bias_part, after=()):
    lanes = weight_part.shape[1]
    return pl.pallas_call(
        terms_kernel,
        in_specs=[pl.BlockSpec(memory_space=pltpu.VMEM)] * 3 + [ANYWHERE] * len(after),
        out_specs=[pl.BlockSpec(memory_space=pltpu.VMEM)] * 2,
        out_shape=[
            jax.ShapeDtypeStruct((devices, 16, lanes), BF16),
            jax.ShapeDtypeStruct((8, lanes), F32),
        ],
        compiler_params=pltpu.CompilerParams(vmem_limit_bytes=VMEM_LIMIT),
        name="gather_terms",
    )(weight_part, projection_part.reshape(devices, lanes), bias_part, *after)


def torus_permute(value, move):
    pairs = []
    for z in range(RING):
        for y in range(RING):
            for x in range(RING):
                for s in range(2):
                    tx, ty, tz, ts = move(x, y, z, s)
                    tx, ty, tz = tx % RING, ty % RING, tz % RING
                    source = ((z * 2 + y // 2) * 8 + x * 2 + y % 2) * 2 + s
                    target = ((tz * 2 + ty // 2) * 8 + tx * 2 + ty % 2) * 2 + ts
                    pairs.append((source, target))
    return lax.ppermute(value, AXES, pairs)


def swap_cores(value):
    return torus_permute(value, lambda x, y, z, s: (x, y, z, 1 - s))


def swap_low_y(value):
    return torus_permute(value, lambda x, y, z, s: (x, y ^ 1, z, s))


def shift_z(value, steps):
    return torus_permute(value, lambda x, y, z, s: (x, y, z + steps, s))


def shift_x(value, steps):
    return torus_permute(value, lambda x, y, z, s: (x + steps, y, z, s))


def transpose_xz(value):
    return torus_permute(value, lambda x, y, z, s: (z, SWAP_Y[y], x, s))


def body(
    alignment_features,
    norm_gain_vector,
    norm_offset_vector,
    projection_weight,
    output_weight,
    output_bias,
    pair_update_cotangent,
):
    half, residues, channels = alignment_features.shape
    width = projection_weight.shape[1] // 2
    pair_channels = output_weight.shape[1]
    rows, cols, _ = pair_update_cotangent.shape
    rows_total = residues * lax.axis_size("ia")
    quarter = half // RING
    inv_seqs = 1.0 / (half * 2)
    x = lax.axis_index("ja") // 2
    low_y = lax.axis_index("ja") % 2
    z = lax.axis_index("ia") // 2
    core = lax.axis_index("sa")
    features = pltpu.with_memory_space_constraint(alignment_features, pltpu.HBM)
    cotangent = pair_update_cotangent
    gain_row = norm_gain_vector.reshape(1, -1)
    offset_row = norm_offset_vector.reshape(1, -1)
    weight_rows = projection_weight.T

    right_piece = project(
        x * 2,
        quarter,
        x * 0,
        residues,
        features,
        pltpu.with_memory_space_constraint(gain_row, pltpu.HBM),
        pltpu.with_memory_space_constraint(offset_row, pltpu.HBM),
        weight_rows[width:],
    )
    arrived = transpose_xz(right_piece.reshape(quarter, width * residues))

    def left_rows(part):
        return project(
            z,
            half,
            part,
            rows,
            alignment_features,
            gain_row,
            offset_row,
            weight_rows[:width],
            after=(right_piece,),
        )

    left_came = swap_cores(left_rows(1 - core)).transpose(2, 1, 0)
    left_kept = left_rows(core).transpose(2, 1, 0)
    own_left = jnp.concatenate([left_kept, left_came], axis=2).reshape(rows * width, 2 * half)

    arrived = add_up([arrived], after=(own_left,))
    right_pieces = [arrived] + [shift_z(arrived, -t) for t in range(1, RING)]
    right_cols = right_pieces + [swap_cores(piece) for piece in right_pieces]

    weight_dc = (
        output_weight.reshape(width, width, pair_channels)
        .transpose(1, 0, 2)
        .reshape(width * width, pair_channels)
    )
    blocks = rows // ROWS_AT_ONCE
    part = right_grad_part(
        0, blocks // 2, cotangent, weight_dc, own_left, None, after=(arrived,)
    )
    right_partial, _, bias_partial = right_grad_part(
        blocks // 2,
        blocks // 2,
        cotangent,
        weight_dc,
        own_left,
        part,
        after=tuple(right_pieces[1:]),
    )

    right_sum = add_up([right_partial[:half], swap_cores(right_partial[half:])])
    pieces = [right_sum[t * quarter : (t + 1) * quarter] for t in range(RING)]
    right_came = [shift_z(pieces[t], t) for t in range(1, RING)]
    left_partial = left_grad_part(
        lax.rem(z - x + RING, RING),
        right_cols,
        cotangent,
        weight_dc,
        after=(right_sum,),
    )

    left_came = [shift_x(left_partial[t], t) for t in range(1, RING)]
    right_sum = transpose_xz(add_up([pieces[0], *right_came], after=(left_partial,)))

    def pair_part(first, count, before, after):
        return pair_and_weight_grad(
            first,
            count,
            right_cols,
            own_left,
            weight_dc.T,
            output_bias,
            cotangent,
            before,
            after,
        )

    pair = pair_part(0, 4, None, (left_partial,))
    left_sum = add_up([left_partial[0], *left_came], after=(pair[1],))

    left_other, right_other = swap_low_y(left_sum), swap_low_y(right_sum)
    pair = pair_part(4, 2, pair, (left_sum,))
    left_sum = add_up([left_sum, left_other], inv_seqs, after=(pair[1],))
    right_grad = add_up([right_sum, right_other], inv_seqs, after=(pair[1],))

    left_own, left_came = left_sum[:quarter], swap_cores(left_sum[quarter:])
    left_low = jnp.where(core == 0, left_own, left_came).reshape(quarter, rows, width)
    left_high = jnp.where(core == 0, left_came, left_own).reshape(quarter, rows, width)
    left_grad = jnp.concatenate(
        [left_low.transpose(0, 2, 1), left_high.transpose(0, 2, 1)], axis=2
    )
    grads = jnp.concatenate([left_grad, right_grad.reshape(quarter, width, residues)], axis=1)
    grad_pieces = [grads] + [shift_x(grads, -t) for t in range(1, RING)]

    pair_update_result, weight_partial = pair_part(6, blocks - 6, pair, (grads,))
    projection_part = projection_grad_part(x, low_y, features, gain_row, offset_row, grads)
    devices = 128
    terms, token = gather_terms(
        devices, weight_partial, projection_part, bias_partial, after=tuple(grad_pieces[1:])
    )

    came = lax.all_to_all(terms, AXES, 0, 0, tiled=True)

    def norm_part(first, before, after):
        pieces = grad_pieces[first : first + 2]
        place = lax.rem(x + first, RING)
        return norm_grad(
            place, pieces, alignment_features, gain_row, weight_rows, before, after
        )

    alignment_gradient, token = norm_part(0, None, (token,))
    share, spread = add_terms(came, 1.0 / rows_total, after=(token,))
    bias_sum = share[9] + share[10]
    everything = lax.all_to_all(spread, AXES, 0, 0, tiled=True).astype(F32)
    alignment_gradient, _ = norm_part(2, alignment_gradient, (share,))
    weight_sum = (
        everything[:, :8]
        .reshape(width, width, pair_channels)
        .transpose(1, 0, 2)
        .reshape(width * width, pair_channels)
    )
    projection_sum = everything[:, 8].reshape(2 * width, channels).T

    return (
        pair_update_result,
        alignment_gradient,
        projection_sum,
        weight_sum,
        bias_sum,
    )


def solution(mesh):
    in_specs = (P("sa", "ia", None), P(), P(), P(), P(), P(), P(("ia", "sa"), "ja", None))
    out_specs = (P(("ia", "sa"), "ja", None), P("sa", "ia", None), P(), P(), P())
    return jax.shard_map(body, mesh=mesh, in_specs=in_specs, out_specs=out_specs, check_vma=False)
```

time: 198 us -> 151 us (0.76)
  starting transfers between devices: 80.7 us -> 56.3 us
  waiting for transfers between devices: 32.6 us -> 15.9 us
  other arithmetic: 7.71 us -> 1.14 us
  Pallas kernels: 57.5 us -> 61.8 us
  local copies, waits for them, and re-layouts: 17.5 us -> 13.8 us
    ppermute x26 -> x23, waiting for transfers between devices: 22.5 us -> 3.94 us  [torus_permute(): return lax.ppermute(value, AXES, pairs)]
    all_to_all x3 -> x2, starting transfers between devices: 31 us -> 15.3 us  [the longest x1 11.5 us: body(): came = lax.all_to_all(terms, AXES, 0, 0, tiled=True)]
    ppermute x26 -> x23, starting transfers between devices: 49.8 us -> 41 us  [torus_permute(): return lax.ppermute(value, AXES, pairs)]
    pallas_call x7 -> x20, Pallas kernels: 57.5 us -> 61.8 us  [the longest x3 15.2 us: pair_and_weight_grad(): pl.pallas_call(functools.partial(pair_kernel, fresh), grid=(count,), in_s...]
    dynamic_slice x4 -> x0, local copies, waits for them, and re-layouts: 2.42 us -> none  [the longest x1 1.31 us: body(): lax.dynamic_slice_in_dim(alignment_features, x * quarter, quarter, 0)]
    all_to_all x3 -> x2, waiting for transfers between devices: 10.1 us -> 12 us  [the longest x1 6.18 us: body(): came = lax.all_to_all(terms, AXES, 0, 0, tiled=True)]
  transfers between devices with their start and end apart: 29 -> 25, of which waited for: 12 -> 6; matrix products, arithmetic and copies ran while one was open for 6% -> 2% of each run, Pallas kernels for 27% -> 32%
where the time goes in v1:
time: 151 us; the launch traced here: 150 us
  Pallas kernels  61.8 us (41%)
  starting transfers between devices  56.3 us (37%)
  waiting for transfers between devices  15.9 us (11%)
  local copies, waits for them, and re-layouts  13.8 us (9%)
    ppermute x23, starting transfers between devices, torus_permute(): return lax.ppermute(value, AXES, pairs)  41 us
    pallas_call x3, Pallas kernels, pair_and_weight_grad(): pl.pallas_call(functools.partial(pair_kernel, fresh), grid=(count,), in_s...  15.2 us
    all_to_all x1, starting transfers between devices, body(): came = lax.all_to_all(terms, AXES, 0, 0, tiled=True)  11.5 us
    pallas_call x2, Pallas kernels, norm_grad(): pl.pallas_call(functools.partial(norm_grad_kernel, len(pieces)), grid_spe...  11.2 us
    pallas_call x1, Pallas kernels, left_grad_part(): pl.pallas_call(left_grad_kernel, grid_spec=pltpu.PrefetchScalarGridSpec(n...  11.2 us
    pallas_call x2, Pallas kernels, right_grad_part(): pl.pallas_call(functools.partial(right_grad_kernel, fresh), grid=(count,)...  9.98 us
    pallas_call x3, Pallas kernels, project(): pl.pallas_call(project_kernel, grid_spec=pltpu.PrefetchScalarGridSpec(num...  9.87 us
    unnamed x24, local copies, waits for them, and re-layouts  7.65 us
  transfers between devices with their start and end apart: 25, of which 6 were waited for; matrix products, arithmetic and copies ran while one was open for 2% of the time, Pallas kernels for 32%

profile of v1, /device:TPU:1, one launch (start us, length us, event | category | flops | bytes accessed | tf_op | source)
XLA Modules:
  0.0 150.1 jit_solution(3467893009768506746)
XLA Ops:
  1.6 3.1 %project.3.refs_0_ = bf16[16,32,128]{2,1,0:T(8,128)(2,1)S(1)} custom-call(s32[2]{0:T(128)S(1)} %pad_add_fusion.place_ref, bf16[64,128,256]{2,1,0:T(8,128)(2,1)} %features_ref.11, f32[1,256]{1,0:T(1,128)} %bitcast.63, f32[1,256]{1,0:T(1,128)} %bitcast.69, bf16[32,256]{1,0:T(8,128)(2,1)S(1)} %get-tuple-element.52.weight_ref), custom_call_target="tpu_custom_call" | custom-call | flops 67108864 | bytes 1179648 | tf_op jit(solution)/shard_map/project/pallas_call | solution.py:85
  4.7 3.4 %project.5 = bf16[64,32,64]{2,1,0:T(8,128)(2,1)S(1)} custom-call(s32[2]{0:T(128)S(1)} %get-tuple-element.54.place_ref, bf16[64,128,256]{2,1,0:T(8,128)(2,1)S(1)} %copy-done, f32[1,256]{1,0:T(1,128)S(1)} %bitcast.64, f32[1,256]{1,0:T(1,128)S(1)} %bitcast.70, bf16[32,256]{1,0:T(8,128)(2,1)S(1)} %get-tuple-element.51.weight_ref, ...), custom_call_target="tpu_custom_call" | custom-call | flops 134217728 | bytes 2359296 | tf_op jit(solution)/shard_map/project/pallas_call | solution.py:85
  10.4 3.4 %project.4 = bf16[64,32,64]{2,1,0:T(8,128)(2,1)S(1)} custom-call(s32[2]{0:T(128)S(1)} %get-tuple-element.53.place_ref, bf16[64,128,256]{2,1,0:T(8,128)(2,1)S(1)} %copy-done, f32[1,256]{1,0:T(1,128)S(1)} %bitcast.65, f32[1,256]{1,0:T(1,128)S(1)} %bitcast.71, bf16[32,256]{1,0:T(8,128)(2,1)S(1)} %get-tuple-element.51.weight_ref, ...), custom_call_target="tpu_custom_call" | custom-call | flops 134217728 | bytes 2359296 | tf_op jit(solution)/shard_map/project/pallas_call | solution.py:85
  15.7 3.8 %collective-permute-start.4 = (bf16[16,4096]{1,0:T(8,128)(2,1)S(1)}, bf16[16,4096]{1,0:T(8,128)(2,1)S(1)}, u32[]{:S(2)}, u32[]{:S(2)}) collective-permute-start(bf16[16,4096]{1,0:T(8,128)(2,1)S(1)} %add_up.6.refs_0_), channel_id=1, source_target_pairs={{0,32},{1,33},{4,36},{5,37},{8,40},{9,41},{12,44},{13,45},{2,34},{... | collective-permute-start | bytes 393224 | tf_op jit(solution)/shard_map/ppermute | solution.py:532
  19.4 8.6 %collective-permute-start.3 = (bf16[16,4096]{1,0:T(8,128)(2,1)S(1)}, bf16[16,4096]{1,0:T(8,128)(2,1)S(1)}, u32[]{:S(2)}, u32[]{:S(2)}) collective-permute-start(bf16[16,4096]{1,0:T(8,128)(2,1)S(1)} %add_up.6.refs_0_), channel_id=1, source_target_pairs={{0,64},{1,65},{4,68},{5,69},{8,72},{9,73},{12,76},{13,77},{2,66},{... | collective-permute-start | bytes 393224 | tf_op jit(solution)/shard_map/ppermute | solution.py:532
  29.6 4.3 %right_grad.2 = (bf16[8,128]{1,0:T(8,128)(2,1)}, f32[128,4096]{1,0:T(8,128)S(1)}, f32[8,128]{1,0:T(8,128)S(1)}) custom-call(bf16[64,128,128]{2,1,0:T(8,128)(2,1)S(1)} %copy-done.6, bf16[1024,128]{1,0:T(8,128)(2,1)S(1)} %bitcast.52, bf16[2048,128]{1,0:T(8,128)(2,1)S(1)} %bitcast.46, ...), custom_call_target="tpu_custom_call" | custom-call | flops 2147483648 | bytes 1048576 | tf_op jit(solution)/shard_map/right_grad/pallas_call | solution.py:161
  34.0 5.6 %right_grad.3 = (bf16[128,4096]{1,0:T(8,128)(2,1)S(1)}, f32[128,4096]{1,0:T(8,128)}, f32[8,128]{1,0:T(8,128)S(1)}) custom-call(bf16[64,128,128]{2,1,0:T(8,128)(2,1)S(1)} %copy-done.6, bf16[1024,128]{1,0:T(8,128)(2,1)S(1)} %bitcast.53, bf16[2048,128]{1,0:T(8,128)(2,1)S(1)} %bitcast.47, f32[128,4096]{1,0:T(8,128)S(1)} %get-tuple-element.22.total_in_ref, ...), custom_call_target="tpu_custom_call" | custom-call | flops 2147483648 | bytes 1048576 | tf_op jit(solution)/shard_map/right_grad/pallas_call | solution.py:161
  47.3 11.2 %left_grad.1.refs_13_.refs_4_ = bf16[4,32,2048]{2,1,0:T(8,128)(2,1)S(1)} custom-call(s32[1]{0:T(128)} %bitcast.15.turn_ref, bf16[16,4096]{1,0:T(8,128)(2,1)S(1)} %add_up.6.refs_0_, bf16[16,4096]{1,0:T(8,128)(2,1)S(1)} %collective-permute-done.2.refs_0_.refs_1_, bf16[16,4096]{1,0:T(8,128)(2,1)S(1)} %collective-permute-done.3.refs_1_.refs_2_, ...), custom_call_target="tpu_custom_call" | custom-call | flops 8589934592 | bytes 2097152 | tf_op jit(solution)/shard_map/left_grad/pallas_call | solution.py:225
  60.2 7.2 %pair_update.3 = (bf16[64,128,128]{2,1,0:T(8,128)(2,1)}, f32[1024,128]{1,0:T(8,128)S(1)}) custom-call(bf16[16,4096]{1,0:T(8,128)(2,1)S(1)} %add_up.6.refs_0_, bf16[16,4096]{1,0:T(8,128)(2,1)S(1)} %collective-permute-done.2.refs_0_.refs_1_, bf16[16,4096]{1,0:T(8,128)(2,1)S(1)} %collective-permute-done.3.refs_1_.refs_2_, ...), custom_call_target="tpu_custom_call" | custom-call | flops 6442450944 | bytes 2097152 | tf_op jit(solution)/shard_map/pair_update/pallas_call | solution.py:334
  68.3 7.9 %collective-permute-start.13 = (bf16[32,2048]{1,0:T(8,128)(2,1)S(1)}, bf16[32,2048]{1,0:T(8,128)(2,1)S(1)}, u32[]{:S(2)}, u32[]{:S(2)}) collective-permute-start(bf16[32,2048]{1,0:T(8,128)(2,1)S(1)} %add_up.8.refs_13_.refs_0_), channel_id=1, source_target_pairs={{0,2},{1,3},{4,6},{5,7},{8,10},{9,11},{12,14},{13,15},{2,0},{3,1},... | collective-permute-start | bytes 393224 | tf_op jit(solution)/shard_map/ppermute | solution.py:532
  76.2 4.0 %pair_update.4 = (bf16[64,128,128]{2,1,0:T(8,128)(2,1)}, f32[1024,128]{1,0:T(8,128)S(1)}) custom-call(bf16[16,4096]{1,0:T(8,128)(2,1)S(1)} %add_up.6.refs_0_, bf16[16,4096]{1,0:T(8,128)(2,1)S(1)} %collective-permute-done.2.refs_0_.refs_1_, bf16[16,4096]{1,0:T(8,128)(2,1)S(1)} %collective-permute-done.3.refs_1_.refs_2_, ...), custom_call_target="tpu_custom_call", output_to_operand_aliasing={{0}: (14, {})} | custom-call | flops 3221225472 | bytes 1048576 | tf_op jit(solution)/shard_map/pair_update/pallas_call | solution.py:334
  80.3 2.3 %collective-permute-start.14 = (bf16[16,2048]{1,0:T(8,128)(2,1)S(1)}, bf16[16,2048]{1,0:T(8,128)(2,1)S(1)}, u32[]{:S(2)}, u32[]{:S(2)}) collective-permute-start(bf16[16,2048]{1,0:T(8,128)(2,1)S(1)} %slice.80), channel_id=1, source_target_pairs={{0,1},{1,0},{4,5},{5,4},{8,9},{9,8},{12,13},{13,12},{2,3},{3,2},{6... | collective-permute-start | bytes 196616 | tf_op jit(solution)/shard_map/ppermute | solution.py:532
  84.2 2.3 %collective-permute-done.19.refs_1_ = bf16[16,4096]{1,0:T(8,128)(2,1)S(1)} collective-permute-done((bf16[16,4096]{1,0:T(8,128)(2,1)S(1)}, bf16[16,4096]{1,0:T(8,128)(2,1)S(1)}, u32[]{:S(2)}, u32[]{:S(2)}) %collective-permute-start.19) | collective-permute-done | bytes 131104 | tf_op jit(solution)/shard_map/ppermute | solution.py:532
  86.7 6.0 %collective-permute-start.22 = (bf16[16,64,128]{2,1,0:T(8,128)(2,1)S(1)}, bf16[16,64,128]{2,1,0:T(8,128)(2,1)S(1)}, u32[]{:S(2)}, u32[]{:S(2)}) collective-permute-start(bf16[16,64,128]{2,1,0:T(8,128)(2,1)S(1)} %pad_maximum_fusion.1.refs_13_.grads_ref.refs_0_), channel_id=1, source_target_pairs={{0,12},{1,13},{4,0},{5,1},{8,4},{9,5},{12,8},{13,9},{2,14},{3,15},... | collective-permute-start | bytes 786440 | tf_op jit(solution)/shard_map/ppermute | solution.py:532
  93.9 2.2 %projection_grad.1 = f32[64,256]{1,0:T(8,128)S(1)} custom-call(s32[2]{0:T(128)S(1)} %pad_add_fusion.3.place_ref, bf16[64,128,256]{2,1,0:T(8,128)(2,1)} %features_ref.11, f32[1,256]{1,0:T(1,128)S(1)} %bitcast.66, f32[1,256]{1,0:T(1,128)S(1)} %bitcast.72, bf16[16,64,128]{2,1,0:T(8,128)(2,1)S(1)} %pad_maximum_fusion.1.refs_13_.grads_ref.refs_0_), custom_call_target="tpu_custom_call" | custom-call | tf_op jit(solution)/shard_map/projection_grad/pallas_call | solution.py:377
  97.7 4.0 %pair_update.5 = (bf16[64,128,128]{2,1,0:T(8,128)(2,1)}, f32[1024,128]{1,0:T(8,128)S(1)}) custom-call(bf16[16,4096]{1,0:T(8,128)(2,1)S(1)} %add_up.6.refs_0_, bf16[16,4096]{1,0:T(8,128)(2,1)S(1)} %collective-permute-done.2.refs_0_.refs_1_, bf16[16,4096]{1,0:T(8,128)(2,1)S(1)} %collective-permute-done.3.refs_1_.refs_2_, ...), custom_call_target="tpu_custom_call", output_to_operand_aliasing={{0}: (14, {})} | custom-call | flops 3221225472 | bytes 1048576 | tf_op jit(solution)/shard_map/pair_update/pallas_call | solution.py:334
  103.6 11.5 %all-to-all-start = ((bf16[128,16,128]{2,1,0:T(8,128)(2,1)}), bf16[128,16,128]{2,1,0:T(8,128)(2,1)S(1)}, u32[]{:S(2)}, u32[]{:S(2)}) async-start(bf16[128,16,128]{2,1,0:T(8,128)(2,1)} %get-tuple-element.32), calls=%async_computation | async-start | bytes 1048576 | tf_op jit(solution)/shard_map/all_to_all | solution.py:684
  115.1 2.2 %copy-done.1 = bf16[64,128,256]{2,1,0:T(8,128)(2,1)S(1)} copy-done((bf16[64,128,256]{2,1,0:T(8,128)(2,1)S(1)}, bf16[64,128,256]{2,1,0:T(8,128)(2,1)}, u32[]{:S(2)}) %copy-start.1) | copy-done | bytes 4194328
  117.3 5.6 %norm_grad.2 = (bf16[64,128,256]{2,1,0:T(8,128)(2,1)}, f32[8,128]{1,0:T(8,128)S(1)}) custom-call(s32[1]{0:T(128)} %bitcast.25.first_ref, bf16[64,128,256]{2,1,0:T(8,128)(2,1)S(1)} %copy-done.1, f32[1,256]{1,0:T(1,128)S(1)} %bitcast.67, bf16[64,256]{1,0:T(8,128)(2,1)S(1)} %bitcast.58, bf16[16,64,128]{2,1,0:T(8,128)(2,1)S(1)} %pad_maximum_fusion.1.refs_13_.grads_ref.refs_0_, ...), custom_call_target="tpu_custom_call" | custom-call | flops 268435456 | bytes 4194304 | tf_op jit(solution)/shard_map/norm_grad/pallas_call | solution.py:439
  122.9 6.2 %all-to-all-done.terms_ref = bf16[128,16,128]{2,1,0:T(8,128)(2,1)S(1)} async-done(((bf16[128,16,128]{2,1,0:T(8,128)(2,1)}), bf16[128,16,128]{2,1,0:T(8,128)(2,1)S(1)}, u32[]{:S(2)}, u32[]{:S(2)}) %all-to-all-start) | async-done | bytes 524320 | tf_op jit(solution)/shard_map/all_to_all | solution.py:684
  130.1 3.8 %all-to-all-start.1 = ((bf16[128,16,128]{2,1,0:T(8,128)(2,1)}), bf16[128,16,128]{2,1,0:T(8,128)(2,1)S(1)}, u32[]{:S(2)}, u32[]{:S(2)}) async-start(bf16[128,16,128]{2,1,0:T(8,128)(2,1)} %get-tuple-element.38), calls=%async_computation.1 | async-start | bytes 1048576 | tf_op jit(solution)/shard_map/all_to_all | solution.py:696
  133.9 2.2 %copy-done.2 = bf16[64,128,256]{2,1,0:T(8,128)(2,1)S(1)} copy-done((bf16[64,128,256]{2,1,0:T(8,128)(2,1)S(1)}, bf16[64,128,256]{2,1,0:T(8,128)(2,1)}, u32[]{:S(2)}) %copy-start.2) | copy-done | bytes 4194328
  136.1 5.6 %norm_grad.3 = (bf16[64,128,256]{2,1,0:T(8,128)(2,1)}, f32[8,128]{1,0:T(8,128)}) custom-call(s32[1]{0:T(128)} %bitcast.22.first_ref, bf16[64,128,256]{2,1,0:T(8,128)(2,1)S(1)} %copy-done.2, f32[1,256]{1,0:T(1,128)S(1)} %bitcast.68, bf16[64,256]{1,0:T(8,128)(2,1)S(1)} %bitcast.59, ...), custom_call_target="tpu_custom_call", output_to_operand_aliasing={{0}: (7, {})} | custom-call | flops 268435456 | bytes 4194304 | tf_op jit(solution)/shard_map/norm_grad/pallas_call | solution.py:439
  142.2 5.8 %all-to-all-done.1 = bf16[128,16,128]{2,1,0:T(8,128)(2,1)S(1)} async-done(((bf16[128,16,128]{2,1,0:T(8,128)(2,1)}), bf16[128,16,128]{2,1,0:T(8,128)(2,1)S(1)}, u32[]{:S(2)}, u32[]{:S(2)}) %all-to-all-start.1) | async-done | bytes 524320 | tf_op jit(solution)/shard_map/all_to_all | solution.py:696
  (96 shorter events, 26.8 us)
Async XLA Ops:
  8.1 5.8 %collective-permute-start.1 = (bf16[64,32,64]{2,1,0:T(8,128)(2,1)S(1)}, bf16[64,32,64]{2,1,0:T(8,128)(2,1)S(1)}, u32[]{:S(2)}, u32[]{:S(2)}) collective-permute-start(bf16[64,32,64]{2,1,0:T(8,128)(2,1)S(1)} %project.5), channel_id=1, source_target_pairs={{0,1},{1,0},{4,5},{5,4},{8,9},{9,8},{12,13},{13,12},{2,3},{3,2},{6... | collective-permute-start | bytes 786440 | tf_op jit(solution)/shard_map/ppermute | solution.py:532
  9.6 6.0 %collective-permute-start = (bf16[16,4096]{1,0:T(8,128)(2,1)S(1)}, bf16[16,4096]{1,0:T(8,128)(2,1)S(1)}, u32[]{:S(2)}, u32[]{:S(2)}) collective-permute-start(bf16[16,4096]{1,0:T(8,128)(2,1)S(1)} %bitcast.83), channel_id=1, source_target_pairs={{0,0},{1,1},{4,32},{5,33},{8,64},{9,65},{12,96},{13,97},{2,16},{3,... | collective-permute-start | bytes 393224 | tf_op jit(solution)/shard_map/ppermute | solution.py:532
  15.7 18.3 %collective-permute-start.4 = (bf16[16,4096]{1,0:T(8,128)(2,1)S(1)}, bf16[16,4096]{1,0:T(8,128)(2,1)S(1)}, u32[]{:S(2)}, u32[]{:S(2)}) collective-permute-start(bf16[16,4096]{1,0:T(8,128)(2,1)S(1)} %add_up.6.refs_0_), channel_id=1, source_target_pairs={{0,32},{1,33},{4,36},{5,37},{8,40},{9,41},{12,44},{13,45},{2,34},{... | collective-permute-start | bytes 393224 | tf_op jit(solution)/shard_map/ppermute | solution.py:532
  19.4 14.6 %collective-permute-start.3 = (bf16[16,4096]{1,0:T(8,128)(2,1)S(1)}, bf16[16,4096]{1,0:T(8,128)(2,1)S(1)}, u32[]{:S(2)}, u32[]{:S(2)}) collective-permute-start(bf16[16,4096]{1,0:T(8,128)(2,1)S(1)} %add_up.6.refs_0_), channel_id=1, source_target_pairs={{0,64},{1,65},{4,68},{5,69},{8,72},{9,73},{12,76},{13,77},{2,66},{... | collective-permute-start | bytes 393224 | tf_op jit(solution)/shard_map/ppermute | solution.py:532
  28.0 6.0 %collective-permute-start.2 = (bf16[16,4096]{1,0:T(8,128)(2,1)S(1)}, bf16[16,4096]{1,0:T(8,128)(2,1)S(1)}, u32[]{:S(2)}, u32[]{:S(2)}) collective-permute-start(bf16[16,4096]{1,0:T(8,128)(2,1)S(1)} %add_up.6.refs_0_), channel_id=1, source_target_pairs={{0,96},{1,97},{4,100},{5,101},{8,104},{9,105},{12,108},{13,109},{2... | collective-permute-start | bytes 393224 | tf_op jit(solution)/shard_map/ppermute | solution.py:532
  42.0 3.7 %collective-permute-start.5 = (bf16[16,4096]{1,0:T(8,128)(2,1)S(1)}, bf16[16,4096]{1,0:T(8,128)(2,1)S(1)}, u32[]{:S(2)}, u32[]{:S(2)}) collective-permute-start(bf16[16,4096]{1,0:T(8,128)(2,1)S(1)} %add_up.6.refs_0_), channel_id=1, source_target_pairs={{0,1},{1,0},{4,5},{5,4},{8,9},{9,8},{12,13},{13,12},{2,3},{3,2},{6... | collective-permute-start | bytes 393224 | tf_op jit(solution)/shard_map/ppermute | solution.py:532
  42.1 5.2 %collective-permute-start.8 = (bf16[16,4096]{1,0:T(8,128)(2,1)S(1)}, bf16[16,4096]{1,0:T(8,128)(2,1)S(1)}, u32[]{:S(2)}, u32[]{:S(2)}) collective-permute-start(bf16[16,4096]{1,0:T(8,128)(2,1)S(1)} %collective-permute-done.4.refs_2_.refs_3_), channel_id=1, source_target_pairs={{0,1},{1,0},{4,5},{5,4},{8,9},{9,8},{12,13},{13,12},{2,3},{3,2},{6... | collective-permute-start | bytes 393224 | tf_op jit(solution)/shard_map/ppermute | solution.py:532
  42.6 4.7 %collective-permute-start.7 = (bf16[16,4096]{1,0:T(8,128)(2,1)S(1)}, bf16[16,4096]{1,0:T(8,128)(2,1)S(1)}, u32[]{:S(2)}, u32[]{:S(2)}) collective-permute-start(bf16[16,4096]{1,0:T(8,128)(2,1)S(1)} %collective-permute-done.3.refs_1_.refs_2_), channel_id=1, source_target_pairs={{0,1},{1,0},{4,5},{5,4},{8,9},{9,8},{12,13},{13,12},{2,3},{3,2},{6... | collective-permute-start | bytes 393224 | tf_op jit(solution)/shard_map/ppermute | solution.py:532
  42.7 4.6 %collective-permute-start.6 = (bf16[16,4096]{1,0:T(8,128)(2,1)S(1)}, bf16[16,4096]{1,0:T(8,128)(2,1)S(1)}, u32[]{:S(2)}, u32[]{:S(2)}) collective-permute-start(bf16[16,4096]{1,0:T(8,128)(2,1)S(1)} %collective-permute-done.2.refs_0_.refs_1_), channel_id=1, source_target_pairs={{0,1},{1,0},{4,5},{5,4},{8,9},{9,8},{12,13},{13,12},{2,3},{3,2},{6... | collective-permute-start | bytes 393224 | tf_op jit(solution)/shard_map/ppermute | solution.py:532
  43.7 15.9 %collective-permute-start.17 = (bf16[16,4096]{1,0:T(8,128)(2,1)S(1)}, bf16[16,4096]{1,0:T(8,128)(2,1)S(1)}, u32[]{:S(2)}, u32[]{:S(2)}) collective-permute-start(bf16[16,4096]{1,0:T(8,128)(2,1)S(1)} %get-tuple-element.41), channel_id=1, source_target_pairs={{0,96},{1,97},{4,100},{5,101},{8,104},{9,105},{12,108},{13,109},{2... | collective-permute-start | bytes 393224 | tf_op jit(solution)/shard_map/ppermute | solution.py:532
  45.7 21.8 %collective-permute-start.16 = (bf16[16,4096]{1,0:T(8,128)(2,1)S(1)}, bf16[16,4096]{1,0:T(8,128)(2,1)S(1)}, u32[]{:S(2)}, u32[]{:S(2)}) collective-permute-start(bf16[16,4096]{1,0:T(8,128)(2,1)S(1)} %get-tuple-element.42), channel_id=1, source_target_pairs={{0,64},{1,65},{4,68},{5,69},{8,72},{9,73},{12,76},{13,77},{2,66},{... | collective-permute-start | bytes 393224 | tf_op jit(solution)/shard_map/ppermute | solution.py:532
  47.2 20.2 %collective-permute-start.15 = (bf16[16,4096]{1,0:T(8,128)(2,1)S(1)}, bf16[16,4096]{1,0:T(8,128)(2,1)S(1)}, u32[]{:S(2)}, u32[]{:S(2)}) collective-permute-start(bf16[16,4096]{1,0:T(8,128)(2,1)S(1)} %get-tuple-element.43), channel_id=1, source_target_pairs={{0,32},{1,33},{4,36},{5,37},{8,40},{9,41},{12,44},{13,45},{2,34},{... | collective-permute-start | bytes 393224 | tf_op jit(solution)/shard_map/ppermute | solution.py:532
  58.5 9.7 %collective-permute-start.12 = (bf16[32,2048]{1,0:T(8,128)(2,1)S(1)}, bf16[32,2048]{1,0:T(8,128)(2,1)S(1)}, u32[]{:S(2)}, u32[]{:S(2)}) collective-permute-start(bf16[32,2048]{1,0:T(8,128)(2,1)S(1)} %get-tuple-element.45), channel_id=1, source_target_pairs={{0,12},{1,13},{4,0},{5,1},{8,4},{9,5},{12,8},{13,9},{2,14},{3,15},... | collective-permute-start | bytes 393224 | tf_op jit(solution)/shard_map/ppermute | solution.py:532
  58.9 9.3 %collective-permute-start.11 = (bf16[32,2048]{1,0:T(8,128)(2,1)S(1)}, bf16[32,2048]{1,0:T(8,128)(2,1)S(1)}, u32[]{:S(2)}, u32[]{:S(2)}) collective-permute-start(bf16[32,2048]{1,0:T(8,128)(2,1)S(1)} %get-tuple-element.46), channel_id=1, source_target_pairs={{0,8},{1,9},{4,12},{5,13},{8,0},{9,1},{12,4},{13,5},{2,10},{3,11},... | collective-permute-start | bytes 393224 | tf_op jit(solution)/shard_map/ppermute | solution.py:532
  59.6 8.6 %collective-permute-start.10 = (bf16[32,2048]{1,0:T(8,128)(2,1)S(1)}, bf16[32,2048]{1,0:T(8,128)(2,1)S(1)}, u32[]{:S(2)}, u32[]{:S(2)}) collective-permute-start(bf16[32,2048]{1,0:T(8,128)(2,1)S(1)} %get-tuple-element.47), channel_id=1, source_target_pairs={{0,4},{1,5},{4,8},{5,9},{8,12},{9,13},{12,0},{13,1},{2,6},{3,7},{6... | collective-permute-start | bytes 393224 | tf_op jit(solution)/shard_map/ppermute | solution.py:532
  67.5 15.1 %collective-permute-start.18 = (bf16[16,4096]{1,0:T(8,128)(2,1)S(1)}, bf16[16,4096]{1,0:T(8,128)(2,1)S(1)}, u32[]{:S(2)}, u32[]{:S(2)}) collective-permute-start(bf16[16,4096]{1,0:T(8,128)(2,1)S(1)} %add_up.10), channel_id=1, source_target_pairs={{0,0},{1,1},{4,32},{5,33},{8,64},{9,65},{12,96},{13,97},{2,16},{3,... | collective-permute-start | bytes 393224 | tf_op jit(solution)/shard_map/ppermute | solution.py:532
  68.3 11.9 %collective-permute-start.13 = (bf16[32,2048]{1,0:T(8,128)(2,1)S(1)}, bf16[32,2048]{1,0:T(8,128)(2,1)S(1)}, u32[]{:S(2)}, u32[]{:S(2)}) collective-permute-start(bf16[32,2048]{1,0:T(8,128)(2,1)S(1)} %add_up.8.refs_13_.refs_0_), channel_id=1, source_target_pairs={{0,2},{1,3},{4,6},{5,7},{8,10},{9,11},{12,14},{13,15},{2,0},{3,1},... | collective-permute-start | bytes 393224 | tf_op jit(solution)/shard_map/ppermute | solution.py:532
  80.3 3.2 %collective-permute-start.14 = (bf16[16,2048]{1,0:T(8,128)(2,1)S(1)}, bf16[16,2048]{1,0:T(8,128)(2,1)S(1)}, u32[]{:S(2)}, u32[]{:S(2)}) collective-permute-start(bf16[16,2048]{1,0:T(8,128)(2,1)S(1)} %slice.80), channel_id=1, source_target_pairs={{0,1},{1,0},{4,5},{5,4},{8,9},{9,8},{12,13},{13,12},{2,3},{3,2},{6... | collective-permute-start | bytes 196616 | tf_op jit(solution)/shard_map/ppermute | solution.py:532
  82.6 3.8 %collective-permute-start.19 = (bf16[16,4096]{1,0:T(8,128)(2,1)S(1)}, bf16[16,4096]{1,0:T(8,128)(2,1)S(1)}, u32[]{:S(2)}, u32[]{:S(2)}) collective-permute-start(bf16[16,4096]{1,0:T(8,128)(2,1)S(1)} %collective-permute-done.18.refs_0_), channel_id=1, source_target_pairs={{0,2},{1,3},{4,6},{5,7},{8,10},{9,11},{12,14},{13,15},{2,0},{3,1},... | collective-permute-start | bytes 393224 | tf_op jit(solution)/shard_map/ppermute | solution.py:532
  86.7 15.1 %collective-permute-start.22 = (bf16[16,64,128]{2,1,0:T(8,128)(2,1)S(1)}, bf16[16,64,128]{2,1,0:T(8,128)(2,1)S(1)}, u32[]{:S(2)}, u32[]{:S(2)}) collective-permute-start(bf16[16,64,128]{2,1,0:T(8,128)(2,1)S(1)} %pad_maximum_fusion.1.refs_13_.grads_ref.refs_0_), channel_id=1, source_target_pairs={{0,12},{1,13},{4,0},{5,1},{8,4},{9,5},{12,8},{13,9},{2,14},{3,15},... | collective-permute-start | bytes 786440 | tf_op jit(solution)/shard_map/ppermute | solution.py:532
  92.6 10.1 %collective-permute-start.21 = (bf16[16,64,128]{2,1,0:T(8,128)(2,1)S(1)}, bf16[16,64,128]{2,1,0:T(8,128)(2,1)S(1)}, u32[]{:S(2)}, u32[]{:S(2)}) collective-permute-start(bf16[16,64,128]{2,1,0:T(8,128)(2,1)S(1)} %pad_maximum_fusion.1.refs_13_.grads_ref.refs_0_), channel_id=1, source_target_pairs={{0,4},{1,5},{4,8},{5,9},{8,12},{9,13},{12,0},{13,1},{2,6},{3,7},{6... | collective-permute-start | bytes 786440 | tf_op jit(solution)/shard_map/ppermute | solution.py:532
  92.6 10.1 %collective-permute-start.20 = (bf16[16,64,128]{2,1,0:T(8,128)(2,1)S(1)}, bf16[16,64,128]{2,1,0:T(8,128)(2,1)S(1)}, u32[]{:S(2)}, u32[]{:S(2)}) collective-permute-start(bf16[16,64,128]{2,1,0:T(8,128)(2,1)S(1)} %pad_maximum_fusion.1.refs_13_.grads_ref.refs_0_), channel_id=1, source_target_pairs={{0,8},{1,9},{4,12},{5,13},{8,0},{9,1},{12,4},{13,5},{2,10},{3,11},... | collective-permute-start | bytes 786440 | tf_op jit(solution)/shard_map/ppermute | solution.py:532
  103.6 25.5 %all-to-all-start = ((bf16[128,16,128]{2,1,0:T(8,128)(2,1)}), bf16[128,16,128]{2,1,0:T(8,128)(2,1)S(1)}, u32[]{:S(2)}, u32[]{:S(2)}) async-start(bf16[128,16,128]{2,1,0:T(8,128)(2,1)} %get-tuple-element.32), calls=%async_computation | async-start | bytes 1048576 | tf_op jit(solution)/shard_map/all_to_all | solution.py:684
  130.1 18.0 %all-to-all-start.1 = ((bf16[128,16,128]{2,1,0:T(8,128)(2,1)}), bf16[128,16,128]{2,1,0:T(8,128)(2,1)S(1)}, u32[]{:S(2)}, u32[]{:S(2)}) async-start(bf16[128,16,128]{2,1,0:T(8,128)(2,1)} %get-tuple-element.38), calls=%async_computation.1 | async-start | bytes 1048576 | tf_op jit(solution)/shard_map/all_to_all | solution.py:696
  (12 other events, 57.1 us)

commit v2 on v1

--- a/solution.py
+++ b/solution.py
@@ -540,6 +540,10 @@
     return torus_permute(value, lambda x, y, z, s: (x, y ^ 1, z, s))
 
 
+def swap_both(value):
+    return torus_permute(value, lambda x, y, z, s: (x, y ^ 1, z, 1 - s))
+
+
 def shift_z(value, steps):
     return torus_permute(value, lambda x, y, z, s: (x, y, z + steps, s))
 
@@ -658,14 +662,16 @@
         )
 
     pair = pair_part(0, 4, None, (left_partial,))
-    left_sum = add_up([left_partial[0], *left_came], after=(pair[1],))
-
-    left_other, right_other = swap_low_y(left_sum), swap_low_y(right_sum)
+    left_sum = add_up([left_partial[0], *left_came], after=(pair[1], right_sum))
+
+    left_own, left_other = left_sum[:quarter], left_sum[quarter:]
+    own_beside, right_beside = swap_low_y(left_own), swap_low_y(right_sum)
+    other_here, other_beside = swap_cores(left_other), swap_both(left_other)
     pair = pair_part(4, 2, pair, (left_sum,))
-    left_sum = add_up([left_sum, left_other], inv_seqs, after=(pair[1],))
-    right_grad = add_up([right_sum, right_other], inv_seqs, after=(pair[1],))
-
-    left_own, left_came = left_sum[:quarter], swap_cores(left_sum[quarter:])
+    left_own = add_up([left_own, own_beside], inv_seqs, after=(pair[1],))
+    left_came = add_up([other_here, other_beside], inv_seqs, after=(pair[1],))
+    right_grad = add_up([right_sum, right_beside], inv_seqs, after=(pair[1],))
+
     left_low = jnp.where(core == 0, left_own, left_came).reshape(quarter, rows, width)
     left_high = jnp.where(core == 0, left_came, left_own).reshape(quarter, rows, width)
     left_grad = jnp.concatenate(
@@ -687,7 +693,7 @@
         pieces = grad_pieces[first : first + 2]
         place = lax.rem(x + first, RING)
         return norm_grad(
-            place, pieces, alignment_features, gain_row, weight_rows, before, after
+            place, pieces, features, gain_row, weight_rows, before, after
         )
 
     alignment_gradient, token = norm_part(0, None, (token,))

time: 151 us -> 148 us (0.980)
  local copies, waits for them, and re-layouts: 13.8 us -> 10.1 us
  Pallas kernels: 61.8 us -> 64.1 us
  starting transfers between devices: 56.3 us -> 54.2 us
    all_to_all x1, starting transfers between devices: 11.5 us -> 7.41 us  [body(): came = lax.all_to_all(terms, AXES, 0, 0, tiled=True)]
    unnamed x24 -> x22, local copies, waits for them, and re-layouts: 7.65 us -> 3.94 us
    pallas_call x2, Pallas kernels: 11.2 us -> 13.4 us  [norm_grad(): pl.pallas_call(functools.partial(norm_grad_kernel, len(pieces)), grid_spe...]
    ppermute x23 -> x24, starting transfers between devices: 41 us -> 43 us  [torus_permute(): return lax.ppermute(value, AXES, pairs)]
    ppermute x23 -> x24, waiting for transfers between devices: 3.94 us -> 2.99 us  [torus_permute(): return lax.ppermute(value, AXES, pairs)]
  transfers between devices with their start and end apart: 25 -> 26, of which waited for: 6 -> 5; matrix products, arithmetic and copies ran while one was open for 2% -> 2% of each run, Pallas kernels for 32% -> 34%
where the time goes in v2:
time: 148 us
  Pallas kernels  64.1 us (43%)
  starting transfers between devices  54.2 us (37%)
  waiting for transfers between devices  17.2 us (12%)
  local copies, waits for them, and re-layouts  10.1 us (7%)
    ppermute x24, starting transfers between devices, torus_permute(): return lax.ppermute(value, AXES, pairs)  43 us
    pallas_call x3, Pallas kernels, pair_and_weight_grad(): pl.pallas_call(functools.partial(pair_kernel, fresh), grid=(count,), in_s...  15.3 us
    pallas_call x2, Pallas kernels, norm_grad(): pl.pallas_call(functools.partial(norm_grad_kernel, len(pieces)), grid_spe...  13.4 us
    pallas_call x1, Pallas kernels, left_grad_part(): pl.pallas_call(left_grad_kernel, grid_spec=pltpu.PrefetchScalarGridSpec(n...  11.2 us
    pallas_call x2, Pallas kernels, right_grad_part(): pl.pallas_call(functools.partial(right_grad_kernel, fresh), grid=(count,)...  9.98 us
    pallas_call x3, Pallas kernels, project(): pl.pallas_call(project_kernel, grid_spec=pltpu.PrefetchScalarGridSpec(num...  9.87 us
    all_to_all x1, starting transfers between devices, body(): came = lax.all_to_all(terms, AXES, 0, 0, tiled=True)  7.41 us
    all_to_all x1, waiting for transfers between devices, body(): came = lax.all_to_all(terms, AXES, 0, 0, tiled=True)  7.28 us
  transfers between devices with their start and end apart: 26, of which 5 were waited for; matrix products, arithmetic and copies ran while one was open for 2% of the time, Pallas kernels for 34%

profile of v2, /device:TPU:1, one launch (start us, length us, event | category | flops | bytes accessed | tf_op | source)
XLA Modules:
  0.0 147.8 jit_solution(9079995441210482216)
XLA Ops:
  1.6 3.1 %project.3.refs_0_ = bf16[16,32,128]{2,1,0:T(8,128)(2,1)S(1)} custom-call(s32[2]{0:T(128)S(1)} %pad_add_fusion.place_ref, bf16[64,128,256]{2,1,0:T(8,128)(2,1)} %features_ref.11, f32[1,256]{1,0:T(1,128)} %bitcast.63, f32[1,256]{1,0:T(1,128)} %bitcast.69, bf16[32,256]{1,0:T(8,128)(2,1)S(1)} %get-tuple-element.54.weight_ref), custom_call_target="tpu_custom_call" | custom-call | flops 67108864 | bytes 1179648 | tf_op jit(solution)/shard_map/project/pallas_call | solution.py:85
  4.7 3.4 %project.5 = bf16[64,32,64]{2,1,0:T(8,128)(2,1)S(1)} custom-call(s32[2]{0:T(128)S(1)} %get-tuple-element.56.place_ref, bf16[64,128,256]{2,1,0:T(8,128)(2,1)S(1)} %copy-done, f32[1,256]{1,0:T(1,128)S(1)} %bitcast.64, f32[1,256]{1,0:T(1,128)S(1)} %bitcast.70, bf16[32,256]{1,0:T(8,128)(2,1)S(1)} %get-tuple-element.53.weight_ref, ...), custom_call_target="tpu_custom_call" | custom-call | flops 134217728 | bytes 2359296 | tf_op jit(solution)/shard_map/project/pallas_call | solution.py:85
  10.4 3.4 %project.4 = bf16[64,32,64]{2,1,0:T(8,128)(2,1)S(1)} custom-call(s32[2]{0:T(128)S(1)} %get-tuple-element.55.place_ref, bf16[64,128,256]{2,1,0:T(8,128)(2,1)S(1)} %copy-done, f32[1,256]{1,0:T(1,128)S(1)} %bitcast.65, f32[1,256]{1,0:T(1,128)S(1)} %bitcast.71, bf16[32,256]{1,0:T(8,128)(2,1)S(1)} %get-tuple-element.53.weight_ref, ...), custom_call_target="tpu_custom_call" | custom-call | flops 134217728 | bytes 2359296 | tf_op jit(solution)/shard_map/project/pallas_call | solution.py:85
  15.7 3.8 %collective-permute-start.4 = (bf16[16,4096]{1,0:T(8,128)(2,1)S(1)}, bf16[16,4096]{1,0:T(8,128)(2,1)S(1)}, u32[]{:S(2)}, u32[]{:S(2)}) collective-permute-start(bf16[16,4096]{1,0:T(8,128)(2,1)S(1)} %add_up.7.refs_0_), channel_id=1, source_target_pairs={{0,32},{1,33},{4,36},{5,37},{8,40},{9,41},{12,44},{13,45},{2,34},{... | collective-permute-start | bytes 393224 | tf_op jit(solution)/shard_map/ppermute | solution.py:532
  19.4 8.6 %collective-permute-start.3 = (bf16[16,4096]{1,0:T(8,128)(2,1)S(1)}, bf16[16,4096]{1,0:T(8,128)(2,1)S(1)}, u32[]{:S(2)}, u32[]{:S(2)}) collective-permute-start(bf16[16,4096]{1,0:T(8,128)(2,1)S(1)} %add_up.7.refs_0_), channel_id=1, source_target_pairs={{0,64},{1,65},{4,68},{5,69},{8,72},{9,73},{12,76},{13,77},{2,66},{... | collective-permute-start | bytes 393224 | tf_op jit(solution)/shard_map/ppermute | solution.py:532
  28.1 1.6 %copy-done.4 = bf16[64,128,128]{2,1,0:T(8,128)(2,1)S(1)} copy-done((bf16[64,128,128]{2,1,0:T(8,128)(2,1)S(1)}, bf16[64,128,128]{2,1,0:T(8,128)(2,1)}, u32[]{:S(2)}) %copy-start.4) | copy-done | bytes 2097176
  29.6 4.3 %right_grad.2 = (bf16[8,128]{1,0:T(8,128)(2,1)}, f32[128,4096]{1,0:T(8,128)S(1)}, f32[8,128]{1,0:T(8,128)S(1)}) custom-call(bf16[64,128,128]{2,1,0:T(8,128)(2,1)S(1)} %copy-done.4, bf16[1024,128]{1,0:T(8,128)(2,1)S(1)} %bitcast.52, bf16[2048,128]{1,0:T(8,128)(2,1)S(1)} %bitcast.46, ...), custom_call_target="tpu_custom_call" | custom-call | flops 2147483648 | bytes 1048576 | tf_op jit(solution)/shard_map/right_grad/pallas_call | solution.py:161
  34.0 5.6 %right_grad.3 = (bf16[128,4096]{1,0:T(8,128)(2,1)S(1)}, f32[128,4096]{1,0:T(8,128)}, f32[8,128]{1,0:T(8,128)S(1)}) custom-call(bf16[64,128,128]{2,1,0:T(8,128)(2,1)S(1)} %copy-done.4, bf16[1024,128]{1,0:T(8,128)(2,1)S(1)} %bitcast.53, bf16[2048,128]{1,0:T(8,128)(2,1)S(1)} %bitcast.47, f32[128,4096]{1,0:T(8,128)S(1)} %get-tuple-element.22.total_in_ref, ...), custom_call_target="tpu_custom_call" | custom-call | flops 2147483648 | bytes 1048576 | tf_op jit(solution)/shard_map/right_grad/pallas_call | solution.py:161
  43.7 1.9 %collective-permute-start.15 = (bf16[16,4096]{1,0:T(8,128)(2,1)S(1)}, bf16[16,4096]{1,0:T(8,128)(2,1)S(1)}, u32[]{:S(2)}, u32[]{:S(2)}) collective-permute-start(bf16[16,4096]{1,0:T(8,128)(2,1)S(1)} %get-tuple-element.41), channel_id=1, source_target_pairs={{0,96},{1,97},{4,100},{5,101},{8,104},{9,105},{12,108},{13,109},{2... | collective-permute-start | bytes 393224 | tf_op jit(solution)/shard_map/ppermute | solution.py:532
  47.3 11.2 %left_grad.1.refs_13_.refs_4_ = bf16[4,32,2048]{2,1,0:T(8,128)(2,1)S(1)} custom-call(s32[1]{0:T(128)} %bitcast.15.turn_ref, bf16[16,4096]{1,0:T(8,128)(2,1)S(1)} %add_up.7.refs_0_, bf16[16,4096]{1,0:T(8,128)(2,1)S(1)} %collective-permute-done.2.refs_0_.refs_1_, bf16[16,4096]{1,0:T(8,128)(2,1)S(1)} %collective-permute-done.3.refs_1_.refs_2_, ...), custom_call_target="tpu_custom_call" | custom-call | flops 8589934592 | bytes 2097152 | tf_op jit(solution)/shard_map/left_grad/pallas_call | solution.py:225
  61.0 7.3 %pair_update.3 = (bf16[64,128,128]{2,1,0:T(8,128)(2,1)}, f32[1024,128]{1,0:T(8,128)S(1)}) custom-call(bf16[16,4096]{1,0:T(8,128)(2,1)S(1)} %add_up.7.refs_0_, bf16[16,4096]{1,0:T(8,128)(2,1)S(1)} %collective-permute-done.2.refs_0_.refs_1_, bf16[16,4096]{1,0:T(8,128)(2,1)S(1)} %collective-permute-done.3.refs_1_.refs_2_, ...), custom_call_target="tpu_custom_call" | custom-call | flops 6442450944 | bytes 2097152 | tf_op jit(solution)/shard_map/pair_update/pallas_call | solution.py:334
  68.4 13.6 %collective-permute-start.19 = (bf16[16,2048]{1,0:T(8,128)(2,1)S(1)}, bf16[16,2048]{1,0:T(8,128)(2,1)S(1)}, u32[]{:S(2)}, u32[]{:S(2)}) collective-permute-start(bf16[16,2048]{1,0:T(8,128)(2,1)S(1)} %get-tuple-element.52), channel_id=1, source_target_pairs={{0,3},{1,2},{4,7},{5,6},{8,11},{9,10},{12,15},{13,14},{2,1},{3,0},... | collective-permute-start | bytes 196616 | tf_op jit(solution)/shard_map/ppermute | solution.py:532
  83.5 4.0 %pair_update.4 = (bf16[64,128,128]{2,1,0:T(8,128)(2,1)}, f32[1024,128]{1,0:T(8,128)S(1)}) custom-call(bf16[16,4096]{1,0:T(8,128)(2,1)S(1)} %add_up.7.refs_0_, bf16[16,4096]{1,0:T(8,128)(2,1)S(1)} %collective-permute-done.2.refs_0_.refs_1_, bf16[16,4096]{1,0:T(8,128)(2,1)S(1)} %collective-permute-done.3.refs_1_.refs_2_, ...), custom_call_target="tpu_custom_call", output_to_operand_aliasing={{0}: (14, {})} | custom-call | flops 3221225472 | bytes 1048576 | tf_op jit(solution)/shard_map/pair_update/pallas_call | solution.py:334
  88.5 3.8 %collective-permute-start.23 = (bf16[16,64,128]{2,1,0:T(8,128)(2,1)S(1)}, bf16[16,64,128]{2,1,0:T(8,128)(2,1)S(1)}, u32[]{:S(2)}, u32[]{:S(2)}) collective-permute-start(bf16[16,64,128]{2,1,0:T(8,128)(2,1)S(1)} %pad_maximum_fusion.1.refs_13_.grads_ref.refs_0_), channel_id=1, source_target_pairs={{0,12},{1,13},{4,0},{5,1},{8,4},{9,5},{12,8},{13,9},{2,14},{3,15},... | collective-permute-start | bytes 786440 | tf_op jit(solution)/shard_map/ppermute | solution.py:532
  93.6 2.2 %projection_grad.1 = f32[64,256]{1,0:T(8,128)S(1)} custom-call(s32[2]{0:T(128)S(1)} %pad_add_fusion.3.place_ref, bf16[64,128,256]{2,1,0:T(8,128)(2,1)} %features_ref.11, f32[1,256]{1,0:T(1,128)S(1)} %bitcast.66, f32[1,256]{1,0:T(1,128)S(1)} %bitcast.72, bf16[16,64,128]{2,1,0:T(8,128)(2,1)S(1)} %pad_maximum_fusion.1.refs_13_.grads_ref.refs_0_), custom_call_target="tpu_custom_call" | custom-call | tf_op jit(solution)/shard_map/projection_grad/pallas_call | solution.py:377
  95.8 1.6 %copy-done.6 = bf16[64,128,128]{2,1,0:T(8,128)(2,1)S(1)} copy-done((bf16[64,128,128]{2,1,0:T(8,128)(2,1)S(1)}, bf16[64,128,128]{2,1,0:T(8,128)(2,1)}, u32[]{:S(2)}) %copy-start.6) | copy-done | bytes 2097176
  98.0 4.0 %pair_update.5 = (bf16[64,128,128]{2,1,0:T(8,128)(2,1)}, f32[1024,128]{1,0:T(8,128)S(1)}) custom-call(bf16[16,4096]{1,0:T(8,128)(2,1)S(1)} %add_up.7.refs_0_, bf16[16,4096]{1,0:T(8,128)(2,1)S(1)} %collective-permute-done.2.refs_0_.refs_1_, bf16[16,4096]{1,0:T(8,128)(2,1)S(1)} %collective-permute-done.3.refs_1_.refs_2_, ...), custom_call_target="tpu_custom_call", output_to_operand_aliasing={{0}: (14, {})} | custom-call | flops 3221225472 | bytes 1048576 | tf_op jit(solution)/shard_map/pair_update/pallas_call | solution.py:334
  102.3 2.2 %collective-permute-done.21.refs_1_.refs_0_ = bf16[16,64,128]{2,1,0:T(8,128)(2,1)S(1)} collective-permute-done((bf16[16,64,128]{2,1,0:T(8,128)(2,1)S(1)}, bf16[16,64,128]{2,1,0:T(8,128)(2,1)S(1)}, u32[]{:S(2)}, u32[]{:S(2)}) %collective-permute-start.21) | collective-permute-done | bytes 262176 | tf_op jit(solution)/shard_map/ppermute | solution.py:532
  105.4 7.4 %all-to-all-start = ((bf16[128,16,128]{2,1,0:T(8,128)(2,1)}), bf16[128,16,128]{2,1,0:T(8,128)(2,1)S(1)}, u32[]{:S(2)}, u32[]{:S(2)}) async-start(bf16[128,16,128]{2,1,0:T(8,128)(2,1)} %get-tuple-element.32), calls=%async_computation | async-start | bytes 1048576 | tf_op jit(solution)/shard_map/all_to_all | solution.py:690
  112.8 6.7 %norm_grad.2 = (bf16[64,128,256]{2,1,0:T(8,128)(2,1)}, f32[8,128]{1,0:T(8,128)S(1)}) custom-call(s32[1]{0:T(128)} %bitcast.25.first_ref, bf16[64,128,256]{2,1,0:T(8,128)(2,1)} %features_ref.11, f32[1,256]{1,0:T(1,128)S(1)} %bitcast.67, bf16[64,256]{1,0:T(8,128)(2,1)S(1)} %bitcast.58, bf16[16,64,128]{2,1,0:T(8,128)(2,1)S(1)} %pad_maximum_fusion.1.refs_13_.grads_ref.refs_0_, ...), custom_call_target="tpu_custom_call" | custom-call | flops 268435456 | bytes 4194304 | tf_op jit(solution)/shard_map/norm_grad/pallas_call | solution.py:439
  119.5 7.3 %all-to-all-done.terms_ref = bf16[128,16,128]{2,1,0:T(8,128)(2,1)S(1)} async-done(((bf16[128,16,128]{2,1,0:T(8,128)(2,1)}), bf16[128,16,128]{2,1,0:T(8,128)(2,1)S(1)}, u32[]{:S(2)}, u32[]{:S(2)}) %all-to-all-start) | async-done | bytes 524320 | tf_op jit(solution)/shard_map/all_to_all | solution.py:690
  127.8 3.8 %all-to-all-start.1 = ((bf16[128,16,128]{2,1,0:T(8,128)(2,1)}), bf16[128,16,128]{2,1,0:T(8,128)(2,1)S(1)}, u32[]{:S(2)}, u32[]{:S(2)}) async-start(bf16[128,16,128]{2,1,0:T(8,128)(2,1)} %get-tuple-element.38), calls=%async_computation.1 | async-start | bytes 1048576 | tf_op jit(solution)/shard_map/all_to_all | solution.py:702
  131.6 6.7 %norm_grad.3 = (bf16[64,128,256]{2,1,0:T(8,128)(2,1)}, f32[8,128]{1,0:T(8,128)}) custom-call(s32[1]{0:T(128)} %bitcast.22.first_ref, bf16[64,128,256]{2,1,0:T(8,128)(2,1)} %features_ref.11, f32[1,256]{1,0:T(1,128)S(1)} %bitcast.68, bf16[64,256]{1,0:T(8,128)(2,1)S(1)} %bitcast.59, ...), custom_call_target="tpu_custom_call", output_to_operand_aliasing={{0}: (7, {})} | custom-call | flops 268435456 | bytes 4194304 | tf_op jit(solution)/shard_map/norm_grad/pallas_call | solution.py:439
  138.8 6.9 %all-to-all-done.1 = bf16[128,16,128]{2,1,0:T(8,128)(2,1)S(1)} async-done(((bf16[128,16,128]{2,1,0:T(8,128)(2,1)}), bf16[128,16,128]{2,1,0:T(8,128)(2,1)S(1)}, u32[]{:S(2)}, u32[]{:S(2)}) %all-to-all-start.1) | async-done | bytes 524320 | tf_op jit(solution)/shard_map/all_to_all | solution.py:702
  (97 shorter events, 22.2 us)
Async XLA Ops:
  8.1 5.8 %collective-permute-start.1 = (bf16[64,32,64]{2,1,0:T(8,128)(2,1)S(1)}, bf16[64,32,64]{2,1,0:T(8,128)(2,1)S(1)}, u32[]{:S(2)}, u32[]{:S(2)}) collective-permute-start(bf16[64,32,64]{2,1,0:T(8,128)(2,1)S(1)} %project.5), channel_id=1, source_target_pairs={{0,1},{1,0},{4,5},{5,4},{8,9},{9,8},{12,13},{13,12},{2,3},{3,2},{6... | collective-permute-start | bytes 786440 | tf_op jit(solution)/shard_map/ppermute | solution.py:532
  9.6 6.0 %collective-permute-start = (bf16[16,4096]{1,0:T(8,128)(2,1)S(1)}, bf16[16,4096]{1,0:T(8,128)(2,1)S(1)}, u32[]{:S(2)}, u32[]{:S(2)}) collective-permute-start(bf16[16,4096]{1,0:T(8,128)(2,1)S(1)} %bitcast.83), channel_id=1, source_target_pairs={{0,0},{1,1},{4,32},{5,33},{8,64},{9,65},{12,96},{13,97},{2,16},{3,... | collective-permute-start | bytes 393224 | tf_op jit(solution)/shard_map/ppermute | solution.py:532
  15.7 18.3 %collective-permute-start.4 = (bf16[16,4096]{1,0:T(8,128)(2,1)S(1)}, bf16[16,4096]{1,0:T(8,128)(2,1)S(1)}, u32[]{:S(2)}, u32[]{:S(2)}) collective-permute-start(bf16[16,4096]{1,0:T(8,128)(2,1)S(1)} %add_up.7.refs_0_), channel_id=1, source_target_pairs={{0,32},{1,33},{4,36},{5,37},{8,40},{9,41},{12,44},{13,45},{2,34},{... | collective-permute-start | bytes 393224 | tf_op jit(solution)/shard_map/ppermute | solution.py:532
  19.4 14.6 %collective-permute-start.3 = (bf16[16,4096]{1,0:T(8,128)(2,1)S(1)}, bf16[16,4096]{1,0:T(8,128)(2,1)S(1)}, u32[]{:S(2)}, u32[]{:S(2)}) collective-permute-start(bf16[16,4096]{1,0:T(8,128)(2,1)S(1)} %add_up.7.refs_0_), channel_id=1, source_target_pairs={{0,64},{1,65},{4,68},{5,69},{8,72},{9,73},{12,76},{13,77},{2,66},{... | collective-permute-start | bytes 393224 | tf_op jit(solution)/shard_map/ppermute | solution.py:532
  28.0 6.0 %collective-permute-start.2 = (bf16[16,4096]{1,0:T(8,128)(2,1)S(1)}, bf16[16,4096]{1,0:T(8,128)(2,1)S(1)}, u32[]{:S(2)}, u32[]{:S(2)}) collective-permute-start(bf16[16,4096]{1,0:T(8,128)(2,1)S(1)} %add_up.7.refs_0_), channel_id=1, source_target_pairs={{0,96},{1,97},{4,100},{5,101},{8,104},{9,105},{12,108},{13,109},{2... | collective-permute-start | bytes 393224 | tf_op jit(solution)/shard_map/ppermute | solution.py:532
  42.1 5.1 %collective-permute-start.8 = (bf16[16,4096]{1,0:T(8,128)(2,1)S(1)}, bf16[16,4096]{1,0:T(8,128)(2,1)S(1)}, u32[]{:S(2)}, u32[]{:S(2)}) collective-permute-start(bf16[16,4096]{1,0:T(8,128)(2,1)S(1)} %collective-permute-done.4.refs_2_.refs_3_), channel_id=1, source_target_pairs={{0,1},{1,0},{4,5},{5,4},{8,9},{9,8},{12,13},{13,12},{2,3},{3,2},{6... | collective-permute-start | bytes 393224 | tf_op jit(solution)/shard_map/ppermute | solution.py:532
  42.6 4.7 %collective-permute-start.7 = (bf16[16,4096]{1,0:T(8,128)(2,1)S(1)}, bf16[16,4096]{1,0:T(8,128)(2,1)S(1)}, u32[]{:S(2)}, u32[]{:S(2)}) collective-permute-start(bf16[16,4096]{1,0:T(8,128)(2,1)S(1)} %collective-permute-done.3.refs_1_.refs_2_), channel_id=1, source_target_pairs={{0,1},{1,0},{4,5},{5,4},{8,9},{9,8},{12,13},{13,12},{2,3},{3,2},{6... | collective-permute-start | bytes 393224 | tf_op jit(solution)/shard_map/ppermute | solution.py:532
  42.7 4.6 %collective-permute-start.6 = (bf16[16,4096]{1,0:T(8,128)(2,1)S(1)}, bf16[16,4096]{1,0:T(8,128)(2,1)S(1)}, u32[]{:S(2)}, u32[]{:S(2)}) collective-permute-start(bf16[16,4096]{1,0:T(8,128)(2,1)S(1)} %collective-permute-done.2.refs_0_.refs_1_), channel_id=1, source_target_pairs={{0,1},{1,0},{4,5},{5,4},{8,9},{9,8},{12,13},{13,12},{2,3},{3,2},{6... | collective-permute-start | bytes 393224 | tf_op jit(solution)/shard_map/ppermute | solution.py:532
  43.7 15.9 %collective-permute-start.15 = (bf16[16,4096]{1,0:T(8,128)(2,1)S(1)}, bf16[16,4096]{1,0:T(8,128)(2,1)S(1)}, u32[]{:S(2)}, u32[]{:S(2)}) collective-permute-start(bf16[16,4096]{1,0:T(8,128)(2,1)S(1)} %get-tuple-element.41), channel_id=1, source_target_pairs={{0,96},{1,97},{4,100},{5,101},{8,104},{9,105},{12,108},{13,109},{2... | collective-permute-start | bytes 393224 | tf_op jit(solution)/shard_map/ppermute | solution.py:532
  45.7 14.6 %collective-permute-start.14 = (bf16[16,4096]{1,0:T(8,128)(2,1)S(1)}, bf16[16,4096]{1,0:T(8,128)(2,1)S(1)}, u32[]{:S(2)}, u32[]{:S(2)}) collective-permute-start(bf16[16,4096]{1,0:T(8,128)(2,1)S(1)} %get-tuple-element.42), channel_id=1, source_target_pairs={{0,64},{1,65},{4,68},{5,69},{8,72},{9,73},{12,76},{13,77},{2,66},{... | collective-permute-start | bytes 393224 | tf_op jit(solution)/shard_map/ppermute | solution.py:532
  47.2 13.0 %collective-permute-start.13 = (bf16[16,4096]{1,0:T(8,128)(2,1)S(1)}, bf16[16,4096]{1,0:T(8,128)(2,1)S(1)}, u32[]{:S(2)}, u32[]{:S(2)}) collective-permute-start(bf16[16,4096]{1,0:T(8,128)(2,1)S(1)} %get-tuple-element.43), channel_id=1, source_target_pairs={{0,32},{1,33},{4,36},{5,37},{8,40},{9,41},{12,44},{13,45},{2,34},{... | collective-permute-start | bytes 393224 | tf_op jit(solution)/shard_map/ppermute | solution.py:532
  58.5 9.7 %collective-permute-start.12 = (bf16[32,2048]{1,0:T(8,128)(2,1)S(1)}, bf16[32,2048]{1,0:T(8,128)(2,1)S(1)}, u32[]{:S(2)}, u32[]{:S(2)}) collective-permute-start(bf16[32,2048]{1,0:T(8,128)(2,1)S(1)} %get-tuple-element.45), channel_id=1, source_target_pairs={{0,12},{1,13},{4,0},{5,1},{8,4},{9,5},{12,8},{13,9},{2,14},{3,15},... | collective-permute-start | bytes 393224 | tf_op jit(solution)/shard_map/ppermute | solution.py:532
  58.9 9.3 %collective-permute-start.11 = (bf16[32,2048]{1,0:T(8,128)(2,1)S(1)}, bf16[32,2048]{1,0:T(8,128)(2,1)S(1)}, u32[]{:S(2)}, u32[]{:S(2)}) collective-permute-start(bf16[32,2048]{1,0:T(8,128)(2,1)S(1)} %get-tuple-element.46), channel_id=1, source_target_pairs={{0,8},{1,9},{4,12},{5,13},{8,0},{9,1},{12,4},{13,5},{2,10},{3,11},... | collective-permute-start | bytes 393224 | tf_op jit(solution)/shard_map/ppermute | solution.py:532
  59.6 8.6 %collective-permute-start.10 = (bf16[32,2048]{1,0:T(8,128)(2,1)S(1)}, bf16[32,2048]{1,0:T(8,128)(2,1)S(1)}, u32[]{:S(2)}, u32[]{:S(2)}) collective-permute-start(bf16[32,2048]{1,0:T(8,128)(2,1)S(1)} %get-tuple-element.47), channel_id=1, source_target_pairs={{0,4},{1,5},{4,8},{5,9},{8,12},{9,13},{12,0},{13,1},{2,6},{3,7},{6... | collective-permute-start | bytes 393224 | tf_op jit(solution)/shard_map/ppermute | solution.py:532
  60.3 8.0 %collective-permute-start.16 = (bf16[16,4096]{1,0:T(8,128)(2,1)S(1)}, bf16[16,4096]{1,0:T(8,128)(2,1)S(1)}, u32[]{:S(2)}, u32[]{:S(2)}) collective-permute-start(bf16[16,4096]{1,0:T(8,128)(2,1)S(1)} %add_up.9), channel_id=1, source_target_pairs={{0,0},{1,1},{4,32},{5,33},{8,64},{9,65},{12,96},{13,97},{2,16},{3,... | collective-permute-start | bytes 393224 | tf_op jit(solution)/shard_map/ppermute | solution.py:532
  68.4 19.1 %collective-permute-start.19 = (bf16[16,2048]{1,0:T(8,128)(2,1)S(1)}, bf16[16,2048]{1,0:T(8,128)(2,1)S(1)}, u32[]{:S(2)}, u32[]{:S(2)}) collective-permute-start(bf16[16,2048]{1,0:T(8,128)(2,1)S(1)} %get-tuple-element.52), channel_id=1, source_target_pairs={{0,3},{1,2},{4,7},{5,6},{8,11},{9,10},{12,15},{13,14},{2,1},{3,0},... | collective-permute-start | bytes 196616 | tf_op jit(solution)/shard_map/ppermute | solution.py:532
  82.0 5.5 %collective-permute-start.18 = (bf16[16,2048]{1,0:T(8,128)(2,1)S(1)}, bf16[16,2048]{1,0:T(8,128)(2,1)S(1)}, u32[]{:S(2)}, u32[]{:S(2)}) collective-permute-start(bf16[16,2048]{1,0:T(8,128)(2,1)S(1)} %get-tuple-element.52), channel_id=1, source_target_pairs={{0,1},{1,0},{4,5},{5,4},{8,9},{9,8},{12,13},{13,12},{2,3},{3,2},{6... | collective-permute-start | bytes 196616 | tf_op jit(solution)/shard_map/ppermute | solution.py:532
  82.0 5.5 %collective-permute-start.17 = (bf16[16,2048]{1,0:T(8,128)(2,1)S(1)}, bf16[16,2048]{1,0:T(8,128)(2,1)S(1)}, u32[]{:S(2)}, u32[]{:S(2)}) collective-permute-start(bf16[16,2048]{1,0:T(8,128)(2,1)S(1)} %get-tuple-element.51.refs_0_), channel_id=1, source_target_pairs={{0,2},{1,3},{4,6},{5,7},{8,10},{9,11},{12,14},{13,15},{2,0},{3,1},... | collective-permute-start | bytes 196616 | tf_op jit(solution)/shard_map/ppermute | solution.py:532
  82.2 6.0 %collective-permute-start.20 = (bf16[16,4096]{1,0:T(8,128)(2,1)S(1)}, bf16[16,4096]{1,0:T(8,128)(2,1)S(1)}, u32[]{:S(2)}, u32[]{:S(2)}) collective-permute-start(bf16[16,4096]{1,0:T(8,128)(2,1)S(1)} %collective-permute-done.16.refs_5_.refs_0_), channel_id=1, source_target_pairs={{0,2},{1,3},{4,6},{5,7},{8,10},{9,11},{12,14},{13,15},{2,0},{3,1},... | collective-permute-start | bytes 393224 | tf_op jit(solution)/shard_map/ppermute | solution.py:532
  88.5 13.8 %collective-permute-start.23 = (bf16[16,64,128]{2,1,0:T(8,128)(2,1)S(1)}, bf16[16,64,128]{2,1,0:T(8,128)(2,1)S(1)}, u32[]{:S(2)}, u32[]{:S(2)}) collective-permute-start(bf16[16,64,128]{2,1,0:T(8,128)(2,1)S(1)} %pad_maximum_fusion.1.refs_13_.grads_ref.refs_0_), channel_id=1, source_target_pairs={{0,12},{1,13},{4,0},{5,1},{8,4},{9,5},{12,8},{13,9},{2,14},{3,15},... | collective-permute-start | bytes 786440 | tf_op jit(solution)/shard_map/ppermute | solution.py:532
  92.3 10.0 %collective-permute-start.22 = (bf16[16,64,128]{2,1,0:T(8,128)(2,1)S(1)}, bf16[16,64,128]{2,1,0:T(8,128)(2,1)S(1)}, u32[]{:S(2)}, u32[]{:S(2)}) collective-permute-start(bf16[16,64,128]{2,1,0:T(8,128)(2,1)S(1)} %pad_maximum_fusion.1.refs_13_.grads_ref.refs_0_), channel_id=1, source_target_pairs={{0,4},{1,5},{4,8},{5,9},{8,12},{9,13},{12,0},{13,1},{2,6},{3,7},{6... | collective-permute-start | bytes 786440 | tf_op jit(solution)/shard_map/ppermute | solution.py:532
  92.3 12.2 %collective-permute-start.21 = (bf16[16,64,128]{2,1,0:T(8,128)(2,1)S(1)}, bf16[16,64,128]{2,1,0:T(8,128)(2,1)S(1)}, u32[]{:S(2)}, u32[]{:S(2)}) collective-permute-start(bf16[16,64,128]{2,1,0:T(8,128)(2,1)S(1)} %pad_maximum_fusion.1.refs_13_.grads_ref.refs_0_), channel_id=1, source_target_pairs={{0,8},{1,9},{4,12},{5,13},{8,0},{9,1},{12,4},{13,5},{2,10},{3,11},... | collective-permute-start | bytes 786440 | tf_op jit(solution)/shard_map/ppermute | solution.py:532
  105.4 21.4 %all-to-all-start = ((bf16[128,16,128]{2,1,0:T(8,128)(2,1)}), bf16[128,16,128]{2,1,0:T(8,128)(2,1)S(1)}, u32[]{:S(2)}, u32[]{:S(2)}) async-start(bf16[128,16,128]{2,1,0:T(8,128)(2,1)} %get-tuple-element.32), calls=%async_computation | async-start | bytes 1048576 | tf_op jit(solution)/shard_map/all_to_all | solution.py:690
  127.8 18.0 %all-to-all-start.1 = ((bf16[128,16,128]{2,1,0:T(8,128)(2,1)}), bf16[128,16,128]{2,1,0:T(8,128)(2,1)S(1)}, u32[]{:S(2)}, u32[]{:S(2)}) async-start(bf16[128,16,128]{2,1,0:T(8,128)(2,1)} %get-tuple-element.38), calls=%async_computation.1 | async-start | bytes 1048576 | tf_op jit(solution)/shard_map/all_to_all | solution.py:702
  (12 other events, 44.0 us)

commit v3 on v2

--- a/solution.py
+++ b/solution.py
@@ -11,10 +11,10 @@
 AXES = ("ia", "ja", "sa")
 RING = 4
 SWAP_Y = (0, 2, 1, 3)
-ROWS_AT_ONCE = 8
+ROWS_AT_ONCE = 16
 BF16 = jnp.bfloat16
 F32 = jnp.float32
-VMEM_LIMIT = 12 * 1024 * 1024
+VMEM_LIMIT = 20 * 1024 * 1024
 
 
 def dot(a, b, contract):
@@ -76,7 +76,7 @@
 def project(first, count, part, residues, features, gain, offset, weight, after=()):
     total, _, channels = features.shape
     width = weight.shape[0]
-    seqs = 1024 // residues
+    seqs = min(2048 // residues, 16)
     steps = total // seqs
 
     def place(n, place_ref):
@@ -418,8 +418,8 @@
 def norm_grad(first, pieces, features, gain, weight, before=None, after=()):
     _, residues, channels = features.shape
     quarter, both_widths, _ = pieces[0].shape
-    seqs = 8
-    steps = quarter // seqs
+    seqs = quarter
+    steps = 1
 
     def place(n, first_ref):
         return (lax.rem(n // steps + first_ref[0], RING) * steps + lax.rem(n, steps), 0, 0)
@@ -583,7 +583,7 @@
     weight_rows = projection_weight.T
 
     right_piece = project(
-        x * 2,
+        x,
         quarter,
         x * 0,
         residues,
@@ -661,13 +661,13 @@
             after,
         )
 
-    pair = pair_part(0, 4, None, (left_partial,))
+    pair = pair_part(0, blocks // 2, None, (left_partial,))
     left_sum = add_up([left_partial[0], *left_came], after=(pair[1], right_sum))
 
     left_own, left_other = left_sum[:quarter], left_sum[quarter:]
     own_beside, right_beside = swap_low_y(left_own), swap_low_y(right_sum)
     other_here, other_beside = swap_cores(left_other), swap_both(left_other)
-    pair = pair_part(4, 2, pair, (left_sum,))
+    pair = pair_part(blocks // 2, blocks // 4, pair, (left_sum,))
     left_own = add_up([left_own, own_beside], inv_seqs, after=(pair[1],))
     left_came = add_up([other_here, other_beside], inv_seqs, after=(pair[1],))
     right_grad = add_up([right_sum, right_beside], inv_seqs, after=(pair[1],))
@@ -680,7 +680,7 @@
     grads = jnp.concatenate([left_grad, right_grad.reshape(quarter, width, residues)], axis=1)
     grad_pieces = [grads] + [shift_x(grads, -t) for t in range(1, RING)]
 
-    pair_update_result, weight_partial = pair_part(6, blocks - 6, pair, (grads,))
+    pair_update_result, weight_partial = pair_part(blocks - blocks // 4, blocks // 4, pair, (grads,))
     projection_part = projection_grad_part(x, low_y, features, gain_row, offset_row, grads)
     devices = 128
     terms, token = gather_terms(

time: 148 us -> 154 us (1.041)
  Pallas kernels: 64.1 us -> 69.3 us
    pallas_call x1, Pallas kernels: 11.2 us -> 18.5 us  [left_grad_part(): pl.pallas_call(left_grad_kernel, grid_spec=pltpu.PrefetchScalarGridSpec(n...]
  transfers between devices with their start and end apart: 26 -> 26, of which waited for: 5 -> 6; matrix products, arithmetic and copies ran while one was open for 2% -> 2% of each run, Pallas kernels for 34% -> 36%
where the time goes in v3:
time: 154 us
  Pallas kernels  69.3 us (45%)
  starting transfers between devices  53.9 us (35%)
  waiting for transfers between devices  18.5 us (12%)
  local copies, waits for them, and re-layouts  10.1 us (7%)
    ppermute x24, starting transfers between devices, torus_permute(): return lax.ppermute(value, AXES, pairs)  42.2 us
    pallas_call x1, Pallas kernels, left_grad_part(): pl.pallas_call(left_grad_kernel, grid_spec=pltpu.PrefetchScalarGridSpec(n...  18.5 us
    pallas_call x3, Pallas kernels, pair_and_weight_grad(): pl.pallas_call(functools.partial(pair_kernel, fresh), grid=(count,), in_s...  14.3 us
    pallas_call x2, Pallas kernels, norm_grad(): pl.pallas_call(functools.partial(norm_grad_kernel, len(pieces)), grid_spe...  13.3 us
    pallas_call x3, Pallas kernels, project(): pl.pallas_call(project_kernel, grid_spec=pltpu.PrefetchScalarGridSpec(num...  9.83 us
    pallas_call x2, Pallas kernels, right_grad_part(): pl.pallas_call(functools.partial(right_grad_kernel, fresh), grid=(count,)...  9.09 us
    all_to_all x1, starting transfers between devices, body(): came = lax.all_to_all(terms, AXES, 0, 0, tiled=True)  7.88 us
    all_to_all x1, waiting for transfers between devices, body(): came = lax.all_to_all(terms, AXES, 0, 0, tiled=True)  7.37 us
  transfers between devices with their start and end apart: 26, of which 6 were waited for; matrix products, arithmetic and copies ran while one was open for 2% of the time, Pallas kernels for 36%

profile of v3, /device:TPU:1, one launch (start us, length us, event | category | flops | bytes accessed | tf_op | source)
XLA Modules:
  0.0 154.0 jit_solution(8182822807312618894)
XLA Ops:
  1.6 3.0 %project.3.refs_0_ = bf16[16,32,128]{2,1,0:T(8,128)(2,1)S(1)} custom-call(s32[2]{0:T(128)S(1)} %pad_add_fusion.place_ref, bf16[64,128,256]{2,1,0:T(8,128)(2,1)} %features_ref.11, f32[1,256]{1,0:T(1,128)} %bitcast.63, f32[1,256]{1,0:T(1,128)} %bitcast.69, bf16[32,256]{1,0:T(8,128)(2,1)S(1)} %get-tuple-element.54.weight_ref), custom_call_target="tpu_custom_call" | custom-call | flops 67108864 | bytes 1179648 | tf_op jit(solution)/shard_map/project/pallas_call | solution.py:85
  4.6 3.4 %project.5 = bf16[64,32,64]{2,1,0:T(8,128)(2,1)S(1)} custom-call(s32[2]{0:T(128)S(1)} %get-tuple-element.56.place_ref, bf16[64,128,256]{2,1,0:T(8,128)(2,1)S(1)} %copy-done, f32[1,256]{1,0:T(1,128)S(1)} %bitcast.64, f32[1,256]{1,0:T(1,128)S(1)} %bitcast.70, bf16[32,256]{1,0:T(8,128)(2,1)S(1)} %get-tuple-element.53.weight_ref, ...), custom_call_target="tpu_custom_call" | custom-call | flops 134217728 | bytes 2359296 | tf_op jit(solution)/shard_map/project/pallas_call | solution.py:85
  10.4 3.4 %project.4 = bf16[64,32,64]{2,1,0:T(8,128)(2,1)S(1)} custom-call(s32[2]{0:T(128)S(1)} %get-tuple-element.55.place_ref, bf16[64,128,256]{2,1,0:T(8,128)(2,1)S(1)} %copy-done, f32[1,256]{1,0:T(1,128)S(1)} %bitcast.65, f32[1,256]{1,0:T(1,128)S(1)} %bitcast.71, bf16[32,256]{1,0:T(8,128)(2,1)S(1)} %get-tuple-element.53.weight_ref, ...), custom_call_target="tpu_custom_call" | custom-call | flops 134217728 | bytes 2359296 | tf_op jit(solution)/shard_map/project/pallas_call | solution.py:85
  15.6 3.8 %collective-permute-start.4 = (bf16[16,4096]{1,0:T(8,128)(2,1)S(1)}, bf16[16,4096]{1,0:T(8,128)(2,1)S(1)}, u32[]{:S(2)}, u32[]{:S(2)}) collective-permute-start(bf16[16,4096]{1,0:T(8,128)(2,1)S(1)} %add_up.7.refs_0_), channel_id=1, source_target_pairs={{0,32},{1,33},{4,36},{5,37},{8,40},{9,41},{12,44},{13,45},{2,34},{... | collective-permute-start | bytes 393224 | tf_op jit(solution)/shard_map/ppermute | solution.py:532
  19.4 8.6 %collective-permute-start.3 = (bf16[16,4096]{1,0:T(8,128)(2,1)S(1)}, bf16[16,4096]{1,0:T(8,128)(2,1)S(1)}, u32[]{:S(2)}, u32[]{:S(2)}) collective-permute-start(bf16[16,4096]{1,0:T(8,128)(2,1)S(1)} %add_up.7.refs_0_), channel_id=1, source_target_pairs={{0,64},{1,65},{4,68},{5,69},{8,72},{9,73},{12,76},{13,77},{2,66},{... | collective-permute-start | bytes 393224 | tf_op jit(solution)/shard_map/ppermute | solution.py:532
  28.0 1.6 %copy-done.4 = bf16[64,128,128]{2,1,0:T(8,128)(2,1)S(1)} copy-done((bf16[64,128,128]{2,1,0:T(8,128)(2,1)S(1)}, bf16[64,128,128]{2,1,0:T(8,128)(2,1)}, u32[]{:S(2)}) %copy-start.4) | copy-done | bytes 2097176
  29.6 3.9 %right_grad.2 = (bf16[8,128]{1,0:T(8,128)(2,1)}, f32[128,4096]{1,0:T(8,128)S(1)}, f32[8,128]{1,0:T(8,128)S(1)}) custom-call(bf16[64,128,128]{2,1,0:T(8,128)(2,1)S(1)} %copy-done.4, bf16[1024,128]{1,0:T(8,128)(2,1)S(1)} %bitcast.52, bf16[2048,128]{1,0:T(8,128)(2,1)S(1)} %bitcast.46, ...), custom_call_target="tpu_custom_call" | custom-call | flops 2147483648 | bytes 1048576 | tf_op jit(solution)/shard_map/right_grad/pallas_call | solution.py:161
  33.8 5.2 %right_grad.3 = (bf16[128,4096]{1,0:T(8,128)(2,1)S(1)}, f32[128,4096]{1,0:T(8,128)}, f32[8,128]{1,0:T(8,128)S(1)}) custom-call(bf16[64,128,128]{2,1,0:T(8,128)(2,1)S(1)} %copy-done.4, bf16[1024,128]{1,0:T(8,128)(2,1)S(1)} %bitcast.53, bf16[2048,128]{1,0:T(8,128)(2,1)S(1)} %bitcast.47, f32[128,4096]{1,0:T(8,128)S(1)} %get-tuple-element.22.total_in_ref, ...), custom_call_target="tpu_custom_call" | custom-call | flops 2147483648 | bytes 1048576 | tf_op jit(solution)/shard_map/right_grad/pallas_call | solution.py:161
  43.2 1.9 %collective-permute-start.15 = (bf16[16,4096]{1,0:T(8,128)(2,1)S(1)}, bf16[16,4096]{1,0:T(8,128)(2,1)S(1)}, u32[]{:S(2)}, u32[]{:S(2)}) collective-permute-start(bf16[16,4096]{1,0:T(8,128)(2,1)S(1)} %get-tuple-element.41), channel_id=1, source_target_pairs={{0,96},{1,97},{4,100},{5,101},{8,104},{9,105},{12,108},{13,109},{2... | collective-permute-start | bytes 393224 | tf_op jit(solution)/shard_map/ppermute | solution.py:532
  46.4 18.5 %left_grad.1.refs_13_.refs_4_ = bf16[4,32,2048]{2,1,0:T(8,128)(2,1)S(1)} custom-call(s32[1]{0:T(128)} %bitcast.15.turn_ref, bf16[16,4096]{1,0:T(8,128)(2,1)S(1)} %add_up.7.refs_0_, bf16[16,4096]{1,0:T(8,128)(2,1)S(1)} %collective-permute-done.2.refs_0_.refs_1_, bf16[16,4096]{1,0:T(8,128)(2,1)S(1)} %collective-permute-done.3.refs_1_.refs_2_, ...), custom_call_target="tpu_custom_call" | custom-call | flops 8589934592 | bytes 2097152 | tf_op jit(solution)/shard_map/left_grad/pallas_call | solution.py:225
  67.2 6.8 %pair_update.3 = (bf16[64,128,128]{2,1,0:T(8,128)(2,1)}, f32[1024,128]{1,0:T(8,128)S(1)}) custom-call(bf16[16,4096]{1,0:T(8,128)(2,1)S(1)} %add_up.7.refs_0_, bf16[16,4096]{1,0:T(8,128)(2,1)S(1)} %collective-permute-done.2.refs_0_.refs_1_, bf16[16,4096]{1,0:T(8,128)(2,1)S(1)} %collective-permute-done.3.refs_1_.refs_2_, ...), custom_call_target="tpu_custom_call" | custom-call | flops 6442450944 | bytes 2097152 | tf_op jit(solution)/shard_map/pair_update/pallas_call | solution.py:334
  75.0 13.6 %collective-permute-start.19 = (bf16[16,2048]{1,0:T(8,128)(2,1)S(1)}, bf16[16,2048]{1,0:T(8,128)(2,1)S(1)}, u32[]{:S(2)}, u32[]{:S(2)}) collective-permute-start(bf16[16,2048]{1,0:T(8,128)(2,1)S(1)} %get-tuple-element.52), channel_id=1, source_target_pairs={{0,3},{1,2},{4,7},{5,6},{8,11},{9,10},{12,15},{13,14},{2,1},{3,0},... | collective-permute-start | bytes 196616 | tf_op jit(solution)/shard_map/ppermute | solution.py:532
  90.1 3.7 %pair_update.4 = (bf16[64,128,128]{2,1,0:T(8,128)(2,1)}, f32[1024,128]{1,0:T(8,128)S(1)}) custom-call(bf16[16,4096]{1,0:T(8,128)(2,1)S(1)} %add_up.7.refs_0_, bf16[16,4096]{1,0:T(8,128)(2,1)S(1)} %collective-permute-done.2.refs_0_.refs_1_, bf16[16,4096]{1,0:T(8,128)(2,1)S(1)} %collective-permute-done.3.refs_1_.refs_2_, ...), custom_call_target="tpu_custom_call", output_to_operand_aliasing={{0}: (14, {})} | custom-call | flops 3221225472 | bytes 1048576 | tf_op jit(solution)/shard_map/pair_update/pallas_call | solution.py:334
  94.9 3.4 %collective-permute-start.23 = (bf16[16,64,128]{2,1,0:T(8,128)(2,1)S(1)}, bf16[16,64,128]{2,1,0:T(8,128)(2,1)S(1)}, u32[]{:S(2)}, u32[]{:S(2)}) collective-permute-start(bf16[16,64,128]{2,1,0:T(8,128)(2,1)S(1)} %pad_maximum_fusion.1.refs_13_.grads_ref.refs_0_), channel_id=1, source_target_pairs={{0,12},{1,13},{4,0},{5,1},{8,4},{9,5},{12,8},{13,9},{2,14},{3,15},... | collective-permute-start | bytes 786440 | tf_op jit(solution)/shard_map/ppermute | solution.py:532
  99.6 2.2 %projection_grad.1 = f32[64,256]{1,0:T(8,128)S(1)} custom-call(s32[2]{0:T(128)S(1)} %pad_add_fusion.3.place_ref, bf16[64,128,256]{2,1,0:T(8,128)(2,1)} %features_ref.11, f32[1,256]{1,0:T(1,128)S(1)} %bitcast.66, f32[1,256]{1,0:T(1,128)S(1)} %bitcast.72, bf16[16,64,128]{2,1,0:T(8,128)(2,1)S(1)} %pad_maximum_fusion.1.refs_13_.grads_ref.refs_0_), custom_call_target="tpu_custom_call" | custom-call | tf_op jit(solution)/shard_map/projection_grad/pallas_call | solution.py:377
  101.8 1.6 %copy-done.6 = bf16[64,128,128]{2,1,0:T(8,128)(2,1)S(1)} copy-done((bf16[64,128,128]{2,1,0:T(8,128)(2,1)S(1)}, bf16[64,128,128]{2,1,0:T(8,128)(2,1)}, u32[]{:S(2)}) %copy-start.6) | copy-done | bytes 2097176
  104.0 3.7 %pair_update.5 = (bf16[64,128,128]{2,1,0:T(8,128)(2,1)}, f32[1024,128]{1,0:T(8,128)S(1)}) custom-call(bf16[16,4096]{1,0:T(8,128)(2,1)S(1)} %add_up.7.refs_0_, bf16[16,4096]{1,0:T(8,128)(2,1)S(1)} %collective-permute-done.2.refs_0_.refs_1_, bf16[16,4096]{1,0:T(8,128)(2,1)S(1)} %collective-permute-done.3.refs_1_.refs_2_, ...), custom_call_target="tpu_custom_call", output_to_operand_aliasing={{0}: (14, {})} | custom-call | flops 3221225472 | bytes 1048576 | tf_op jit(solution)/shard_map/pair_update/pallas_call | solution.py:334
  107.7 2.5 %collective-permute-done.21.refs_1_.refs_0_ = bf16[16,64,128]{2,1,0:T(8,128)(2,1)S(1)} collective-permute-done((bf16[16,64,128]{2,1,0:T(8,128)(2,1)S(1)}, bf16[16,64,128]{2,1,0:T(8,128)(2,1)S(1)}, u32[]{:S(2)}, u32[]{:S(2)}) %collective-permute-start.21) | collective-permute-done | bytes 262176 | tf_op jit(solution)/shard_map/ppermute | solution.py:532
  111.1 7.9 %all-to-all-start = ((bf16[128,16,128]{2,1,0:T(8,128)(2,1)}), bf16[128,16,128]{2,1,0:T(8,128)(2,1)S(1)}, u32[]{:S(2)}, u32[]{:S(2)}) async-start(bf16[128,16,128]{2,1,0:T(8,128)(2,1)} %get-tuple-element.32), calls=%async_computation | async-start | bytes 1048576 | tf_op jit(solution)/shard_map/all_to_all | solution.py:690
  119.0 6.6 %norm_grad.2 = (bf16[64,128,256]{2,1,0:T(8,128)(2,1)}, f32[8,128]{1,0:T(8,128)S(1)}) custom-call(s32[1]{0:T(128)} %bitcast.25.first_ref, bf16[64,128,256]{2,1,0:T(8,128)(2,1)} %features_ref.11, f32[1,256]{1,0:T(1,128)S(1)} %bitcast.67, bf16[64,256]{1,0:T(8,128)(2,1)S(1)} %bitcast.58, bf16[16,64,128]{2,1,0:T(8,128)(2,1)S(1)} %pad_maximum_fusion.1.refs_13_.grads_ref.refs_0_, ...), custom_call_target="tpu_custom_call" | custom-call | flops 268435456 | bytes 4194304 | tf_op jit(solution)/shard_map/norm_grad/pallas_call | solution.py:439
  125.7 7.4 %all-to-all-done.terms_ref = bf16[128,16,128]{2,1,0:T(8,128)(2,1)S(1)} async-done(((bf16[128,16,128]{2,1,0:T(8,128)(2,1)}), bf16[128,16,128]{2,1,0:T(8,128)(2,1)S(1)}, u32[]{:S(2)}, u32[]{:S(2)}) %all-to-all-start) | async-done | bytes 524320 | tf_op jit(solution)/shard_map/all_to_all | solution.py:690
  134.0 3.8 %all-to-all-start.1 = ((bf16[128,16,128]{2,1,0:T(8,128)(2,1)}), bf16[128,16,128]{2,1,0:T(8,128)(2,1)S(1)}, u32[]{:S(2)}, u32[]{:S(2)}) async-start(bf16[128,16,128]{2,1,0:T(8,128)(2,1)} %get-tuple-element.38), calls=%async_computation.1 | async-start | bytes 1048576 | tf_op jit(solution)/shard_map/all_to_all | solution.py:702
  137.8 6.6 %norm_grad.3 = (bf16[64,128,256]{2,1,0:T(8,128)(2,1)}, f32[8,128]{1,0:T(8,128)}) custom-call(s32[1]{0:T(128)} %bitcast.22.first_ref, bf16[64,128,256]{2,1,0:T(8,128)(2,1)} %features_ref.11, f32[1,256]{1,0:T(1,128)S(1)} %bitcast.68, bf16[64,256]{1,0:T(8,128)(2,1)S(1)} %bitcast.59, ...), custom_call_target="tpu_custom_call", output_to_operand_aliasing={{0}: (7, {})} | custom-call | flops 268435456 | bytes 4194304 | tf_op jit(solution)/shard_map/norm_grad/pallas_call | solution.py:439
  145.0 7.0 %all-to-all-done.1 = bf16[128,16,128]{2,1,0:T(8,128)(2,1)S(1)} async-done(((bf16[128,16,128]{2,1,0:T(8,128)(2,1)}), bf16[128,16,128]{2,1,0:T(8,128)(2,1)S(1)}, u32[]{:S(2)}, u32[]{:S(2)}) %all-to-all-start.1) | async-done | bytes 524320 | tf_op jit(solution)/shard_map/all_to_all | solution.py:702
  (97 shorter events, 22.6 us)
Async XLA Ops:
  8.0 5.8 %collective-permute-start.1 = (bf16[64,32,64]{2,1,0:T(8,128)(2,1)S(1)}, bf16[64,32,64]{2,1,0:T(8,128)(2,1)S(1)}, u32[]{:S(2)}, u32[]{:S(2)}) collective-permute-start(bf16[64,32,64]{2,1,0:T(8,128)(2,1)S(1)} %project.5), channel_id=1, source_target_pairs={{0,1},{1,0},{4,5},{5,4},{8,9},{9,8},{12,13},{13,12},{2,3},{3,2},{6... | collective-permute-start | bytes 786440 | tf_op jit(solution)/shard_map/ppermute | solution.py:532
  9.6 6.0 %collective-permute-start = (bf16[16,4096]{1,0:T(8,128)(2,1)S(1)}, bf16[16,4096]{1,0:T(8,128)(2,1)S(1)}, u32[]{:S(2)}, u32[]{:S(2)}) collective-permute-start(bf16[16,4096]{1,0:T(8,128)(2,1)S(1)} %bitcast.83), channel_id=1, source_target_pairs={{0,0},{1,1},{4,32},{5,33},{8,64},{9,65},{12,96},{13,97},{2,16},{3,... | collective-permute-start | bytes 393224 | tf_op jit(solution)/shard_map/ppermute | solution.py:532
  15.6 17.9 %collective-permute-start.4 = (bf16[16,4096]{1,0:T(8,128)(2,1)S(1)}, bf16[16,4096]{1,0:T(8,128)(2,1)S(1)}, u32[]{:S(2)}, u32[]{:S(2)}) collective-permute-start(bf16[16,4096]{1,0:T(8,128)(2,1)S(1)} %add_up.7.refs_0_), channel_id=1, source_target_pairs={{0,32},{1,33},{4,36},{5,37},{8,40},{9,41},{12,44},{13,45},{2,34},{... | collective-permute-start | bytes 393224 | tf_op jit(solution)/shard_map/ppermute | solution.py:532
  19.4 14.4 %collective-permute-start.3 = (bf16[16,4096]{1,0:T(8,128)(2,1)S(1)}, bf16[16,4096]{1,0:T(8,128)(2,1)S(1)}, u32[]{:S(2)}, u32[]{:S(2)}) collective-permute-start(bf16[16,4096]{1,0:T(8,128)(2,1)S(1)} %add_up.7.refs_0_), channel_id=1, source_target_pairs={{0,64},{1,65},{4,68},{5,69},{8,72},{9,73},{12,76},{13,77},{2,66},{... | collective-permute-start | bytes 393224 | tf_op jit(solution)/shard_map/ppermute | solution.py:532
  28.0 5.8 %collective-permute-start.2 = (bf16[16,4096]{1,0:T(8,128)(2,1)S(1)}, bf16[16,4096]{1,0:T(8,128)(2,1)S(1)}, u32[]{:S(2)}, u32[]{:S(2)}) collective-permute-start(bf16[16,4096]{1,0:T(8,128)(2,1)S(1)} %add_up.7.refs_0_), channel_id=1, source_target_pairs={{0,96},{1,97},{4,100},{5,101},{8,104},{9,105},{12,108},{13,109},{2... | collective-permute-start | bytes 393224 | tf_op jit(solution)/shard_map/ppermute | solution.py:532
  41.6 4.7 %collective-permute-start.8 = (bf16[16,4096]{1,0:T(8,128)(2,1)S(1)}, bf16[16,4096]{1,0:T(8,128)(2,1)S(1)}, u32[]{:S(2)}, u32[]{:S(2)}) collective-permute-start(bf16[16,4096]{1,0:T(8,128)(2,1)S(1)} %collective-permute-done.4.refs_2_.refs_3_), channel_id=1, source_target_pairs={{0,1},{1,0},{4,5},{5,4},{8,9},{9,8},{12,13},{13,12},{2,3},{3,2},{6... | collective-permute-start | bytes 393224 | tf_op jit(solution)/shard_map/ppermute | solution.py:532
  42.1 4.2 %collective-permute-start.7 = (bf16[16,4096]{1,0:T(8,128)(2,1)S(1)}, bf16[16,4096]{1,0:T(8,128)(2,1)S(1)}, u32[]{:S(2)}, u32[]{:S(2)}) collective-permute-start(bf16[16,4096]{1,0:T(8,128)(2,1)S(1)} %collective-permute-done.3.refs_1_.refs_2_), channel_id=1, source_target_pairs={{0,1},{1,0},{4,5},{5,4},{8,9},{9,8},{12,13},{13,12},{2,3},{3,2},{6... | collective-permute-start | bytes 393224 | tf_op jit(solution)/shard_map/ppermute | solution.py:532
  42.2 4.1 %collective-permute-start.6 = (bf16[16,4096]{1,0:T(8,128)(2,1)S(1)}, bf16[16,4096]{1,0:T(8,128)(2,1)S(1)}, u32[]{:S(2)}, u32[]{:S(2)}) collective-permute-start(bf16[16,4096]{1,0:T(8,128)(2,1)S(1)} %collective-permute-done.2.refs_0_.refs_1_), channel_id=1, source_target_pairs={{0,1},{1,0},{4,5},{5,4},{8,9},{9,8},{12,13},{13,12},{2,3},{3,2},{6... | collective-permute-start | bytes 393224 | tf_op jit(solution)/shard_map/ppermute | solution.py:532
  43.2 22.6 %collective-permute-start.15 = (bf16[16,4096]{1,0:T(8,128)(2,1)S(1)}, bf16[16,4096]{1,0:T(8,128)(2,1)S(1)}, u32[]{:S(2)}, u32[]{:S(2)}) collective-permute-start(bf16[16,4096]{1,0:T(8,128)(2,1)S(1)} %get-tuple-element.41), channel_id=1, source_target_pairs={{0,96},{1,97},{4,100},{5,101},{8,104},{9,105},{12,108},{13,109},{2... | collective-permute-start | bytes 393224 | tf_op jit(solution)/shard_map/ppermute | solution.py:532
  45.2 21.3 %collective-permute-start.14 = (bf16[16,4096]{1,0:T(8,128)(2,1)S(1)}, bf16[16,4096]{1,0:T(8,128)(2,1)S(1)}, u32[]{:S(2)}, u32[]{:S(2)}) collective-permute-start(bf16[16,4096]{1,0:T(8,128)(2,1)S(1)} %get-tuple-element.42), channel_id=1, source_target_pairs={{0,64},{1,65},{4,68},{5,69},{8,72},{9,73},{12,76},{13,77},{2,66},{... | collective-permute-start | bytes 393224 | tf_op jit(solution)/shard_map/ppermute | solution.py:532
  46.3 20.1 %collective-permute-start.13 = (bf16[16,4096]{1,0:T(8,128)(2,1)S(1)}, bf16[16,4096]{1,0:T(8,128)(2,1)S(1)}, u32[]{:S(2)}, u32[]{:S(2)}) collective-permute-start(bf16[16,4096]{1,0:T(8,128)(2,1)S(1)} %get-tuple-element.43), channel_id=1, source_target_pairs={{0,32},{1,33},{4,36},{5,37},{8,40},{9,41},{12,44},{13,45},{2,34},{... | collective-permute-start | bytes 393224 | tf_op jit(solution)/shard_map/ppermute | solution.py:532
  64.9 9.2 %collective-permute-start.12 = (bf16[32,2048]{1,0:T(8,128)(2,1)S(1)}, bf16[32,2048]{1,0:T(8,128)(2,1)S(1)}, u32[]{:S(2)}, u32[]{:S(2)}) collective-permute-start(bf16[32,2048]{1,0:T(8,128)(2,1)S(1)} %get-tuple-element.45), channel_id=1, source_target_pairs={{0,12},{1,13},{4,0},{5,1},{8,4},{9,5},{12,8},{13,9},{2,14},{3,15},... | collective-permute-start | bytes 393224 | tf_op jit(solution)/shard_map/ppermute | solution.py:532
  65.4 8.7 %collective-permute-start.11 = (bf16[32,2048]{1,0:T(8,128)(2,1)S(1)}, bf16[32,2048]{1,0:T(8,128)(2,1)S(1)}, u32[]{:S(2)}, u32[]{:S(2)}) collective-permute-start(bf16[32,2048]{1,0:T(8,128)(2,1)S(1)} %get-tuple-element.46), channel_id=1, source_target_pairs={{0,8},{1,9},{4,12},{5,13},{8,0},{9,1},{12,4},{13,5},{2,10},{3,11},... | collective-permute-start | bytes 393224 | tf_op jit(solution)/shard_map/ppermute | solution.py:532
  65.9 9.1 %collective-permute-start.10 = (bf16[32,2048]{1,0:T(8,128)(2,1)S(1)}, bf16[32,2048]{1,0:T(8,128)(2,1)S(1)}, u32[]{:S(2)}, u32[]{:S(2)}) collective-permute-start(bf16[32,2048]{1,0:T(8,128)(2,1)S(1)} %get-tuple-element.47), channel_id=1, source_target_pairs={{0,4},{1,5},{4,8},{5,9},{8,12},{9,13},{12,0},{13,1},{2,6},{3,7},{6... | collective-permute-start | bytes 393224 | tf_op jit(solution)/shard_map/ppermute | solution.py:532
  66.5 8.4 %collective-permute-start.16 = (bf16[16,4096]{1,0:T(8,128)(2,1)S(1)}, bf16[16,4096]{1,0:T(8,128)(2,1)S(1)}, u32[]{:S(2)}, u32[]{:S(2)}) collective-permute-start(bf16[16,4096]{1,0:T(8,128)(2,1)S(1)} %add_up.9), channel_id=1, source_target_pairs={{0,0},{1,1},{4,32},{5,33},{8,64},{9,65},{12,96},{13,97},{2,16},{3,... | collective-permute-start | bytes 393224 | tf_op jit(solution)/shard_map/ppermute | solution.py:532
  75.0 18.9 %collective-permute-start.19 = (bf16[16,2048]{1,0:T(8,128)(2,1)S(1)}, bf16[16,2048]{1,0:T(8,128)(2,1)S(1)}, u32[]{:S(2)}, u32[]{:S(2)}) collective-permute-start(bf16[16,2048]{1,0:T(8,128)(2,1)S(1)} %get-tuple-element.52), channel_id=1, source_target_pairs={{0,3},{1,2},{4,7},{5,6},{8,11},{9,10},{12,15},{13,14},{2,1},{3,0},... | collective-permute-start | bytes 196616 | tf_op jit(solution)/shard_map/ppermute | solution.py:532
  88.7 5.3 %collective-permute-start.18 = (bf16[16,2048]{1,0:T(8,128)(2,1)S(1)}, bf16[16,2048]{1,0:T(8,128)(2,1)S(1)}, u32[]{:S(2)}, u32[]{:S(2)}) collective-permute-start(bf16[16,2048]{1,0:T(8,128)(2,1)S(1)} %get-tuple-element.52), channel_id=1, source_target_pairs={{0,1},{1,0},{4,5},{5,4},{8,9},{9,8},{12,13},{13,12},{2,3},{3,2},{6... | collective-permute-start | bytes 196616 | tf_op jit(solution)/shard_map/ppermute | solution.py:532
  88.7 5.2 %collective-permute-start.17 = (bf16[16,2048]{1,0:T(8,128)(2,1)S(1)}, bf16[16,2048]{1,0:T(8,128)(2,1)S(1)}, u32[]{:S(2)}, u32[]{:S(2)}) collective-permute-start(bf16[16,2048]{1,0:T(8,128)(2,1)S(1)} %get-tuple-element.51.refs_0_), channel_id=1, source_target_pairs={{0,2},{1,3},{4,6},{5,7},{8,10},{9,11},{12,14},{13,15},{2,0},{3,1},... | collective-permute-start | bytes 196616 | tf_op jit(solution)/shard_map/ppermute | solution.py:532
  88.9 5.8 %collective-permute-start.20 = (bf16[16,4096]{1,0:T(8,128)(2,1)S(1)}, bf16[16,4096]{1,0:T(8,128)(2,1)S(1)}, u32[]{:S(2)}, u32[]{:S(2)}) collective-permute-start(bf16[16,4096]{1,0:T(8,128)(2,1)S(1)} %collective-permute-done.16.refs_5_.refs_0_), channel_id=1, source_target_pairs={{0,2},{1,3},{4,6},{5,7},{8,10},{9,11},{12,14},{13,15},{2,0},{3,1},... | collective-permute-start | bytes 393224 | tf_op jit(solution)/shard_map/ppermute | solution.py:532
  94.9 12.9 %collective-permute-start.23 = (bf16[16,64,128]{2,1,0:T(8,128)(2,1)S(1)}, bf16[16,64,128]{2,1,0:T(8,128)(2,1)S(1)}, u32[]{:S(2)}, u32[]{:S(2)}) collective-permute-start(bf16[16,64,128]{2,1,0:T(8,128)(2,1)S(1)} %pad_maximum_fusion.1.refs_13_.grads_ref.refs_0_), channel_id=1, source_target_pairs={{0,12},{1,13},{4,0},{5,1},{8,4},{9,5},{12,8},{13,9},{2,14},{3,15},... | collective-permute-start | bytes 786440 | tf_op jit(solution)/shard_map/ppermute | solution.py:532
  98.3 9.4 %collective-permute-start.22 = (bf16[16,64,128]{2,1,0:T(8,128)(2,1)S(1)}, bf16[16,64,128]{2,1,0:T(8,128)(2,1)S(1)}, u32[]{:S(2)}, u32[]{:S(2)}) collective-permute-start(bf16[16,64,128]{2,1,0:T(8,128)(2,1)S(1)} %pad_maximum_fusion.1.refs_13_.grads_ref.refs_0_), channel_id=1, source_target_pairs={{0,4},{1,5},{4,8},{5,9},{8,12},{9,13},{12,0},{13,1},{2,6},{3,7},{6... | collective-permute-start | bytes 786440 | tf_op jit(solution)/shard_map/ppermute | solution.py:532
  98.3 12.0 %collective-permute-start.21 = (bf16[16,64,128]{2,1,0:T(8,128)(2,1)S(1)}, bf16[16,64,128]{2,1,0:T(8,128)(2,1)S(1)}, u32[]{:S(2)}, u32[]{:S(2)}) collective-permute-start(bf16[16,64,128]{2,1,0:T(8,128)(2,1)S(1)} %pad_maximum_fusion.1.refs_13_.grads_ref.refs_0_), channel_id=1, source_target_pairs={{0,8},{1,9},{4,12},{5,13},{8,0},{9,1},{12,4},{13,5},{2,10},{3,11},... | collective-permute-start | bytes 786440 | tf_op jit(solution)/shard_map/ppermute | solution.py:532
  111.1 21.9 %all-to-all-start = ((bf16[128,16,128]{2,1,0:T(8,128)(2,1)}), bf16[128,16,128]{2,1,0:T(8,128)(2,1)S(1)}, u32[]{:S(2)}, u32[]{:S(2)}) async-start(bf16[128,16,128]{2,1,0:T(8,128)(2,1)} %get-tuple-element.32), calls=%async_computation | async-start | bytes 1048576 | tf_op jit(solution)/shard_map/all_to_all | solution.py:690
  134.0 18.0 %all-to-all-start.1 = ((bf16[128,16,128]{2,1,0:T(8,128)(2,1)}), bf16[128,16,128]{2,1,0:T(8,128)(2,1)S(1)}, u32[]{:S(2)}, u32[]{:S(2)}) async-start(bf16[128,16,128]{2,1,0:T(8,128)(2,1)} %get-tuple-element.38), calls=%async_computation.1 | async-start | bytes 1048576 | tf_op jit(solution)/shard_map/all_to_all | solution.py:702
  (12 other events, 44.0 us)

commit v4 on v3

--- a/solution.py
+++ b/solution.py
@@ -64,10 +64,12 @@
     seqs, residues, channels = features_ref.shape
     at_once = 256 // residues
     for s in range(0, seqs, at_once):
-        rescaled = norm_rows(
-            features_ref[s : s + at_once].reshape(at_once * residues, channels)
-        )
-        normed = (rescaled * gain_ref[...] + offset_ref[...]).astype(BF16)
+        normed = [
+            (norm_rows(features_ref[n, r : r + 64]) * gain_ref[...] + offset_ref[...]).astype(BF16)
+            for n in range(s, s + at_once)
+            for r in range(0, residues, 64)
+        ]
+        normed = jnp.concatenate(normed, axis=0)
         several = dot(weight_ref[...], normed, ((1,), (1,))).astype(BF16)
         for n in range(at_once):
             out_ref[s + n] = several[:, n * residues : (n + 1) * residues]
@@ -203,17 +205,22 @@
             cols_ref[here, :] = part.T
 
     outer_grad_block(cot_ref, weight_ref, grad_ref)
-    total = None
-    for d in range(0, width, 2):
-        both = jnp.concatenate([grad_ref[d], grad_ref[d + 1]], axis=1)
-        term = dot(both, cols_ref[d * cols : (d + 2) * cols, :], ((1,), (0,)))
-        total = term if total is None else total + term
-    total = total.T.astype(BF16)
-    for p in range(RING):
-        place = lax.rem(turn_ref[0] + p, RING)
-        for h in range(2):
-            first = (h * RING + p) * quarter
-            out_ref[place, h * quarter : (h + 1) * quarter, :] = total[first : first + quarter]
+    block = 8 * width
+    for first_row in range(0, grad_ref.shape[1], block):
+        here = slice(first_row, first_row + block)
+        total = None
+        for d in range(0, width, 2):
+            both = jnp.concatenate([grad_ref[d, here], grad_ref[d + 1, here]], axis=1)
+            term = dot(both, cols_ref[d * cols : (d + 2) * cols, :], ((1,), (0,)))
+            total = term if total is None else total + term
+        total = total.T.astype(BF16)
+        for p in range(RING):
+            place = lax.rem(turn_ref[0] + p, RING)
+            for h in range(2):
+                first = (h * RING + p) * quarter
+                out_ref[place, h * quarter : (h + 1) * quarter, here] = total[
+                    first : first + quarter
+                ]
 
 
 def left_grad_part(turn, pieces, cotangent, weight, after=()):

time: 154 us -> 146 us (0.948)
  Pallas kernels: 69.3 us -> 61.1 us
    pallas_call x1, Pallas kernels: 18.5 us -> 10.2 us  [left_grad_part(): pl.pallas_call(left_grad_kernel, grid_spec=pltpu.PrefetchScalarGridSpec(n...]
  transfers between devices with their start and end apart: 26 -> 26, of which waited for: 6 -> 6; matrix products, arithmetic and copies ran while one was open for 2% -> 2% of each run, Pallas kernels for 36% -> 33%
where the time goes in v4:
time: 146 us
  Pallas kernels  61.1 us (42%)
  starting transfers between devices  53.8 us (37%)
  waiting for transfers between devices  18.5 us (13%)
  local copies, waits for them, and re-layouts  10.1 us (7%)
    ppermute x24, starting transfers between devices, torus_permute(): return lax.ppermute(value, AXES, pairs)  42.4 us
    pallas_call x3, Pallas kernels, pair_and_weight_grad(): pl.pallas_call(functools.partial(pair_kernel, fresh), grid=(count,), in_s...  14.3 us
    pallas_call x2, Pallas kernels, norm_grad(): pl.pallas_call(functools.partial(norm_grad_kernel, len(pieces)), grid_spe...  13.3 us
    pallas_call x1, Pallas kernels, left_grad_part(): pl.pallas_call(left_grad_kernel, grid_spec=pltpu.PrefetchScalarGridSpec(n...  10.2 us
    pallas_call x3, Pallas kernels, project(): pl.pallas_call(project_kernel, grid_spec=pltpu.PrefetchScalarGridSpec(num...  9.9 us
    pallas_call x2, Pallas kernels, right_grad_part(): pl.pallas_call(functools.partial(right_grad_kernel, fresh), grid=(count,)...  9.09 us
    all_to_all x1, starting transfers between devices, body(): came = lax.all_to_all(terms, AXES, 0, 0, tiled=True)  7.67 us
    all_to_all x1, waiting for transfers between devices, body(): came = lax.all_to_all(terms, AXES, 0, 0, tiled=True)  7.36 us
  transfers between devices with their start and end apart: 26, of which 6 were waited for; matrix products, arithmetic and copies ran while one was open for 2% of the time, Pallas kernels for 33%

profile of v4, /device:TPU:1, one launch (start us, length us, event | category | flops | bytes accessed | tf_op | source)
XLA Modules:
  0.0 145.7 jit_solution(6836678493778728158)
XLA Ops:
  1.6 3.1 %project.3.refs_0_ = bf16[16,32,128]{2,1,0:T(8,128)(2,1)S(1)} custom-call(s32[2]{0:T(128)S(1)} %pad_add_fusion.place_ref, bf16[64,128,256]{2,1,0:T(8,128)(2,1)} %features_ref.11, f32[1,256]{1,0:T(1,128)} %bitcast.63, f32[1,256]{1,0:T(1,128)} %bitcast.69, bf16[32,256]{1,0:T(8,128)(2,1)S(1)} %get-tuple-element.54.weight_ref), custom_call_target="tpu_custom_call" | custom-call | flops 67108864 | bytes 1179648 | tf_op jit(solution)/shard_map/project/pallas_call | solution.py:87
  4.7 3.4 %project.5 = bf16[64,32,64]{2,1,0:T(8,128)(2,1)S(1)} custom-call(s32[2]{0:T(128)S(1)} %get-tuple-element.56.place_ref, bf16[64,128,256]{2,1,0:T(8,128)(2,1)S(1)} %copy-done, f32[1,256]{1,0:T(1,128)S(1)} %bitcast.64, f32[1,256]{1,0:T(1,128)S(1)} %bitcast.70, bf16[32,256]{1,0:T(8,128)(2,1)S(1)} %get-tuple-element.53.weight_ref, ...), custom_call_target="tpu_custom_call" | custom-call | flops 134217728 | bytes 2359296 | tf_op jit(solution)/shard_map/project/pallas_call | solution.py:87
  10.4 3.4 %project.4 = bf16[64,32,64]{2,1,0:T(8,128)(2,1)S(1)} custom-call(s32[2]{0:T(128)S(1)} %get-tuple-element.55.place_ref, bf16[64,128,256]{2,1,0:T(8,128)(2,1)S(1)} %copy-done, f32[1,256]{1,0:T(1,128)S(1)} %bitcast.65, f32[1,256]{1,0:T(1,128)S(1)} %bitcast.71, bf16[32,256]{1,0:T(8,128)(2,1)S(1)} %get-tuple-element.53.weight_ref, ...), custom_call_target="tpu_custom_call" | custom-call | flops 134217728 | bytes 2359296 | tf_op jit(solution)/shard_map/project/pallas_call | solution.py:87
  15.7 3.8 %collective-permute-start.4 = (bf16[16,4096]{1,0:T(8,128)(2,1)S(1)}, bf16[16,4096]{1,0:T(8,128)(2,1)S(1)}, u32[]{:S(2)}, u32[]{:S(2)}) collective-permute-start(bf16[16,4096]{1,0:T(8,128)(2,1)S(1)} %add_up.7.refs_0_), channel_id=1, source_target_pairs={{0,32},{1,33},{4,36},{5,37},{8,40},{9,41},{12,44},{13,45},{2,34},{... | collective-permute-start | bytes 393224 | tf_op jit(solution)/shard_map/ppermute | solution.py:539
  19.5 8.6 %collective-permute-start.3 = (bf16[16,4096]{1,0:T(8,128)(2,1)S(1)}, bf16[16,4096]{1,0:T(8,128)(2,1)S(1)}, u32[]{:S(2)}, u32[]{:S(2)}) collective-permute-start(bf16[16,4096]{1,0:T(8,128)(2,1)S(1)} %add_up.7.refs_0_), channel_id=1, source_target_pairs={{0,64},{1,65},{4,68},{5,69},{8,72},{9,73},{12,76},{13,77},{2,66},{... | collective-permute-start | bytes 393224 | tf_op jit(solution)/shard_map/ppermute | solution.py:539
  28.1 1.6 %copy-done.4 = bf16[64,128,128]{2,1,0:T(8,128)(2,1)S(1)} copy-done((bf16[64,128,128]{2,1,0:T(8,128)(2,1)S(1)}, bf16[64,128,128]{2,1,0:T(8,128)(2,1)}, u32[]{:S(2)}) %copy-start.4) | copy-done | bytes 2097176
  29.7 3.9 %right_grad.2 = (bf16[8,128]{1,0:T(8,128)(2,1)}, f32[128,4096]{1,0:T(8,128)S(1)}, f32[8,128]{1,0:T(8,128)S(1)}) custom-call(bf16[64,128,128]{2,1,0:T(8,128)(2,1)S(1)} %copy-done.4, bf16[1024,128]{1,0:T(8,128)(2,1)S(1)} %bitcast.52, bf16[2048,128]{1,0:T(8,128)(2,1)S(1)} %bitcast.46, ...), custom_call_target="tpu_custom_call" | custom-call | flops 2147483648 | bytes 1048576 | tf_op jit(solution)/shard_map/right_grad/pallas_call | solution.py:163
  33.8 5.2 %right_grad.3 = (bf16[128,4096]{1,0:T(8,128)(2,1)S(1)}, f32[128,4096]{1,0:T(8,128)}, f32[8,128]{1,0:T(8,128)S(1)}) custom-call(bf16[64,128,128]{2,1,0:T(8,128)(2,1)S(1)} %copy-done.4, bf16[1024,128]{1,0:T(8,128)(2,1)S(1)} %bitcast.53, bf16[2048,128]{1,0:T(8,128)(2,1)S(1)} %bitcast.47, f32[128,4096]{1,0:T(8,128)S(1)} %get-tuple-element.22.total_in_ref, ...), custom_call_target="tpu_custom_call" | custom-call | flops 2147483648 | bytes 1048576 | tf_op jit(solution)/shard_map/right_grad/pallas_call | solution.py:163
  43.3 1.9 %collective-permute-start.15 = (bf16[16,4096]{1,0:T(8,128)(2,1)S(1)}, bf16[16,4096]{1,0:T(8,128)(2,1)S(1)}, u32[]{:S(2)}, u32[]{:S(2)}) collective-permute-start(bf16[16,4096]{1,0:T(8,128)(2,1)S(1)} %get-tuple-element.41), channel_id=1, source_target_pairs={{0,96},{1,97},{4,100},{5,101},{8,104},{9,105},{12,108},{13,109},{2... | collective-permute-start | bytes 393224 | tf_op jit(solution)/shard_map/ppermute | solution.py:539
  46.4 10.2 %left_grad.1.refs_13_.refs_4_ = bf16[4,32,2048]{2,1,0:T(8,128)(2,1)S(1)} custom-call(s32[1]{0:T(128)} %bitcast.15.turn_ref, bf16[16,4096]{1,0:T(8,128)(2,1)S(1)} %add_up.7.refs_0_, bf16[16,4096]{1,0:T(8,128)(2,1)S(1)} %collective-permute-done.2.refs_0_.refs_1_, bf16[16,4096]{1,0:T(8,128)(2,1)S(1)} %collective-permute-done.3.refs_1_.refs_2_, ...), custom_call_target="tpu_custom_call" | custom-call | flops 8589934592 | bytes 2097152 | tf_op jit(solution)/shard_map/left_grad/pallas_call | solution.py:232
  59.0 6.9 %pair_update.3 = (bf16[64,128,128]{2,1,0:T(8,128)(2,1)}, f32[1024,128]{1,0:T(8,128)S(1)}) custom-call(bf16[16,4096]{1,0:T(8,128)(2,1)S(1)} %add_up.7.refs_0_, bf16[16,4096]{1,0:T(8,128)(2,1)S(1)} %collective-permute-done.2.refs_0_.refs_1_, bf16[16,4096]{1,0:T(8,128)(2,1)S(1)} %collective-permute-done.3.refs_1_.refs_2_, ...), custom_call_target="tpu_custom_call" | custom-call | flops 6442450944 | bytes 2097152 | tf_op jit(solution)/shard_map/pair_update/pallas_call | solution.py:341
  66.8 13.6 %collective-permute-start.19 = (bf16[16,2048]{1,0:T(8,128)(2,1)S(1)}, bf16[16,2048]{1,0:T(8,128)(2,1)S(1)}, u32[]{:S(2)}, u32[]{:S(2)}) collective-permute-start(bf16[16,2048]{1,0:T(8,128)(2,1)S(1)} %get-tuple-element.52), channel_id=1, source_target_pairs={{0,3},{1,2},{4,7},{5,6},{8,11},{9,10},{12,15},{13,14},{2,1},{3,0},... | collective-permute-start | bytes 196616 | tf_op jit(solution)/shard_map/ppermute | solution.py:539
  81.9 3.7 %pair_update.4 = (bf16[64,128,128]{2,1,0:T(8,128)(2,1)}, f32[1024,128]{1,0:T(8,128)S(1)}) custom-call(bf16[16,4096]{1,0:T(8,128)(2,1)S(1)} %add_up.7.refs_0_, bf16[16,4096]{1,0:T(8,128)(2,1)S(1)} %collective-permute-done.2.refs_0_.refs_1_, bf16[16,4096]{1,0:T(8,128)(2,1)S(1)} %collective-permute-done.3.refs_1_.refs_2_, ...), custom_call_target="tpu_custom_call", output_to_operand_aliasing={{0}: (14, {})} | custom-call | flops 3221225472 | bytes 1048576 | tf_op jit(solution)/shard_map/pair_update/pallas_call | solution.py:341
  86.6 3.4 %collective-permute-start.23 = (bf16[16,64,128]{2,1,0:T(8,128)(2,1)S(1)}, bf16[16,64,128]{2,1,0:T(8,128)(2,1)S(1)}, u32[]{:S(2)}, u32[]{:S(2)}) collective-permute-start(bf16[16,64,128]{2,1,0:T(8,128)(2,1)S(1)} %pad_maximum_fusion.1.refs_13_.grads_ref.refs_0_), channel_id=1, source_target_pairs={{0,12},{1,13},{4,0},{5,1},{8,4},{9,5},{12,8},{13,9},{2,14},{3,15},... | collective-permute-start | bytes 786440 | tf_op jit(solution)/shard_map/ppermute | solution.py:539
  91.5 2.2 %projection_grad.1 = f32[64,256]{1,0:T(8,128)S(1)} custom-call(s32[2]{0:T(128)S(1)} %pad_add_fusion.3.place_ref, bf16[64,128,256]{2,1,0:T(8,128)(2,1)} %features_ref.11, f32[1,256]{1,0:T(1,128)S(1)} %bitcast.66, f32[1,256]{1,0:T(1,128)S(1)} %bitcast.72, bf16[16,64,128]{2,1,0:T(8,128)(2,1)S(1)} %pad_maximum_fusion.1.refs_13_.grads_ref.refs_0_), custom_call_target="tpu_custom_call" | custom-call | tf_op jit(solution)/shard_map/projection_grad/pallas_call | solution.py:384
  93.7 1.6 %copy-done.6 = bf16[64,128,128]{2,1,0:T(8,128)(2,1)S(1)} copy-done((bf16[64,128,128]{2,1,0:T(8,128)(2,1)S(1)}, bf16[64,128,128]{2,1,0:T(8,128)(2,1)}, u32[]{:S(2)}) %copy-start.6) | copy-done | bytes 2097176
  95.9 3.7 %pair_update.5 = (bf16[64,128,128]{2,1,0:T(8,128)(2,1)}, f32[1024,128]{1,0:T(8,128)S(1)}) custom-call(bf16[16,4096]{1,0:T(8,128)(2,1)S(1)} %add_up.7.refs_0_, bf16[16,4096]{1,0:T(8,128)(2,1)S(1)} %collective-permute-done.2.refs_0_.refs_1_, bf16[16,4096]{1,0:T(8,128)(2,1)S(1)} %collective-permute-done.3.refs_1_.refs_2_, ...), custom_call_target="tpu_custom_call", output_to_operand_aliasing={{0}: (14, {})} | custom-call | flops 3221225472 | bytes 1048576 | tf_op jit(solution)/shard_map/pair_update/pallas_call | solution.py:341
  99.7 2.5 %collective-permute-done.21.refs_1_.refs_0_ = bf16[16,64,128]{2,1,0:T(8,128)(2,1)S(1)} collective-permute-done((bf16[16,64,128]{2,1,0:T(8,128)(2,1)S(1)}, bf16[16,64,128]{2,1,0:T(8,128)(2,1)S(1)}, u32[]{:S(2)}, u32[]{:S(2)}) %collective-permute-start.21) | collective-permute-done | bytes 262176 | tf_op jit(solution)/shard_map/ppermute | solution.py:539
  103.1 7.7 %all-to-all-start = ((bf16[128,16,128]{2,1,0:T(8,128)(2,1)}), bf16[128,16,128]{2,1,0:T(8,128)(2,1)S(1)}, u32[]{:S(2)}, u32[]{:S(2)}) async-start(bf16[128,16,128]{2,1,0:T(8,128)(2,1)} %get-tuple-element.32), calls=%async_computation | async-start | bytes 1048576 | tf_op jit(solution)/shard_map/all_to_all | solution.py:697
  110.8 6.6 %norm_grad.2 = (bf16[64,128,256]{2,1,0:T(8,128)(2,1)}, f32[8,128]{1,0:T(8,128)S(1)}) custom-call(s32[1]{0:T(128)} %bitcast.25.first_ref, bf16[64,128,256]{2,1,0:T(8,128)(2,1)} %features_ref.11, f32[1,256]{1,0:T(1,128)S(1)} %bitcast.67, bf16[64,256]{1,0:T(8,128)(2,1)S(1)} %bitcast.58, bf16[16,64,128]{2,1,0:T(8,128)(2,1)S(1)} %pad_maximum_fusion.1.refs_13_.grads_ref.refs_0_, ...), custom_call_target="tpu_custom_call" | custom-call | flops 268435456 | bytes 4194304 | tf_op jit(solution)/shard_map/norm_grad/pallas_call | solution.py:446
  117.4 7.4 %all-to-all-done.terms_ref = bf16[128,16,128]{2,1,0:T(8,128)(2,1)S(1)} async-done(((bf16[128,16,128]{2,1,0:T(8,128)(2,1)}), bf16[128,16,128]{2,1,0:T(8,128)(2,1)S(1)}, u32[]{:S(2)}, u32[]{:S(2)}) %all-to-all-start) | async-done | bytes 524320 | tf_op jit(solution)/shard_map/all_to_all | solution.py:697
  125.7 3.8 %all-to-all-start.1 = ((bf16[128,16,128]{2,1,0:T(8,128)(2,1)}), bf16[128,16,128]{2,1,0:T(8,128)(2,1)S(1)}, u32[]{:S(2)}, u32[]{:S(2)}) async-start(bf16[128,16,128]{2,1,0:T(8,128)(2,1)} %get-tuple-element.38), calls=%async_computation.1 | async-start | bytes 1048576 | tf_op jit(solution)/shard_map/all_to_all | solution.py:709
  129.6 6.6 %norm_grad.3 = (bf16[64,128,256]{2,1,0:T(8,128)(2,1)}, f32[8,128]{1,0:T(8,128)}) custom-call(s32[1]{0:T(128)} %bitcast.22.first_ref, bf16[64,128,256]{2,1,0:T(8,128)(2,1)} %features_ref.11, f32[1,256]{1,0:T(1,128)S(1)} %bitcast.68, bf16[64,256]{1,0:T(8,128)(2,1)S(1)} %bitcast.59, ...), custom_call_target="tpu_custom_call", output_to_operand_aliasing={{0}: (7, {})} | custom-call | flops 268435456 | bytes 4194304 | tf_op jit(solution)/shard_map/norm_grad/pallas_call | solution.py:446
  136.7 7.0 %all-to-all-done.1 = bf16[128,16,128]{2,1,0:T(8,128)(2,1)S(1)} async-done(((bf16[128,16,128]{2,1,0:T(8,128)(2,1)}), bf16[128,16,128]{2,1,0:T(8,128)(2,1)S(1)}, u32[]{:S(2)}, u32[]{:S(2)}) %all-to-all-start.1) | async-done | bytes 524320 | tf_op jit(solution)/shard_map/all_to_all | solution.py:709
  (97 shorter events, 22.8 us)
Async XLA Ops:
  8.1 5.8 %collective-permute-start.1 = (bf16[64,32,64]{2,1,0:T(8,128)(2,1)S(1)}, bf16[64,32,64]{2,1,0:T(8,128)(2,1)S(1)}, u32[]{:S(2)}, u32[]{:S(2)}) collective-permute-start(bf16[64,32,64]{2,1,0:T(8,128)(2,1)S(1)} %project.5), channel_id=1, source_target_pairs={{0,1},{1,0},{4,5},{5,4},{8,9},{9,8},{12,13},{13,12},{2,3},{3,2},{6... | collective-permute-start | bytes 786440 | tf_op jit(solution)/shard_map/ppermute | solution.py:539
  9.7 6.0 %collective-permute-start = (bf16[16,4096]{1,0:T(8,128)(2,1)S(1)}, bf16[16,4096]{1,0:T(8,128)(2,1)S(1)}, u32[]{:S(2)}, u32[]{:S(2)}) collective-permute-start(bf16[16,4096]{1,0:T(8,128)(2,1)S(1)} %bitcast.83), channel_id=1, source_target_pairs={{0,0},{1,1},{4,32},{5,33},{8,64},{9,65},{12,96},{13,97},{2,16},{3,... | collective-permute-start | bytes 393224 | tf_op jit(solution)/shard_map/ppermute | solution.py:539
  15.7 17.9 %collective-permute-start.4 = (bf16[16,4096]{1,0:T(8,128)(2,1)S(1)}, bf16[16,4096]{1,0:T(8,128)(2,1)S(1)}, u32[]{:S(2)}, u32[]{:S(2)}) collective-permute-start(bf16[16,4096]{1,0:T(8,128)(2,1)S(1)} %add_up.7.refs_0_), channel_id=1, source_target_pairs={{0,32},{1,33},{4,36},{5,37},{8,40},{9,41},{12,44},{13,45},{2,34},{... | collective-permute-start | bytes 393224 | tf_op jit(solution)/shard_map/ppermute | solution.py:539
  19.5 14.3 %collective-permute-start.3 = (bf16[16,4096]{1,0:T(8,128)(2,1)S(1)}, bf16[16,4096]{1,0:T(8,128)(2,1)S(1)}, u32[]{:S(2)}, u32[]{:S(2)}) collective-permute-start(bf16[16,4096]{1,0:T(8,128)(2,1)S(1)} %add_up.7.refs_0_), channel_id=1, source_target_pairs={{0,64},{1,65},{4,68},{5,69},{8,72},{9,73},{12,76},{13,77},{2,66},{... | collective-permute-start | bytes 393224 | tf_op jit(solution)/shard_map/ppermute | solution.py:539
  28.1 5.8 %collective-permute-start.2 = (bf16[16,4096]{1,0:T(8,128)(2,1)S(1)}, bf16[16,4096]{1,0:T(8,128)(2,1)S(1)}, u32[]{:S(2)}, u32[]{:S(2)}) collective-permute-start(bf16[16,4096]{1,0:T(8,128)(2,1)S(1)} %add_up.7.refs_0_), channel_id=1, source_target_pairs={{0,96},{1,97},{4,100},{5,101},{8,104},{9,105},{12,108},{13,109},{2... | collective-permute-start | bytes 393224 | tf_op jit(solution)/shard_map/ppermute | solution.py:539
  41.7 4.7 %collective-permute-start.8 = (bf16[16,4096]{1,0:T(8,128)(2,1)S(1)}, bf16[16,4096]{1,0:T(8,128)(2,1)S(1)}, u32[]{:S(2)}, u32[]{:S(2)}) collective-permute-start(bf16[16,4096]{1,0:T(8,128)(2,1)S(1)} %collective-permute-done.4.refs_2_.refs_3_), channel_id=1, source_target_pairs={{0,1},{1,0},{4,5},{5,4},{8,9},{9,8},{12,13},{13,12},{2,3},{3,2},{6... | collective-permute-start | bytes 393224 | tf_op jit(solution)/shard_map/ppermute | solution.py:539
  42.2 4.2 %collective-permute-start.7 = (bf16[16,4096]{1,0:T(8,128)(2,1)S(1)}, bf16[16,4096]{1,0:T(8,128)(2,1)S(1)}, u32[]{:S(2)}, u32[]{:S(2)}) collective-permute-start(bf16[16,4096]{1,0:T(8,128)(2,1)S(1)} %collective-permute-done.3.refs_1_.refs_2_), channel_id=1, source_target_pairs={{0,1},{1,0},{4,5},{5,4},{8,9},{9,8},{12,13},{13,12},{2,3},{3,2},{6... | collective-permute-start | bytes 393224 | tf_op jit(solution)/shard_map/ppermute | solution.py:539
  42.3 4.1 %collective-permute-start.6 = (bf16[16,4096]{1,0:T(8,128)(2,1)S(1)}, bf16[16,4096]{1,0:T(8,128)(2,1)S(1)}, u32[]{:S(2)}, u32[]{:S(2)}) collective-permute-start(bf16[16,4096]{1,0:T(8,128)(2,1)S(1)} %collective-permute-done.2.refs_0_.refs_1_), channel_id=1, source_target_pairs={{0,1},{1,0},{4,5},{5,4},{8,9},{9,8},{12,13},{13,12},{2,3},{3,2},{6... | collective-permute-start | bytes 393224 | tf_op jit(solution)/shard_map/ppermute | solution.py:539
  43.3 14.3 %collective-permute-start.15 = (bf16[16,4096]{1,0:T(8,128)(2,1)S(1)}, bf16[16,4096]{1,0:T(8,128)(2,1)S(1)}, u32[]{:S(2)}, u32[]{:S(2)}) collective-permute-start(bf16[16,4096]{1,0:T(8,128)(2,1)S(1)} %get-tuple-element.41), channel_id=1, source_target_pairs={{0,96},{1,97},{4,100},{5,101},{8,104},{9,105},{12,108},{13,109},{2... | collective-permute-start | bytes 393224 | tf_op jit(solution)/shard_map/ppermute | solution.py:539
  45.2 13.0 %collective-permute-start.14 = (bf16[16,4096]{1,0:T(8,128)(2,1)S(1)}, bf16[16,4096]{1,0:T(8,128)(2,1)S(1)}, u32[]{:S(2)}, u32[]{:S(2)}) collective-permute-start(bf16[16,4096]{1,0:T(8,128)(2,1)S(1)} %get-tuple-element.42), channel_id=1, source_target_pairs={{0,64},{1,65},{4,68},{5,69},{8,72},{9,73},{12,76},{13,77},{2,66},{... | collective-permute-start | bytes 393224 | tf_op jit(solution)/shard_map/ppermute | solution.py:539
  46.4 11.8 %collective-permute-start.13 = (bf16[16,4096]{1,0:T(8,128)(2,1)S(1)}, bf16[16,4096]{1,0:T(8,128)(2,1)S(1)}, u32[]{:S(2)}, u32[]{:S(2)}) collective-permute-start(bf16[16,4096]{1,0:T(8,128)(2,1)S(1)} %get-tuple-element.43), channel_id=1, source_target_pairs={{0,32},{1,33},{4,36},{5,37},{8,40},{9,41},{12,44},{13,45},{2,34},{... | collective-permute-start | bytes 393224 | tf_op jit(solution)/shard_map/ppermute | solution.py:539
  56.6 9.2 %collective-permute-start.12 = (bf16[32,2048]{1,0:T(8,128)(2,1)S(1)}, bf16[32,2048]{1,0:T(8,128)(2,1)S(1)}, u32[]{:S(2)}, u32[]{:S(2)}) collective-permute-start(bf16[32,2048]{1,0:T(8,128)(2,1)S(1)} %get-tuple-element.45), channel_id=1, source_target_pairs={{0,12},{1,13},{4,0},{5,1},{8,4},{9,5},{12,8},{13,9},{2,14},{3,15},... | collective-permute-start | bytes 393224 | tf_op jit(solution)/shard_map/ppermute | solution.py:539
  57.2 8.7 %collective-permute-start.11 = (bf16[32,2048]{1,0:T(8,128)(2,1)S(1)}, bf16[32,2048]{1,0:T(8,128)(2,1)S(1)}, u32[]{:S(2)}, u32[]{:S(2)}) collective-permute-start(bf16[32,2048]{1,0:T(8,128)(2,1)S(1)} %get-tuple-element.46), channel_id=1, source_target_pairs={{0,8},{1,9},{4,12},{5,13},{8,0},{9,1},{12,4},{13,5},{2,10},{3,11},... | collective-permute-start | bytes 393224 | tf_op jit(solution)/shard_map/ppermute | solution.py:539
  57.6 9.1 %collective-permute-start.10 = (bf16[32,2048]{1,0:T(8,128)(2,1)S(1)}, bf16[32,2048]{1,0:T(8,128)(2,1)S(1)}, u32[]{:S(2)}, u32[]{:S(2)}) collective-permute-start(bf16[32,2048]{1,0:T(8,128)(2,1)S(1)} %get-tuple-element.47), channel_id=1, source_target_pairs={{0,4},{1,5},{4,8},{5,9},{8,12},{9,13},{12,0},{13,1},{2,6},{3,7},{6... | collective-permute-start | bytes 393224 | tf_op jit(solution)/shard_map/ppermute | solution.py:539
  58.3 8.4 %collective-permute-start.16 = (bf16[16,4096]{1,0:T(8,128)(2,1)S(1)}, bf16[16,4096]{1,0:T(8,128)(2,1)S(1)}, u32[]{:S(2)}, u32[]{:S(2)}) collective-permute-start(bf16[16,4096]{1,0:T(8,128)(2,1)S(1)} %add_up.9), channel_id=1, source_target_pairs={{0,0},{1,1},{4,32},{5,33},{8,64},{9,65},{12,96},{13,97},{2,16},{3,... | collective-permute-start | bytes 393224 | tf_op jit(solution)/shard_map/ppermute | solution.py:539
  66.8 18.9 %collective-permute-start.19 = (bf16[16,2048]{1,0:T(8,128)(2,1)S(1)}, bf16[16,2048]{1,0:T(8,128)(2,1)S(1)}, u32[]{:S(2)}, u32[]{:S(2)}) collective-permute-start(bf16[16,2048]{1,0:T(8,128)(2,1)S(1)} %get-tuple-element.52), channel_id=1, source_target_pairs={{0,3},{1,2},{4,7},{5,6},{8,11},{9,10},{12,15},{13,14},{2,1},{3,0},... | collective-permute-start | bytes 196616 | tf_op jit(solution)/shard_map/ppermute | solution.py:539
  80.4 5.3 %collective-permute-start.18 = (bf16[16,2048]{1,0:T(8,128)(2,1)S(1)}, bf16[16,2048]{1,0:T(8,128)(2,1)S(1)}, u32[]{:S(2)}, u32[]{:S(2)}) collective-permute-start(bf16[16,2048]{1,0:T(8,128)(2,1)S(1)} %get-tuple-element.52), channel_id=1, source_target_pairs={{0,1},{1,0},{4,5},{5,4},{8,9},{9,8},{12,13},{13,12},{2,3},{3,2},{6... | collective-permute-start | bytes 196616 | tf_op jit(solution)/shard_map/ppermute | solution.py:539
  80.4 5.2 %collective-permute-start.17 = (bf16[16,2048]{1,0:T(8,128)(2,1)S(1)}, bf16[16,2048]{1,0:T(8,128)(2,1)S(1)}, u32[]{:S(2)}, u32[]{:S(2)}) collective-permute-start(bf16[16,2048]{1,0:T(8,128)(2,1)S(1)} %get-tuple-element.51.refs_0_), channel_id=1, source_target_pairs={{0,2},{1,3},{4,6},{5,7},{8,10},{9,11},{12,14},{13,15},{2,0},{3,1},... | collective-permute-start | bytes 196616 | tf_op jit(solution)/shard_map/ppermute | solution.py:539
  80.6 5.8 %collective-permute-start.20 = (bf16[16,4096]{1,0:T(8,128)(2,1)S(1)}, bf16[16,4096]{1,0:T(8,128)(2,1)S(1)}, u32[]{:S(2)}, u32[]{:S(2)}) collective-permute-start(bf16[16,4096]{1,0:T(8,128)(2,1)S(1)} %collective-permute-done.16.refs_5_.refs_0_), channel_id=1, source_target_pairs={{0,2},{1,3},{4,6},{5,7},{8,10},{9,11},{12,14},{13,15},{2,0},{3,1},... | collective-permute-start | bytes 393224 | tf_op jit(solution)/shard_map/ppermute | solution.py:539
  86.6 13.1 %collective-permute-start.23 = (bf16[16,64,128]{2,1,0:T(8,128)(2,1)S(1)}, bf16[16,64,128]{2,1,0:T(8,128)(2,1)S(1)}, u32[]{:S(2)}, u32[]{:S(2)}) collective-permute-start(bf16[16,64,128]{2,1,0:T(8,128)(2,1)S(1)} %pad_maximum_fusion.1.refs_13_.grads_ref.refs_0_), channel_id=1, source_target_pairs={{0,12},{1,13},{4,0},{5,1},{8,4},{9,5},{12,8},{13,9},{2,14},{3,15},... | collective-permute-start | bytes 786440 | tf_op jit(solution)/shard_map/ppermute | solution.py:539
  90.0 9.7 %collective-permute-start.22 = (bf16[16,64,128]{2,1,0:T(8,128)(2,1)S(1)}, bf16[16,64,128]{2,1,0:T(8,128)(2,1)S(1)}, u32[]{:S(2)}, u32[]{:S(2)}) collective-permute-start(bf16[16,64,128]{2,1,0:T(8,128)(2,1)S(1)} %pad_maximum_fusion.1.refs_13_.grads_ref.refs_0_), channel_id=1, source_target_pairs={{0,4},{1,5},{4,8},{5,9},{8,12},{9,13},{12,0},{13,1},{2,6},{3,7},{6... | collective-permute-start | bytes 786440 | tf_op jit(solution)/shard_map/ppermute | solution.py:539
  90.0 12.2 %collective-permute-start.21 = (bf16[16,64,128]{2,1,0:T(8,128)(2,1)S(1)}, bf16[16,64,128]{2,1,0:T(8,128)(2,1)S(1)}, u32[]{:S(2)}, u32[]{:S(2)}) collective-permute-start(bf16[16,64,128]{2,1,0:T(8,128)(2,1)S(1)} %pad_maximum_fusion.1.refs_13_.grads_ref.refs_0_), channel_id=1, source_target_pairs={{0,8},{1,9},{4,12},{5,13},{8,0},{9,1},{12,4},{13,5},{2,10},{3,11},... | collective-permute-start | bytes 786440 | tf_op jit(solution)/shard_map/ppermute | solution.py:539
  103.1 21.7 %all-to-all-start = ((bf16[128,16,128]{2,1,0:T(8,128)(2,1)}), bf16[128,16,128]{2,1,0:T(8,128)(2,1)S(1)}, u32[]{:S(2)}, u32[]{:S(2)}) async-start(bf16[128,16,128]{2,1,0:T(8,128)(2,1)} %get-tuple-element.32), calls=%async_computation | async-start | bytes 1048576 | tf_op jit(solution)/shard_map/all_to_all | solution.py:697
  125.7 18.0 %all-to-all-start.1 = ((bf16[128,16,128]{2,1,0:T(8,128)(2,1)}), bf16[128,16,128]{2,1,0:T(8,128)(2,1)S(1)}, u32[]{:S(2)}, u32[]{:S(2)}) async-start(bf16[128,16,128]{2,1,0:T(8,128)(2,1)} %get-tuple-element.38), calls=%async_computation.1 | async-start | bytes 1048576 | tf_op jit(solution)/shard_map/all_to_all | solution.py:709
  (12 other events, 44.0 us)

commit v5 on v4

--- a/solution.py
+++ b/solution.py
@@ -70,14 +70,14 @@
             for r in range(0, residues, 64)
         ]
         normed = jnp.concatenate(normed, axis=0)
-        several = dot(weight_ref[...], normed, ((1,), (1,))).astype(BF16)
+        several = dot(normed, weight_ref[...], ((1,), (0,))).T.astype(BF16)
         for n in range(at_once):
             out_ref[s + n] = several[:, n * residues : (n + 1) * residues]
 
 
 def project(first, count, part, residues, features, gain, offset, weight, after=()):
     total, _, channels = features.shape
-    width = weight.shape[0]
+    width = weight.shape[1]
     seqs = min(2048 // residues, 16)
     steps = total // seqs
 
@@ -93,7 +93,7 @@
                 pl.BlockSpec((seqs, residues, channels), place),
                 whole((1, channels)),
                 whole((1, channels)),
-                whole((width, channels)),
+                whole((channels, width)),
             ]
             + [ANYWHERE] * len(after),
             out_specs=pl.BlockSpec((seqs, width, residues), lambda n, place_ref: (n, 0, 0)),
@@ -597,7 +597,7 @@
         features,
         pltpu.with_memory_space_constraint(gain_row, pltpu.HBM),
         pltpu.with_memory_space_constraint(offset_row, pltpu.HBM),
-        weight_rows[width:],
+        projection_weight[:, width:],
     )
     arrived = transpose_xz(right_piece.reshape(quarter, width * residues))
 
@@ -610,7 +610,7 @@
             alignment_features,
             gain_row,
             offset_row,
-            weight_rows[:width],
+            projection_weight[:, :width],
             after=(right_piece,),
         )
 
@@ -655,7 +655,7 @@
     left_came = [shift_x(left_partial[t], t) for t in range(1, RING)]
     right_sum = transpose_xz(add_up([pieces[0], *right_came], after=(left_partial,)))
 
-    def pair_part(first, count, before, after):
+    def pair_part(first, count, before, after, cotangent=cotangent):
         return pair_and_weight_grad(
             first,
             count,
@@ -687,7 +687,13 @@
     grads = jnp.concatenate([left_grad, right_grad.reshape(quarter, width, residues)], axis=1)
     grad_pieces = [grads] + [shift_x(grads, -t) for t in range(1, RING)]
 
-    pair_update_result, weight_partial = pair_part(blocks - blocks // 4, blocks // 4, pair, (grads,))
+    pair_update_result, weight_partial = pair_part(
+        blocks - blocks // 4,
+        blocks // 4,
+        pair,
+        (grads,),
+        pltpu.with_memory_space_constraint(cotangent, pltpu.HBM),
+    )
     projection_part = projection_grad_part(x, low_y, features, gain_row, offset_row, grads)
     devices = 128
     terms, token = gather_terms(

time: 146 us -> 149 us (1.021)
  Pallas kernels: 61.1 us -> 66.6 us
  starting transfers between devices: 53.8 us -> 51.8 us
    pallas_call x3, Pallas kernels: 9.9 us -> 14.4 us  [project(): pl.pallas_call(project_kernel, grid_spec=pltpu.PrefetchScalarGridSpec(num...]
    ppermute x24, starting transfers between devices: 42.4 us -> 40.1 us  [torus_permute(): return lax.ppermute(value, AXES, pairs)]
  transfers between devices with their start and end apart: 26 -> 26, of which waited for: 6 -> 6; matrix products, arithmetic and copies ran while one was open for 2% -> 2% of each run, Pallas kernels for 33% -> 34%
where the time goes in v5:
time: 149 us
  Pallas kernels  66.6 us (45%)
  starting transfers between devices  51.8 us (35%)
  waiting for transfers between devices  19.5 us (13%)
  local copies, waits for them, and re-layouts  8.71 us (6%)
    ppermute x24, starting transfers between devices, torus_permute(): return lax.ppermute(value, AXES, pairs)  40.1 us
    pallas_call x3, Pallas kernels, pair_and_weight_grad(): pl.pallas_call(functools.partial(pair_kernel, fresh), grid=(count,), in_s...  15.4 us
    pallas_call x3, Pallas kernels, project(): pl.pallas_call(project_kernel, grid_spec=pltpu.PrefetchScalarGridSpec(num...  14.4 us
    pallas_call x2, Pallas kernels, norm_grad(): pl.pallas_call(functools.partial(norm_grad_kernel, len(pieces)), grid_spe...  13.3 us
    pallas_call x1, Pallas kernels, left_grad_part(): pl.pallas_call(left_grad_kernel, grid_spec=pltpu.PrefetchScalarGridSpec(n...  10.2 us
    pallas_call x2, Pallas kernels, right_grad_part(): pl.pallas_call(functools.partial(right_grad_kernel, fresh), grid=(count,)...  9.08 us
    all_to_all x1, starting transfers between devices, body(): came = lax.all_to_all(terms, AXES, 0, 0, tiled=True)  7.88 us
    all_to_all x1, waiting for transfers between devices, body(): came = lax.all_to_all(terms, AXES, 0, 0, tiled=True)  7.36 us
  transfers between devices with their start and end apart: 26, of which 6 were waited for; matrix products, arithmetic and copies ran while one was open for 2% of the time, Pallas kernels for 34%

profile of v5, /device:TPU:1, one launch (start us, length us, event | category | flops | bytes accessed | tf_op | source)
XLA Modules:
  0.0 149.0 jit_solution(13897386776166855291)
XLA Ops:
  1.8 4.5 %project.3.refs_0_ = bf16[16,32,128]{2,1,0:T(8,128)(2,1)S(1)} custom-call(s32[2]{0:T(128)S(1)} %pad_add_fusion.place_ref, bf16[64,128,256]{2,1,0:T(8,128)(2,1)} %features_ref.11, f32[1,256]{1,0:T(1,128)} %bitcast.62, f32[1,256]{1,0:T(1,128)} %bitcast.68, bf16[256,32]{1,0:T(8,128)(2,1)S(1)} %copy.38.weight_ref), custom_call_target="tpu_custom_call" | custom-call | flops 67108864 | bytes 1179648 | tf_op jit(solution)/shard_map/project/pallas_call | solution.py:87
  6.4 5.0 %project.5 = bf16[64,32,64]{2,1,0:T(8,128)(2,1)S(1)} custom-call(s32[2]{0:T(128)S(1)} %get-tuple-element.56.place_ref, bf16[64,128,256]{2,1,0:T(8,128)(2,1)S(1)} %copy-done, f32[1,256]{1,0:T(1,128)S(1)} %bitcast.63, f32[1,256]{1,0:T(1,128)S(1)} %bitcast.69, bf16[256,32]{1,0:T(8,128)(2,1)S(1)} %copy.39.weight_ref, bf16[16,32,128]{2,1,0:T(8,128)(2,1)S(1)} %project.3.refs_0_), custom_call_target="tpu_custom_call" | custom-call | flops 134217728 | bytes 2359296 | tf_op jit(solution)/shard_map/project/pallas_call | solution.py:87
  13.7 5.0 %project.4 = bf16[64,32,64]{2,1,0:T(8,128)(2,1)S(1)} custom-call(s32[2]{0:T(128)S(1)} %get-tuple-element.55.place_ref, bf16[64,128,256]{2,1,0:T(8,128)(2,1)S(1)} %copy-done, f32[1,256]{1,0:T(1,128)S(1)} %bitcast.64, f32[1,256]{1,0:T(1,128)S(1)} %bitcast.70, bf16[256,32]{1,0:T(8,128)(2,1)S(1)} %copy.39.weight_ref, bf16[16,32,128]{2,1,0:T(8,128)(2,1)S(1)} %project.3.refs_0_), custom_call_target="tpu_custom_call" | custom-call | flops 134217728 | bytes 2359296 | tf_op jit(solution)/shard_map/project/pallas_call | solution.py:87
  18.9 1.5 %copy.32 = bf16[64,32,128]{2,1,0:T(8,128)(2,1)S(1)} copy(bf16[64,32,128]{0,1,2:T(8,128)(2,1)S(1)} %pad_maximum_fusion) | data formatting | bytes 1048576 | tf_op jit(solution)/shard_map/concatenate | solution.py:619
  20.5 3.8 %collective-permute-start.4 = (bf16[16,4096]{1,0:T(8,128)(2,1)S(1)}, bf16[16,4096]{1,0:T(8,128)(2,1)S(1)}, u32[]{:S(2)}, u32[]{:S(2)}) collective-permute-start(bf16[16,4096]{1,0:T(8,128)(2,1)S(1)} %add_up.7.refs_0_), channel_id=1, source_target_pairs={{0,32},{1,33},{4,36},{5,37},{8,40},{9,41},{12,44},{13,45},{2,34},{... | collective-permute-start | bytes 393224 | tf_op jit(solution)/shard_map/ppermute | solution.py:539
  24.3 7.1 %collective-permute-start.3 = (bf16[16,4096]{1,0:T(8,128)(2,1)S(1)}, bf16[16,4096]{1,0:T(8,128)(2,1)S(1)}, u32[]{:S(2)}, u32[]{:S(2)}) collective-permute-start(bf16[16,4096]{1,0:T(8,128)(2,1)S(1)} %add_up.7.refs_0_), channel_id=1, source_target_pairs={{0,64},{1,65},{4,68},{5,69},{8,72},{9,73},{12,76},{13,77},{2,66},{... | collective-permute-start | bytes 393224 | tf_op jit(solution)/shard_map/ppermute | solution.py:539
  31.3 1.6 %copy-done.4 = bf16[64,128,128]{2,1,0:T(8,128)(2,1)S(1)} copy-done((bf16[64,128,128]{2,1,0:T(8,128)(2,1)S(1)}, bf16[64,128,128]{2,1,0:T(8,128)(2,1)}, u32[]{:S(2)}) %copy-start.4) | copy-done | bytes 2097176
  32.9 3.9 %right_grad.2 = (bf16[8,128]{1,0:T(8,128)(2,1)}, f32[128,4096]{1,0:T(8,128)S(1)}, f32[8,128]{1,0:T(8,128)S(1)}) custom-call(bf16[64,128,128]{2,1,0:T(8,128)(2,1)S(1)} %copy-done.4, bf16[1024,128]{1,0:T(8,128)(2,1)S(1)} %bitcast.52, bf16[2048,128]{1,0:T(8,128)(2,1)S(1)} %bitcast.46, ...), custom_call_target="tpu_custom_call" | custom-call | flops 2147483648 | bytes 1048576 | tf_op jit(solution)/shard_map/right_grad/pallas_call | solution.py:163
  37.1 5.2 %right_grad.3 = (bf16[128,4096]{1,0:T(8,128)(2,1)S(1)}, f32[128,4096]{1,0:T(8,128)}, f32[8,128]{1,0:T(8,128)S(1)}) custom-call(bf16[64,128,128]{2,1,0:T(8,128)(2,1)S(1)} %copy-done.4, bf16[1024,128]{1,0:T(8,128)(2,1)S(1)} %bitcast.53, bf16[2048,128]{1,0:T(8,128)(2,1)S(1)} %bitcast.47, f32[128,4096]{1,0:T(8,128)S(1)} %get-tuple-element.22.total_in_ref, ...), custom_call_target="tpu_custom_call" | custom-call | flops 2147483648 | bytes 1048576 | tf_op jit(solution)/shard_map/right_grad/pallas_call | solution.py:163
  46.5 2.0 %collective-permute-start.15 = (bf16[16,4096]{1,0:T(8,128)(2,1)S(1)}, bf16[16,4096]{1,0:T(8,128)(2,1)S(1)}, u32[]{:S(2)}, u32[]{:S(2)}) collective-permute-start(bf16[16,4096]{1,0:T(8,128)(2,1)S(1)} %get-tuple-element.41), channel_id=1, source_target_pairs={{0,96},{1,97},{4,100},{5,101},{8,104},{9,105},{12,108},{13,109},{2... | collective-permute-start | bytes 393224 | tf_op jit(solution)/shard_map/ppermute | solution.py:539
  49.7 10.2 %left_grad.1.refs_13_.refs_4_ = bf16[4,32,2048]{2,1,0:T(8,128)(2,1)S(1)} custom-call(s32[1]{0:T(128)} %bitcast.14.turn_ref, bf16[16,4096]{1,0:T(8,128)(2,1)S(1)} %add_up.7.refs_0_, bf16[16,4096]{1,0:T(8,128)(2,1)S(1)} %collective-permute-done.2.refs_0_.refs_1_, bf16[16,4096]{1,0:T(8,128)(2,1)S(1)} %collective-permute-done.3.refs_1_.refs_2_, ...), custom_call_target="tpu_custom_call" | custom-call | flops 8589934592 | bytes 2097152 | tf_op jit(solution)/shard_map/left_grad/pallas_call | solution.py:232
  62.2 6.8 %pair_update.3 = (bf16[64,128,128]{2,1,0:T(8,128)(2,1)}, f32[1024,128]{1,0:T(8,128)S(1)}) custom-call(bf16[16,4096]{1,0:T(8,128)(2,1)S(1)} %add_up.7.refs_0_, bf16[16,4096]{1,0:T(8,128)(2,1)S(1)} %collective-permute-done.2.refs_0_.refs_1_, bf16[16,4096]{1,0:T(8,128)(2,1)S(1)} %collective-permute-done.3.refs_1_.refs_2_, ...), custom_call_target="tpu_custom_call" | custom-call | flops 6442450944 | bytes 2097152 | tf_op jit(solution)/shard_map/pair_update/pallas_call | solution.py:341
  70.5 13.2 %collective-permute-start.19 = (bf16[16,2048]{1,0:T(8,128)(2,1)S(1)}, bf16[16,2048]{1,0:T(8,128)(2,1)S(1)}, u32[]{:S(2)}, u32[]{:S(2)}) collective-permute-start(bf16[16,2048]{1,0:T(8,128)(2,1)S(1)} %get-tuple-element.52), channel_id=1, source_target_pairs={{0,3},{1,2},{4,7},{5,6},{8,11},{9,10},{12,15},{13,14},{2,1},{3,0},... | collective-permute-start | bytes 196616 | tf_op jit(solution)/shard_map/ppermute | solution.py:539
  85.1 3.7 %pair_update.4 = (bf16[64,128,128]{2,1,0:T(8,128)(2,1)}, f32[1024,128]{1,0:T(8,128)S(1)}) custom-call(bf16[16,4096]{1,0:T(8,128)(2,1)S(1)} %add_up.7.refs_0_, bf16[16,4096]{1,0:T(8,128)(2,1)S(1)} %collective-permute-done.2.refs_0_.refs_1_, bf16[16,4096]{1,0:T(8,128)(2,1)S(1)} %collective-permute-done.3.refs_1_.refs_2_, ...), custom_call_target="tpu_custom_call", output_to_operand_aliasing={{0}: (14, {})} | custom-call | flops 3221225472 | bytes 1048576 | tf_op jit(solution)/shard_map/pair_update/pallas_call | solution.py:341
  89.9 3.4 %collective-permute-start.23 = (bf16[16,64,128]{2,1,0:T(8,128)(2,1)S(1)}, bf16[16,64,128]{2,1,0:T(8,128)(2,1)S(1)}, u32[]{:S(2)}, u32[]{:S(2)}) collective-permute-start(bf16[16,64,128]{2,1,0:T(8,128)(2,1)S(1)} %pad_maximum_fusion.1.refs_13_.grads_ref.refs_0_), channel_id=1, source_target_pairs={{0,12},{1,13},{4,0},{5,1},{8,4},{9,5},{12,8},{13,9},{2,14},{3,15},... | collective-permute-start | bytes 786440 | tf_op jit(solution)/shard_map/ppermute | solution.py:539
  94.5 2.2 %projection_grad.1 = f32[64,256]{1,0:T(8,128)S(1)} custom-call(s32[2]{0:T(128)S(1)} %pad_add_fusion.3.place_ref, bf16[64,128,256]{2,1,0:T(8,128)(2,1)} %features_ref.11, f32[1,256]{1,0:T(1,128)S(1)} %bitcast.65, f32[1,256]{1,0:T(1,128)S(1)} %bitcast.71, bf16[16,64,128]{2,1,0:T(8,128)(2,1)S(1)} %pad_maximum_fusion.1.refs_13_.grads_ref.refs_0_), custom_call_target="tpu_custom_call" | custom-call | tf_op jit(solution)/shard_map/projection_grad/pallas_call | solution.py:384
  97.4 4.8 %pair_update.5 = (bf16[64,128,128]{2,1,0:T(8,128)(2,1)}, f32[1024,128]{1,0:T(8,128)S(1)}) custom-call(bf16[16,4096]{1,0:T(8,128)(2,1)S(1)} %add_up.7.refs_0_, bf16[16,4096]{1,0:T(8,128)(2,1)S(1)} %collective-permute-done.2.refs_0_.refs_1_, bf16[16,4096]{1,0:T(8,128)(2,1)S(1)} %collective-permute-done.3.refs_1_.refs_2_, ...), custom_call_target="tpu_custom_call", output_to_operand_aliasing={{0}: (14, {})} | custom-call | flops 3221225472 | bytes 1048576 | tf_op jit(solution)/shard_map/pair_update/pallas_call | solution.py:341
  102.2 3.1 %collective-permute-done.21.refs_1_.refs_0_ = bf16[16,64,128]{2,1,0:T(8,128)(2,1)S(1)} collective-permute-done((bf16[16,64,128]{2,1,0:T(8,128)(2,1)S(1)}, bf16[16,64,128]{2,1,0:T(8,128)(2,1)S(1)}, u32[]{:S(2)}, u32[]{:S(2)}) %collective-permute-start.21) | collective-permute-done | bytes 262176 | tf_op jit(solution)/shard_map/ppermute | solution.py:539
  106.1 7.9 %all-to-all-start = ((bf16[128,16,128]{2,1,0:T(8,128)(2,1)}), bf16[128,16,128]{2,1,0:T(8,128)(2,1)S(1)}, u32[]{:S(2)}, u32[]{:S(2)}) async-start(bf16[128,16,128]{2,1,0:T(8,128)(2,1)} %get-tuple-element.32), calls=%async_computation | async-start | bytes 1048576 | tf_op jit(solution)/shard_map/all_to_all | solution.py:703
  114.0 6.6 %norm_grad.2 = (bf16[64,128,256]{2,1,0:T(8,128)(2,1)}, f32[8,128]{1,0:T(8,128)S(1)}) custom-call(s32[1]{0:T(128)} %bitcast.25.first_ref, bf16[64,128,256]{2,1,0:T(8,128)(2,1)} %features_ref.11, f32[1,256]{1,0:T(1,128)S(1)} %bitcast.66, bf16[64,256]{1,0:T(8,128)(2,1)S(1)} %bitcast.57, bf16[16,64,128]{2,1,0:T(8,128)(2,1)S(1)} %pad_maximum_fusion.1.refs_13_.grads_ref.refs_0_, ...), custom_call_target="tpu_custom_call" | custom-call | flops 268435456 | bytes 4194304 | tf_op jit(solution)/shard_map/norm_grad/pallas_call | solution.py:446
  120.6 7.4 %all-to-all-done.terms_ref = bf16[128,16,128]{2,1,0:T(8,128)(2,1)S(1)} async-done(((bf16[128,16,128]{2,1,0:T(8,128)(2,1)}), bf16[128,16,128]{2,1,0:T(8,128)(2,1)S(1)}, u32[]{:S(2)}, u32[]{:S(2)}) %all-to-all-start) | async-done | bytes 524320 | tf_op jit(solution)/shard_map/all_to_all | solution.py:703
  129.0 3.8 %all-to-all-start.1 = ((bf16[128,16,128]{2,1,0:T(8,128)(2,1)}), bf16[128,16,128]{2,1,0:T(8,128)(2,1)S(1)}, u32[]{:S(2)}, u32[]{:S(2)}) async-start(bf16[128,16,128]{2,1,0:T(8,128)(2,1)} %get-tuple-element.38), calls=%async_computation.1 | async-start | bytes 1048576 | tf_op jit(solution)/shard_map/all_to_all | solution.py:715
  132.8 6.6 %norm_grad.3 = (bf16[64,128,256]{2,1,0:T(8,128)(2,1)}, f32[8,128]{1,0:T(8,128)}) custom-call(s32[1]{0:T(128)} %bitcast.21.first_ref, bf16[64,128,256]{2,1,0:T(8,128)(2,1)} %features_ref.11, f32[1,256]{1,0:T(1,128)S(1)} %bitcast.67, bf16[64,256]{1,0:T(8,128)(2,1)S(1)} %bitcast.58, ...), custom_call_target="tpu_custom_call", output_to_operand_aliasing={{0}: (7, {})} | custom-call | flops 268435456 | bytes 4194304 | tf_op jit(solution)/shard_map/norm_grad/pallas_call | solution.py:446
  140.0 7.0 %all-to-all-done.1 = bf16[128,16,128]{2,1,0:T(8,128)(2,1)S(1)} async-done(((bf16[128,16,128]{2,1,0:T(8,128)(2,1)}), bf16[128,16,128]{2,1,0:T(8,128)(2,1)S(1)}, u32[]{:S(2)}, u32[]{:S(2)}) %all-to-all-start.1) | async-done | bytes 524320 | tf_op jit(solution)/shard_map/all_to_all | solution.py:715
  (97 shorter events, 21.8 us)
Async XLA Ops:
  11.3 7.3 %collective-permute-start.1 = (bf16[64,32,64]{2,1,0:T(8,128)(2,1)S(1)}, bf16[64,32,64]{2,1,0:T(8,128)(2,1)S(1)}, u32[]{:S(2)}, u32[]{:S(2)}) collective-permute-start(bf16[64,32,64]{2,1,0:T(8,128)(2,1)S(1)} %project.5), channel_id=1, source_target_pairs={{0,1},{1,0},{4,5},{5,4},{8,9},{9,8},{12,13},{13,12},{2,3},{3,2},{6... | collective-permute-start | bytes 786440 | tf_op jit(solution)/shard_map/ppermute | solution.py:539
  12.9 7.5 %collective-permute-start = (bf16[16,4096]{1,0:T(8,128)(2,1)S(1)}, bf16[16,4096]{1,0:T(8,128)(2,1)S(1)}, u32[]{:S(2)}, u32[]{:S(2)}) collective-permute-start(bf16[16,4096]{1,0:T(8,128)(2,1)S(1)} %bitcast.82), channel_id=1, source_target_pairs={{0,0},{1,1},{4,32},{5,33},{8,64},{9,65},{12,96},{13,97},{2,16},{3,... | collective-permute-start | bytes 393224 | tf_op jit(solution)/shard_map/ppermute | solution.py:539
  20.5 16.4 %collective-permute-start.4 = (bf16[16,4096]{1,0:T(8,128)(2,1)S(1)}, bf16[16,4096]{1,0:T(8,128)(2,1)S(1)}, u32[]{:S(2)}, u32[]{:S(2)}) collective-permute-start(bf16[16,4096]{1,0:T(8,128)(2,1)S(1)} %add_up.7.refs_0_), channel_id=1, source_target_pairs={{0,32},{1,33},{4,36},{5,37},{8,40},{9,41},{12,44},{13,45},{2,34},{... | collective-permute-start | bytes 393224 | tf_op jit(solution)/shard_map/ppermute | solution.py:539
  24.3 12.8 %collective-permute-start.3 = (bf16[16,4096]{1,0:T(8,128)(2,1)S(1)}, bf16[16,4096]{1,0:T(8,128)(2,1)S(1)}, u32[]{:S(2)}, u32[]{:S(2)}) collective-permute-start(bf16[16,4096]{1,0:T(8,128)(2,1)S(1)} %add_up.7.refs_0_), channel_id=1, source_target_pairs={{0,64},{1,65},{4,68},{5,69},{8,72},{9,73},{12,76},{13,77},{2,66},{... | collective-permute-start | bytes 393224 | tf_op jit(solution)/shard_map/ppermute | solution.py:539
  31.3 5.8 %collective-permute-start.2 = (bf16[16,4096]{1,0:T(8,128)(2,1)S(1)}, bf16[16,4096]{1,0:T(8,128)(2,1)S(1)}, u32[]{:S(2)}, u32[]{:S(2)}) collective-permute-start(bf16[16,4096]{1,0:T(8,128)(2,1)S(1)} %add_up.7.refs_0_), channel_id=1, source_target_pairs={{0,96},{1,97},{4,100},{5,101},{8,104},{9,105},{12,108},{13,109},{2... | collective-permute-start | bytes 393224 | tf_op jit(solution)/shard_map/ppermute | solution.py:539
  44.9 4.7 %collective-permute-start.8 = (bf16[16,4096]{1,0:T(8,128)(2,1)S(1)}, bf16[16,4096]{1,0:T(8,128)(2,1)S(1)}, u32[]{:S(2)}, u32[]{:S(2)}) collective-permute-start(bf16[16,4096]{1,0:T(8,128)(2,1)S(1)} %collective-permute-done.4.refs_2_.refs_3_), channel_id=1, source_target_pairs={{0,1},{1,0},{4,5},{5,4},{8,9},{9,8},{12,13},{13,12},{2,3},{3,2},{6... | collective-permute-start | bytes 393224 | tf_op jit(solution)/shard_map/ppermute | solution.py:539
  45.4 4.2 %collective-permute-start.7 = (bf16[16,4096]{1,0:T(8,128)(2,1)S(1)}, bf16[16,4096]{1,0:T(8,128)(2,1)S(1)}, u32[]{:S(2)}, u32[]{:S(2)}) collective-permute-start(bf16[16,4096]{1,0:T(8,128)(2,1)S(1)} %collective-permute-done.3.refs_1_.refs_2_), channel_id=1, source_target_pairs={{0,1},{1,0},{4,5},{5,4},{8,9},{9,8},{12,13},{13,12},{2,3},{3,2},{6... | collective-permute-start | bytes 393224 | tf_op jit(solution)/shard_map/ppermute | solution.py:539
  45.5 4.1 %collective-permute-start.6 = (bf16[16,4096]{1,0:T(8,128)(2,1)S(1)}, bf16[16,4096]{1,0:T(8,128)(2,1)S(1)}, u32[]{:S(2)}, u32[]{:S(2)}) collective-permute-start(bf16[16,4096]{1,0:T(8,128)(2,1)S(1)} %collective-permute-done.2.refs_0_.refs_1_), channel_id=1, source_target_pairs={{0,1},{1,0},{4,5},{5,4},{8,9},{9,8},{12,13},{13,12},{2,3},{3,2},{6... | collective-permute-start | bytes 393224 | tf_op jit(solution)/shard_map/ppermute | solution.py:539
  46.5 14.3 %collective-permute-start.15 = (bf16[16,4096]{1,0:T(8,128)(2,1)S(1)}, bf16[16,4096]{1,0:T(8,128)(2,1)S(1)}, u32[]{:S(2)}, u32[]{:S(2)}) collective-permute-start(bf16[16,4096]{1,0:T(8,128)(2,1)S(1)} %get-tuple-element.41), channel_id=1, source_target_pairs={{0,96},{1,97},{4,100},{5,101},{8,104},{9,105},{12,108},{13,109},{2... | collective-permute-start | bytes 393224 | tf_op jit(solution)/shard_map/ppermute | solution.py:539
  48.5 12.9 %collective-permute-start.14 = (bf16[16,4096]{1,0:T(8,128)(2,1)S(1)}, bf16[16,4096]{1,0:T(8,128)(2,1)S(1)}, u32[]{:S(2)}, u32[]{:S(2)}) collective-permute-start(bf16[16,4096]{1,0:T(8,128)(2,1)S(1)} %get-tuple-element.42), channel_id=1, source_target_pairs={{0,64},{1,65},{4,68},{5,69},{8,72},{9,73},{12,76},{13,77},{2,66},{... | collective-permute-start | bytes 393224 | tf_op jit(solution)/shard_map/ppermute | solution.py:539
  49.6 11.8 %collective-permute-start.13 = (bf16[16,4096]{1,0:T(8,128)(2,1)S(1)}, bf16[16,4096]{1,0:T(8,128)(2,1)S(1)}, u32[]{:S(2)}, u32[]{:S(2)}) collective-permute-start(bf16[16,4096]{1,0:T(8,128)(2,1)S(1)} %get-tuple-element.43), channel_id=1, source_target_pairs={{0,32},{1,33},{4,36},{5,37},{8,40},{9,41},{12,44},{13,45},{2,34},{... | collective-permute-start | bytes 393224 | tf_op jit(solution)/shard_map/ppermute | solution.py:539
  59.9 9.2 %collective-permute-start.12 = (bf16[32,2048]{1,0:T(8,128)(2,1)S(1)}, bf16[32,2048]{1,0:T(8,128)(2,1)S(1)}, u32[]{:S(2)}, u32[]{:S(2)}) collective-permute-start(bf16[32,2048]{1,0:T(8,128)(2,1)S(1)} %get-tuple-element.45), channel_id=1, source_target_pairs={{0,12},{1,13},{4,0},{5,1},{8,4},{9,5},{12,8},{13,9},{2,14},{3,15},... | collective-permute-start | bytes 393224 | tf_op jit(solution)/shard_map/ppermute | solution.py:539
  60.6 8.4 %collective-permute-start.11 = (bf16[32,2048]{1,0:T(8,128)(2,1)S(1)}, bf16[32,2048]{1,0:T(8,128)(2,1)S(1)}, u32[]{:S(2)}, u32[]{:S(2)}) collective-permute-start(bf16[32,2048]{1,0:T(8,128)(2,1)S(1)} %get-tuple-element.46), channel_id=1, source_target_pairs={{0,8},{1,9},{4,12},{5,13},{8,0},{9,1},{12,4},{13,5},{2,10},{3,11},... | collective-permute-start | bytes 393224 | tf_op jit(solution)/shard_map/ppermute | solution.py:539
  60.8 9.5 %collective-permute-start.10 = (bf16[32,2048]{1,0:T(8,128)(2,1)S(1)}, bf16[32,2048]{1,0:T(8,128)(2,1)S(1)}, u32[]{:S(2)}, u32[]{:S(2)}) collective-permute-start(bf16[32,2048]{1,0:T(8,128)(2,1)S(1)} %get-tuple-element.47), channel_id=1, source_target_pairs={{0,4},{1,5},{4,8},{5,9},{8,12},{9,13},{12,0},{13,1},{2,6},{3,7},{6... | collective-permute-start | bytes 393224 | tf_op jit(solution)/shard_map/ppermute | solution.py:539
  61.5 8.9 %collective-permute-start.16 = (bf16[16,4096]{1,0:T(8,128)(2,1)S(1)}, bf16[16,4096]{1,0:T(8,128)(2,1)S(1)}, u32[]{:S(2)}, u32[]{:S(2)}) collective-permute-start(bf16[16,4096]{1,0:T(8,128)(2,1)S(1)} %add_up.9), channel_id=1, source_target_pairs={{0,0},{1,1},{4,32},{5,33},{8,64},{9,65},{12,96},{13,97},{2,16},{3,... | collective-permute-start | bytes 393224 | tf_op jit(solution)/shard_map/ppermute | solution.py:539
  70.5 18.4 %collective-permute-start.19 = (bf16[16,2048]{1,0:T(8,128)(2,1)S(1)}, bf16[16,2048]{1,0:T(8,128)(2,1)S(1)}, u32[]{:S(2)}, u32[]{:S(2)}) collective-permute-start(bf16[16,2048]{1,0:T(8,128)(2,1)S(1)} %get-tuple-element.52), channel_id=1, source_target_pairs={{0,3},{1,2},{4,7},{5,6},{8,11},{9,10},{12,15},{13,14},{2,1},{3,0},... | collective-permute-start | bytes 196616 | tf_op jit(solution)/shard_map/ppermute | solution.py:539
  83.6 5.3 %collective-permute-start.18 = (bf16[16,2048]{1,0:T(8,128)(2,1)S(1)}, bf16[16,2048]{1,0:T(8,128)(2,1)S(1)}, u32[]{:S(2)}, u32[]{:S(2)}) collective-permute-start(bf16[16,2048]{1,0:T(8,128)(2,1)S(1)} %get-tuple-element.52), channel_id=1, source_target_pairs={{0,1},{1,0},{4,5},{5,4},{8,9},{9,8},{12,13},{13,12},{2,3},{3,2},{6... | collective-permute-start | bytes 196616 | tf_op jit(solution)/shard_map/ppermute | solution.py:539
  83.6 5.2 %collective-permute-start.17 = (bf16[16,2048]{1,0:T(8,128)(2,1)S(1)}, bf16[16,2048]{1,0:T(8,128)(2,1)S(1)}, u32[]{:S(2)}, u32[]{:S(2)}) collective-permute-start(bf16[16,2048]{1,0:T(8,128)(2,1)S(1)} %get-tuple-element.51.refs_0_), channel_id=1, source_target_pairs={{0,2},{1,3},{4,6},{5,7},{8,10},{9,11},{12,14},{13,15},{2,0},{3,1},... | collective-permute-start | bytes 196616 | tf_op jit(solution)/shard_map/ppermute | solution.py:539
  83.9 5.8 %collective-permute-start.20 = (bf16[16,4096]{1,0:T(8,128)(2,1)S(1)}, bf16[16,4096]{1,0:T(8,128)(2,1)S(1)}, u32[]{:S(2)}, u32[]{:S(2)}) collective-permute-start(bf16[16,4096]{1,0:T(8,128)(2,1)S(1)} %collective-permute-done.16.refs_5_.refs_0_), channel_id=1, source_target_pairs={{0,2},{1,3},{4,6},{5,7},{8,10},{9,11},{12,14},{13,15},{2,0},{3,1},... | collective-permute-start | bytes 393224 | tf_op jit(solution)/shard_map/ppermute | solution.py:539
  89.9 12.3 %collective-permute-start.23 = (bf16[16,64,128]{2,1,0:T(8,128)(2,1)S(1)}, bf16[16,64,128]{2,1,0:T(8,128)(2,1)S(1)}, u32[]{:S(2)}, u32[]{:S(2)}) collective-permute-start(bf16[16,64,128]{2,1,0:T(8,128)(2,1)S(1)} %pad_maximum_fusion.1.refs_13_.grads_ref.refs_0_), channel_id=1, source_target_pairs={{0,12},{1,13},{4,0},{5,1},{8,4},{9,5},{12,8},{13,9},{2,14},{3,15},... | collective-permute-start | bytes 786440 | tf_op jit(solution)/shard_map/ppermute | solution.py:539
  93.3 8.9 %collective-permute-start.22 = (bf16[16,64,128]{2,1,0:T(8,128)(2,1)S(1)}, bf16[16,64,128]{2,1,0:T(8,128)(2,1)S(1)}, u32[]{:S(2)}, u32[]{:S(2)}) collective-permute-start(bf16[16,64,128]{2,1,0:T(8,128)(2,1)S(1)} %pad_maximum_fusion.1.refs_13_.grads_ref.refs_0_), channel_id=1, source_target_pairs={{0,4},{1,5},{4,8},{5,9},{8,12},{9,13},{12,0},{13,1},{2,6},{3,7},{6... | collective-permute-start | bytes 786440 | tf_op jit(solution)/shard_map/ppermute | solution.py:539
  93.3 12.0 %collective-permute-start.21 = (bf16[16,64,128]{2,1,0:T(8,128)(2,1)S(1)}, bf16[16,64,128]{2,1,0:T(8,128)(2,1)S(1)}, u32[]{:S(2)}, u32[]{:S(2)}) collective-permute-start(bf16[16,64,128]{2,1,0:T(8,128)(2,1)S(1)} %pad_maximum_fusion.1.refs_13_.grads_ref.refs_0_), channel_id=1, source_target_pairs={{0,8},{1,9},{4,12},{5,13},{8,0},{9,1},{12,4},{13,5},{2,10},{3,11},... | collective-permute-start | bytes 786440 | tf_op jit(solution)/shard_map/ppermute | solution.py:539
  106.1 21.9 %all-to-all-start = ((bf16[128,16,128]{2,1,0:T(8,128)(2,1)}), bf16[128,16,128]{2,1,0:T(8,128)(2,1)S(1)}, u32[]{:S(2)}, u32[]{:S(2)}) async-start(bf16[128,16,128]{2,1,0:T(8,128)(2,1)} %get-tuple-element.32), calls=%async_computation | async-start | bytes 1048576 | tf_op jit(solution)/shard_map/all_to_all | solution.py:703
  129.0 18.0 %all-to-all-start.1 = ((bf16[128,16,128]{2,1,0:T(8,128)(2,1)}), bf16[128,16,128]{2,1,0:T(8,128)(2,1)S(1)}, u32[]{:S(2)}, u32[]{:S(2)}) async-start(bf16[128,16,128]{2,1,0:T(8,128)(2,1)} %get-tuple-element.38), calls=%async_computation.1 | async-start | bytes 1048576 | tf_op jit(solution)/shard_map/all_to_all | solution.py:715
  (11 other events, 48.9 us)

commit v6 on v5

--- a/solution.py
+++ b/solution.py
@@ -70,14 +70,14 @@
             for r in range(0, residues, 64)
         ]
         normed = jnp.concatenate(normed, axis=0)
-        several = dot(normed, weight_ref[...], ((1,), (0,))).T.astype(BF16)
+        several = dot(weight_ref[...], normed, ((1,), (1,))).astype(BF16)
         for n in range(at_once):
             out_ref[s + n] = several[:, n * residues : (n + 1) * residues]
 
 
 def project(first, count, part, residues, features, gain, offset, weight, after=()):
     total, _, channels = features.shape
-    width = weight.shape[1]
+    width = weight.shape[0]
     seqs = min(2048 // residues, 16)
     steps = total // seqs
 
@@ -93,7 +93,7 @@
                 pl.BlockSpec((seqs, residues, channels), place),
                 whole((1, channels)),
                 whole((1, channels)),
-                whole((channels, width)),
+                whole((width, channels)),
             ]
             + [ANYWHERE] * len(after),
             out_specs=pl.BlockSpec((seqs, width, residues), lambda n, place_ref: (n, 0, 0)),
@@ -597,7 +597,7 @@
         features,
         pltpu.with_memory_space_constraint(gain_row, pltpu.HBM),
         pltpu.with_memory_space_constraint(offset_row, pltpu.HBM),
-        projection_weight[:, width:],
+        weight_rows[width:],
     )
     arrived = transpose_xz(right_piece.reshape(quarter, width * residues))
 
@@ -610,7 +610,7 @@
             alignment_features,
             gain_row,
             offset_row,
-            projection_weight[:, :width],
+            weight_rows[:width],
             after=(right_piece,),
         )
 
@@ -669,7 +669,7 @@
         )
 
     pair = pair_part(0, blocks // 2, None, (left_partial,))
-    left_sum = add_up([left_partial[0], *left_came], after=(pair[1], right_sum))
+    left_sum = add_up([left_partial[0], *left_came], after=(pair[1],))
 
     left_own, left_other = left_sum[:quarter], left_sum[quarter:]
     own_beside, right_beside = swap_low_y(left_own), swap_low_y(right_sum)

time: 149 us -> 151 us (1.013)
  starting transfers between devices: 51.8 us -> 58.5 us
  Pallas kernels: 66.6 us -> 62.1 us
    pallas_call x3, Pallas kernels: 14.4 us -> 9.9 us  [project(): pl.pallas_call(project_kernel, grid_spec=pltpu.PrefetchScalarGridSpec(num...]
    all_to_all x1, starting transfers between devices: 7.88 us -> 11.4 us  [body(): came = lax.all_to_all(terms, AXES, 0, 0, tiled=True)]
    ppermute x24, starting transfers between devices: 40.1 us -> 43.3 us  [torus_permute(): return lax.ppermute(value, AXES, pairs)]
  transfers between devices with their start and end apart: 26 -> 26, of which waited for: 6 -> 7; matrix products, arithmetic and copies ran while one was open for 2% -> 2% of each run, Pallas kernels for 34% -> 32%
where the time goes in v6:
time: 151 us; the launch traced here: 150 us
  Pallas kernels  62.1 us (41%)
  starting transfers between devices  58.5 us (39%)
  waiting for transfers between devices  18.8 us (12%)
  local copies, waits for them, and re-layouts  8.47 us (6%)
    ppermute x24, starting transfers between devices, torus_permute(): return lax.ppermute(value, AXES, pairs)  43.3 us
    pallas_call x3, Pallas kernels, pair_and_weight_grad(): pl.pallas_call(functools.partial(pair_kernel, fresh), grid=(count,), in_s...  15.3 us
    pallas_call x2, Pallas kernels, norm_grad(): pl.pallas_call(functools.partial(norm_grad_kernel, len(pieces)), grid_spe...  13.3 us
    all_to_all x1, starting transfers between devices, body(): came = lax.all_to_all(terms, AXES, 0, 0, tiled=True)  11.4 us
    pallas_call x1, Pallas kernels, left_grad_part(): pl.pallas_call(left_grad_kernel, grid_spec=pltpu.PrefetchScalarGridSpec(n...  10.2 us
    pallas_call x3, Pallas kernels, project(): pl.pallas_call(project_kernel, grid_spec=pltpu.PrefetchScalarGridSpec(num...  9.9 us
    pallas_call x2, Pallas kernels, right_grad_part(): pl.pallas_call(functools.partial(right_grad_kernel, fresh), grid=(count,)...  9.09 us
    all_to_all x1, waiting for transfers between devices, body(): came = lax.all_to_all(terms, AXES, 0, 0, tiled=True)  7.36 us
  transfers between devices with their start and end apart: 26, of which 7 were waited for; matrix products, arithmetic and copies ran while one was open for 2% of the time, Pallas kernels for 32%

profile of v6, /device:TPU:1, one launch (start us, length us, event | category | flops | bytes accessed | tf_op | source)
XLA Modules:
  0.0 150.1 jit_solution(12920929685634810911)
XLA Ops:
  1.6 3.1 %project.3.refs_0_ = bf16[16,32,128]{2,1,0:T(8,128)(2,1)S(1)} custom-call(s32[2]{0:T(128)S(1)} %pad_add_fusion.place_ref, bf16[64,128,256]{2,1,0:T(8,128)(2,1)} %features_ref.11, f32[1,256]{1,0:T(1,128)} %bitcast.63, f32[1,256]{1,0:T(1,128)} %bitcast.69, bf16[32,256]{1,0:T(8,128)(2,1)S(1)} %get-tuple-element.54.weight_ref), custom_call_target="tpu_custom_call" | custom-call | flops 67108864 | bytes 1179648 | tf_op jit(solution)/shard_map/project/pallas_call | solution.py:87
  4.7 3.4 %project.5 = bf16[64,32,64]{2,1,0:T(8,128)(2,1)S(1)} custom-call(s32[2]{0:T(128)S(1)} %get-tuple-element.56.place_ref, bf16[64,128,256]{2,1,0:T(8,128)(2,1)S(1)} %copy-done, f32[1,256]{1,0:T(1,128)S(1)} %bitcast.64, f32[1,256]{1,0:T(1,128)S(1)} %bitcast.70, bf16[32,256]{1,0:T(8,128)(2,1)S(1)} %get-tuple-element.53.weight_ref, ...), custom_call_target="tpu_custom_call" | custom-call | flops 134217728 | bytes 2359296 | tf_op jit(solution)/shard_map/project/pallas_call | solution.py:87
  10.4 3.4 %project.4 = bf16[64,32,64]{2,1,0:T(8,128)(2,1)S(1)} custom-call(s32[2]{0:T(128)S(1)} %get-tuple-element.55.place_ref, bf16[64,128,256]{2,1,0:T(8,128)(2,1)S(1)} %copy-done, f32[1,256]{1,0:T(1,128)S(1)} %bitcast.65, f32[1,256]{1,0:T(1,128)S(1)} %bitcast.71, bf16[32,256]{1,0:T(8,128)(2,1)S(1)} %get-tuple-element.53.weight_ref, ...), custom_call_target="tpu_custom_call" | custom-call | flops 134217728 | bytes 2359296 | tf_op jit(solution)/shard_map/project/pallas_call | solution.py:87
  15.7 3.8 %collective-permute-start.4 = (bf16[16,4096]{1,0:T(8,128)(2,1)S(1)}, bf16[16,4096]{1,0:T(8,128)(2,1)S(1)}, u32[]{:S(2)}, u32[]{:S(2)}) collective-permute-start(bf16[16,4096]{1,0:T(8,128)(2,1)S(1)} %add_up.7.refs_0_), channel_id=1, source_target_pairs={{0,32},{1,33},{4,36},{5,37},{8,40},{9,41},{12,44},{13,45},{2,34},{... | collective-permute-start | bytes 393224 | tf_op jit(solution)/shard_map/ppermute | solution.py:539
  19.5 8.6 %collective-permute-start.3 = (bf16[16,4096]{1,0:T(8,128)(2,1)S(1)}, bf16[16,4096]{1,0:T(8,128)(2,1)S(1)}, u32[]{:S(2)}, u32[]{:S(2)}) collective-permute-start(bf16[16,4096]{1,0:T(8,128)(2,1)S(1)} %add_up.7.refs_0_), channel_id=1, source_target_pairs={{0,64},{1,65},{4,68},{5,69},{8,72},{9,73},{12,76},{13,77},{2,66},{... | collective-permute-start | bytes 393224 | tf_op jit(solution)/shard_map/ppermute | solution.py:539
  28.1 1.6 %copy-done.4 = bf16[64,128,128]{2,1,0:T(8,128)(2,1)S(1)} copy-done((bf16[64,128,128]{2,1,0:T(8,128)(2,1)S(1)}, bf16[64,128,128]{2,1,0:T(8,128)(2,1)}, u32[]{:S(2)}) %copy-start.4) | copy-done | bytes 2097176
  29.7 3.9 %right_grad.2 = (bf16[8,128]{1,0:T(8,128)(2,1)}, f32[128,4096]{1,0:T(8,128)S(1)}, f32[8,128]{1,0:T(8,128)S(1)}) custom-call(bf16[64,128,128]{2,1,0:T(8,128)(2,1)S(1)} %copy-done.4, bf16[1024,128]{1,0:T(8,128)(2,1)S(1)} %bitcast.52, bf16[2048,128]{1,0:T(8,128)(2,1)S(1)} %bitcast.46, ...), custom_call_target="tpu_custom_call" | custom-call | flops 2147483648 | bytes 1048576 | tf_op jit(solution)/shard_map/right_grad/pallas_call | solution.py:163
  33.8 5.2 %right_grad.3 = (bf16[128,4096]{1,0:T(8,128)(2,1)S(1)}, f32[128,4096]{1,0:T(8,128)}, f32[8,128]{1,0:T(8,128)S(1)}) custom-call(bf16[64,128,128]{2,1,0:T(8,128)(2,1)S(1)} %copy-done.4, bf16[1024,128]{1,0:T(8,128)(2,1)S(1)} %bitcast.53, bf16[2048,128]{1,0:T(8,128)(2,1)S(1)} %bitcast.47, f32[128,4096]{1,0:T(8,128)S(1)} %get-tuple-element.22.total_in_ref, ...), custom_call_target="tpu_custom_call" | custom-call | flops 2147483648 | bytes 1048576 | tf_op jit(solution)/shard_map/right_grad/pallas_call | solution.py:163
  43.3 1.9 %collective-permute-start.18 = (bf16[16,4096]{1,0:T(8,128)(2,1)S(1)}, bf16[16,4096]{1,0:T(8,128)(2,1)S(1)}, u32[]{:S(2)}, u32[]{:S(2)}) collective-permute-start(bf16[16,4096]{1,0:T(8,128)(2,1)S(1)} %get-tuple-element.41), channel_id=1, source_target_pairs={{0,96},{1,97},{4,100},{5,101},{8,104},{9,105},{12,108},{13,109},{2... | collective-permute-start | bytes 393224 | tf_op jit(solution)/shard_map/ppermute | solution.py:539
  46.4 10.2 %left_grad.1.refs_13_.refs_4_ = bf16[4,32,2048]{2,1,0:T(8,128)(2,1)S(1)} custom-call(s32[1]{0:T(128)} %bitcast.15.turn_ref, bf16[16,4096]{1,0:T(8,128)(2,1)S(1)} %add_up.7.refs_0_, bf16[16,4096]{1,0:T(8,128)(2,1)S(1)} %collective-permute-done.2.refs_0_.refs_1_, bf16[16,4096]{1,0:T(8,128)(2,1)S(1)} %collective-permute-done.3.refs_1_.refs_2_, ...), custom_call_target="tpu_custom_call" | custom-call | flops 8589934592 | bytes 2097152 | tf_op jit(solution)/shard_map/left_grad/pallas_call | solution.py:232
  58.2 6.8 %pair_update.3 = (bf16[64,128,128]{2,1,0:T(8,128)(2,1)}, f32[1024,128]{1,0:T(8,128)S(1)}) custom-call(bf16[16,4096]{1,0:T(8,128)(2,1)S(1)} %add_up.7.refs_0_, bf16[16,4096]{1,0:T(8,128)(2,1)S(1)} %collective-permute-done.2.refs_0_.refs_1_, bf16[16,4096]{1,0:T(8,128)(2,1)S(1)} %collective-permute-done.3.refs_1_.refs_2_, ...), custom_call_target="tpu_custom_call" | custom-call | flops 6442450944 | bytes 2097152 | tf_op jit(solution)/shard_map/pair_update/pallas_call | solution.py:341
  66.4 6.3 %collective-permute-start.15 = (bf16[16,2048]{1,0:T(8,128)(2,1)S(1)}, bf16[16,2048]{1,0:T(8,128)(2,1)S(1)}, u32[]{:S(2)}, u32[]{:S(2)}) collective-permute-start(bf16[16,2048]{1,0:T(8,128)(2,1)S(1)} %get-tuple-element.52), channel_id=1, source_target_pairs={{0,3},{1,2},{4,7},{5,6},{8,11},{9,10},{12,15},{13,14},{2,1},{3,0},... | collective-permute-start | bytes 196616 | tf_op jit(solution)/shard_map/ppermute | solution.py:539
  73.5 5.1 %collective-permute-start.13 = (bf16[16,2048]{1,0:T(8,128)(2,1)S(1)}, bf16[16,2048]{1,0:T(8,128)(2,1)S(1)}, u32[]{:S(2)}, u32[]{:S(2)}) collective-permute-start(bf16[16,2048]{1,0:T(8,128)(2,1)S(1)} %get-tuple-element.51.refs_0_), channel_id=1, source_target_pairs={{0,2},{1,3},{4,6},{5,7},{8,10},{9,11},{12,14},{13,15},{2,0},{3,1},... | collective-permute-start | bytes 196616 | tf_op jit(solution)/shard_map/ppermute | solution.py:539
  78.7 3.7 %pair_update.4 = (bf16[64,128,128]{2,1,0:T(8,128)(2,1)}, f32[1024,128]{1,0:T(8,128)S(1)}) custom-call(bf16[16,4096]{1,0:T(8,128)(2,1)S(1)} %add_up.7.refs_0_, bf16[16,4096]{1,0:T(8,128)(2,1)S(1)} %collective-permute-done.2.refs_0_.refs_1_, bf16[16,4096]{1,0:T(8,128)(2,1)S(1)} %collective-permute-done.3.refs_1_.refs_2_, ...), custom_call_target="tpu_custom_call", output_to_operand_aliasing={{0}: (14, {})} | custom-call | flops 3221225472 | bytes 1048576 | tf_op jit(solution)/shard_map/pair_update/pallas_call | solution.py:341
  82.5 6.5 %collective-permute-start.20 = (bf16[16,4096]{1,0:T(8,128)(2,1)S(1)}, bf16[16,4096]{1,0:T(8,128)(2,1)S(1)}, u32[]{:S(2)}, u32[]{:S(2)}) collective-permute-start(bf16[16,4096]{1,0:T(8,128)(2,1)S(1)} %collective-permute-done.19.refs_0_), channel_id=1, source_target_pairs={{0,2},{1,3},{4,6},{5,7},{8,10},{9,11},{12,14},{13,15},{2,0},{3,1},... | collective-permute-start | bytes 393224 | tf_op jit(solution)/shard_map/ppermute | solution.py:539
  89.7 1.6 %collective-permute-done.20.refs_1_ = bf16[16,4096]{1,0:T(8,128)(2,1)S(1)} collective-permute-done((bf16[16,4096]{1,0:T(8,128)(2,1)S(1)}, bf16[16,4096]{1,0:T(8,128)(2,1)S(1)}, u32[]{:S(2)}, u32[]{:S(2)}) %collective-permute-start.20) | collective-permute-done | bytes 131104 | tf_op jit(solution)/shard_map/ppermute | solution.py:539
  94.5 2.2 %projection_grad.1 = f32[64,256]{1,0:T(8,128)S(1)} custom-call(s32[2]{0:T(128)S(1)} %pad_add_fusion.3.place_ref, bf16[64,128,256]{2,1,0:T(8,128)(2,1)} %features_ref.11, f32[1,256]{1,0:T(1,128)S(1)} %bitcast.66, f32[1,256]{1,0:T(1,128)S(1)} %bitcast.72, bf16[16,64,128]{2,1,0:T(8,128)(2,1)S(1)} %pad_maximum_fusion.1.refs_13_.grads_ref.refs_0_), custom_call_target="tpu_custom_call" | custom-call | tf_op jit(solution)/shard_map/projection_grad/pallas_call | solution.py:384
  97.4 4.8 %pair_update.5 = (bf16[64,128,128]{2,1,0:T(8,128)(2,1)}, f32[1024,128]{1,0:T(8,128)S(1)}) custom-call(bf16[16,4096]{1,0:T(8,128)(2,1)S(1)} %add_up.7.refs_0_, bf16[16,4096]{1,0:T(8,128)(2,1)S(1)} %collective-permute-done.2.refs_0_.refs_1_, bf16[16,4096]{1,0:T(8,128)(2,1)S(1)} %collective-permute-done.3.refs_1_.refs_2_, ...), custom_call_target="tpu_custom_call", output_to_operand_aliasing={{0}: (14, {})} | custom-call | flops 3221225472 | bytes 1048576 | tf_op jit(solution)/shard_map/pair_update/pallas_call | solution.py:341
  103.7 11.4 %all-to-all-start = ((bf16[128,16,128]{2,1,0:T(8,128)(2,1)}), bf16[128,16,128]{2,1,0:T(8,128)(2,1)S(1)}, u32[]{:S(2)}, u32[]{:S(2)}) async-start(bf16[128,16,128]{2,1,0:T(8,128)(2,1)} %get-tuple-element.32), calls=%async_computation | async-start | bytes 1048576 | tf_op jit(solution)/shard_map/all_to_all | solution.py:703
  115.1 6.6 %norm_grad.2 = (bf16[64,128,256]{2,1,0:T(8,128)(2,1)}, f32[8,128]{1,0:T(8,128)S(1)}) custom-call(s32[1]{0:T(128)} %bitcast.25.first_ref, bf16[64,128,256]{2,1,0:T(8,128)(2,1)} %features_ref.11, f32[1,256]{1,0:T(1,128)S(1)} %bitcast.67, bf16[64,256]{1,0:T(8,128)(2,1)S(1)} %bitcast.58, bf16[16,64,128]{2,1,0:T(8,128)(2,1)S(1)} %pad_maximum_fusion.1.refs_13_.grads_ref.refs_0_, ...), custom_call_target="tpu_custom_call" | custom-call | flops 268435456 | bytes 4194304 | tf_op jit(solution)/shard_map/norm_grad/pallas_call | solution.py:446
  121.8 7.4 %all-to-all-done.terms_ref = bf16[128,16,128]{2,1,0:T(8,128)(2,1)S(1)} async-done(((bf16[128,16,128]{2,1,0:T(8,128)(2,1)}), bf16[128,16,128]{2,1,0:T(8,128)(2,1)S(1)}, u32[]{:S(2)}, u32[]{:S(2)}) %all-to-all-start) | async-done | bytes 524320 | tf_op jit(solution)/shard_map/all_to_all | solution.py:703
  130.1 3.8 %all-to-all-start.1 = ((bf16[128,16,128]{2,1,0:T(8,128)(2,1)}), bf16[128,16,128]{2,1,0:T(8,128)(2,1)S(1)}, u32[]{:S(2)}, u32[]{:S(2)}) async-start(bf16[128,16,128]{2,1,0:T(8,128)(2,1)} %get-tuple-element.38), calls=%async_computation.1 | async-start | bytes 1048576 | tf_op jit(solution)/shard_map/all_to_all | solution.py:715
  133.9 6.6 %norm_grad.3 = (bf16[64,128,256]{2,1,0:T(8,128)(2,1)}, f32[8,128]{1,0:T(8,128)}) custom-call(s32[1]{0:T(128)} %bitcast.22.first_ref, bf16[64,128,256]{2,1,0:T(8,128)(2,1)} %features_ref.11, f32[1,256]{1,0:T(1,128)S(1)} %bitcast.68, bf16[64,256]{1,0:T(8,128)(2,1)S(1)} %bitcast.59, ...), custom_call_target="tpu_custom_call", output_to_operand_aliasing={{0}: (7, {})} | custom-call | flops 268435456 | bytes 4194304 | tf_op jit(solution)/shard_map/norm_grad/pallas_call | solution.py:446
  141.1 7.0 %all-to-all-done.1 = bf16[128,16,128]{2,1,0:T(8,128)(2,1)S(1)} async-done(((bf16[128,16,128]{2,1,0:T(8,128)(2,1)}), bf16[128,16,128]{2,1,0:T(8,128)(2,1)S(1)}, u32[]{:S(2)}, u32[]{:S(2)}) %all-to-all-start.1) | async-done | bytes 524320 | tf_op jit(solution)/shard_map/all_to_all | solution.py:715
  (95 shorter events, 24.1 us)
Async XLA Ops:
  8.1 5.8 %collective-permute-start.1 = (bf16[64,32,64]{2,1,0:T(8,128)(2,1)S(1)}, bf16[64,32,64]{2,1,0:T(8,128)(2,1)S(1)}, u32[]{:S(2)}, u32[]{:S(2)}) collective-permute-start(bf16[64,32,64]{2,1,0:T(8,128)(2,1)S(1)} %project.5), channel_id=1, source_target_pairs={{0,1},{1,0},{4,5},{5,4},{8,9},{9,8},{12,13},{13,12},{2,3},{3,2},{6... | collective-permute-start | bytes 786440 | tf_op jit(solution)/shard_map/ppermute | solution.py:539
  9.7 6.0 %collective-permute-start = (bf16[16,4096]{1,0:T(8,128)(2,1)S(1)}, bf16[16,4096]{1,0:T(8,128)(2,1)S(1)}, u32[]{:S(2)}, u32[]{:S(2)}) collective-permute-start(bf16[16,4096]{1,0:T(8,128)(2,1)S(1)} %bitcast.83), channel_id=1, source_target_pairs={{0,0},{1,1},{4,32},{5,33},{8,64},{9,65},{12,96},{13,97},{2,16},{3,... | collective-permute-start | bytes 393224 | tf_op jit(solution)/shard_map/ppermute | solution.py:539
  15.7 17.9 %collective-permute-start.4 = (bf16[16,4096]{1,0:T(8,128)(2,1)S(1)}, bf16[16,4096]{1,0:T(8,128)(2,1)S(1)}, u32[]{:S(2)}, u32[]{:S(2)}) collective-permute-start(bf16[16,4096]{1,0:T(8,128)(2,1)S(1)} %add_up.7.refs_0_), channel_id=1, source_target_pairs={{0,32},{1,33},{4,36},{5,37},{8,40},{9,41},{12,44},{13,45},{2,34},{... | collective-permute-start | bytes 393224 | tf_op jit(solution)/shard_map/ppermute | solution.py:539
  19.5 14.3 %collective-permute-start.3 = (bf16[16,4096]{1,0:T(8,128)(2,1)S(1)}, bf16[16,4096]{1,0:T(8,128)(2,1)S(1)}, u32[]{:S(2)}, u32[]{:S(2)}) collective-permute-start(bf16[16,4096]{1,0:T(8,128)(2,1)S(1)} %add_up.7.refs_0_), channel_id=1, source_target_pairs={{0,64},{1,65},{4,68},{5,69},{8,72},{9,73},{12,76},{13,77},{2,66},{... | collective-permute-start | bytes 393224 | tf_op jit(solution)/shard_map/ppermute | solution.py:539
  28.1 5.8 %collective-permute-start.2 = (bf16[16,4096]{1,0:T(8,128)(2,1)S(1)}, bf16[16,4096]{1,0:T(8,128)(2,1)S(1)}, u32[]{:S(2)}, u32[]{:S(2)}) collective-permute-start(bf16[16,4096]{1,0:T(8,128)(2,1)S(1)} %add_up.7.refs_0_), channel_id=1, source_target_pairs={{0,96},{1,97},{4,100},{5,101},{8,104},{9,105},{12,108},{13,109},{2... | collective-permute-start | bytes 393224 | tf_op jit(solution)/shard_map/ppermute | solution.py:539
  41.7 4.7 %collective-permute-start.8 = (bf16[16,4096]{1,0:T(8,128)(2,1)S(1)}, bf16[16,4096]{1,0:T(8,128)(2,1)S(1)}, u32[]{:S(2)}, u32[]{:S(2)}) collective-permute-start(bf16[16,4096]{1,0:T(8,128)(2,1)S(1)} %collective-permute-done.4.refs_2_.refs_3_), channel_id=1, source_target_pairs={{0,1},{1,0},{4,5},{5,4},{8,9},{9,8},{12,13},{13,12},{2,3},{3,2},{6... | collective-permute-start | bytes 393224 | tf_op jit(solution)/shard_map/ppermute | solution.py:539
  42.2 4.2 %collective-permute-start.7 = (bf16[16,4096]{1,0:T(8,128)(2,1)S(1)}, bf16[16,4096]{1,0:T(8,128)(2,1)S(1)}, u32[]{:S(2)}, u32[]{:S(2)}) collective-permute-start(bf16[16,4096]{1,0:T(8,128)(2,1)S(1)} %collective-permute-done.3.refs_1_.refs_2_), channel_id=1, source_target_pairs={{0,1},{1,0},{4,5},{5,4},{8,9},{9,8},{12,13},{13,12},{2,3},{3,2},{6... | collective-permute-start | bytes 393224 | tf_op jit(solution)/shard_map/ppermute | solution.py:539
  42.3 4.1 %collective-permute-start.6 = (bf16[16,4096]{1,0:T(8,128)(2,1)S(1)}, bf16[16,4096]{1,0:T(8,128)(2,1)S(1)}, u32[]{:S(2)}, u32[]{:S(2)}) collective-permute-start(bf16[16,4096]{1,0:T(8,128)(2,1)S(1)} %collective-permute-done.2.refs_0_.refs_1_), channel_id=1, source_target_pairs={{0,1},{1,0},{4,5},{5,4},{8,9},{9,8},{12,13},{13,12},{2,3},{3,2},{6... | collective-permute-start | bytes 393224 | tf_op jit(solution)/shard_map/ppermute | solution.py:539
  43.3 29.5 %collective-permute-start.18 = (bf16[16,4096]{1,0:T(8,128)(2,1)S(1)}, bf16[16,4096]{1,0:T(8,128)(2,1)S(1)}, u32[]{:S(2)}, u32[]{:S(2)}) collective-permute-start(bf16[16,4096]{1,0:T(8,128)(2,1)S(1)} %get-tuple-element.41), channel_id=1, source_target_pairs={{0,96},{1,97},{4,100},{5,101},{8,104},{9,105},{12,108},{13,109},{2... | collective-permute-start | bytes 393224 | tf_op jit(solution)/shard_map/ppermute | solution.py:539
  45.2 27.5 %collective-permute-start.17 = (bf16[16,4096]{1,0:T(8,128)(2,1)S(1)}, bf16[16,4096]{1,0:T(8,128)(2,1)S(1)}, u32[]{:S(2)}, u32[]{:S(2)}) collective-permute-start(bf16[16,4096]{1,0:T(8,128)(2,1)S(1)} %get-tuple-element.42), channel_id=1, source_target_pairs={{0,64},{1,65},{4,68},{5,69},{8,72},{9,73},{12,76},{13,77},{2,66},{... | collective-permute-start | bytes 393224 | tf_op jit(solution)/shard_map/ppermute | solution.py:539
  56.6 8.4 %collective-permute-start.12 = (bf16[32,2048]{1,0:T(8,128)(2,1)S(1)}, bf16[32,2048]{1,0:T(8,128)(2,1)S(1)}, u32[]{:S(2)}, u32[]{:S(2)}) collective-permute-start(bf16[32,2048]{1,0:T(8,128)(2,1)S(1)} %get-tuple-element.45), channel_id=1, source_target_pairs={{0,12},{1,13},{4,0},{5,1},{8,4},{9,5},{12,8},{13,9},{2,14},{3,15},... | collective-permute-start | bytes 393224 | tf_op jit(solution)/shard_map/ppermute | solution.py:539
  56.7 8.3 %collective-permute-start.11 = (bf16[32,2048]{1,0:T(8,128)(2,1)S(1)}, bf16[32,2048]{1,0:T(8,128)(2,1)S(1)}, u32[]{:S(2)}, u32[]{:S(2)}) collective-permute-start(bf16[32,2048]{1,0:T(8,128)(2,1)S(1)} %get-tuple-element.46), channel_id=1, source_target_pairs={{0,8},{1,9},{4,12},{5,13},{8,0},{9,1},{12,4},{13,5},{2,10},{3,11},... | collective-permute-start | bytes 393224 | tf_op jit(solution)/shard_map/ppermute | solution.py:539
  57.6 8.8 %collective-permute-start.10 = (bf16[32,2048]{1,0:T(8,128)(2,1)S(1)}, bf16[32,2048]{1,0:T(8,128)(2,1)S(1)}, u32[]{:S(2)}, u32[]{:S(2)}) collective-permute-start(bf16[32,2048]{1,0:T(8,128)(2,1)S(1)} %get-tuple-element.47), channel_id=1, source_target_pairs={{0,4},{1,5},{4,8},{5,9},{8,12},{9,13},{12,0},{13,1},{2,6},{3,7},{6... | collective-permute-start | bytes 393224 | tf_op jit(solution)/shard_map/ppermute | solution.py:539
  65.0 7.8 %collective-permute-start.16 = (bf16[16,4096]{1,0:T(8,128)(2,1)S(1)}, bf16[16,4096]{1,0:T(8,128)(2,1)S(1)}, u32[]{:S(2)}, u32[]{:S(2)}) collective-permute-start(bf16[16,4096]{1,0:T(8,128)(2,1)S(1)} %get-tuple-element.43), channel_id=1, source_target_pairs={{0,32},{1,33},{4,36},{5,37},{8,40},{9,41},{12,44},{13,45},{2,34},{... | collective-permute-start | bytes 393224 | tf_op jit(solution)/shard_map/ppermute | solution.py:539
  66.4 16.0 %collective-permute-start.15 = (bf16[16,2048]{1,0:T(8,128)(2,1)S(1)}, bf16[16,2048]{1,0:T(8,128)(2,1)S(1)}, u32[]{:S(2)}, u32[]{:S(2)}) collective-permute-start(bf16[16,2048]{1,0:T(8,128)(2,1)S(1)} %get-tuple-element.52), channel_id=1, source_target_pairs={{0,3},{1,2},{4,7},{5,6},{8,11},{9,10},{12,15},{13,14},{2,1},{3,0},... | collective-permute-start | bytes 196616 | tf_op jit(solution)/shard_map/ppermute | solution.py:539
  72.8 9.7 %collective-permute-start.14 = (bf16[16,2048]{1,0:T(8,128)(2,1)S(1)}, bf16[16,2048]{1,0:T(8,128)(2,1)S(1)}, u32[]{:S(2)}, u32[]{:S(2)}) collective-permute-start(bf16[16,2048]{1,0:T(8,128)(2,1)S(1)} %get-tuple-element.52), channel_id=1, source_target_pairs={{0,1},{1,0},{4,5},{5,4},{8,9},{9,8},{12,13},{13,12},{2,3},{3,2},{6... | collective-permute-start | bytes 196616 | tf_op jit(solution)/shard_map/ppermute | solution.py:539
  72.9 9.6 %collective-permute-start.19 = (bf16[16,4096]{1,0:T(8,128)(2,1)S(1)}, bf16[16,4096]{1,0:T(8,128)(2,1)S(1)}, u32[]{:S(2)}, u32[]{:S(2)}) collective-permute-start(bf16[16,4096]{1,0:T(8,128)(2,1)S(1)} %add_up.12), channel_id=1, source_target_pairs={{0,0},{1,1},{4,32},{5,33},{8,64},{9,65},{12,96},{13,97},{2,16},{3,... | collective-permute-start | bytes 393224 | tf_op jit(solution)/shard_map/ppermute | solution.py:539
  73.5 8.9 %collective-permute-start.13 = (bf16[16,2048]{1,0:T(8,128)(2,1)S(1)}, bf16[16,2048]{1,0:T(8,128)(2,1)S(1)}, u32[]{:S(2)}, u32[]{:S(2)}) collective-permute-start(bf16[16,2048]{1,0:T(8,128)(2,1)S(1)} %get-tuple-element.51.refs_0_), channel_id=1, source_target_pairs={{0,2},{1,3},{4,6},{5,7},{8,10},{9,11},{12,14},{13,15},{2,0},{3,1},... | collective-permute-start | bytes 196616 | tf_op jit(solution)/shard_map/ppermute | solution.py:539
  82.5 8.8 %collective-permute-start.20 = (bf16[16,4096]{1,0:T(8,128)(2,1)S(1)}, bf16[16,4096]{1,0:T(8,128)(2,1)S(1)}, u32[]{:S(2)}, u32[]{:S(2)}) collective-permute-start(bf16[16,4096]{1,0:T(8,128)(2,1)S(1)} %collective-permute-done.19.refs_0_), channel_id=1, source_target_pairs={{0,2},{1,3},{4,6},{5,7},{8,10},{9,11},{12,14},{13,15},{2,0},{3,1},... | collective-permute-start | bytes 393224 | tf_op jit(solution)/shard_map/ppermute | solution.py:539
  91.5 10.6 %collective-permute-start.23 = (bf16[16,64,128]{2,1,0:T(8,128)(2,1)S(1)}, bf16[16,64,128]{2,1,0:T(8,128)(2,1)S(1)}, u32[]{:S(2)}, u32[]{:S(2)}) collective-permute-start(bf16[16,64,128]{2,1,0:T(8,128)(2,1)S(1)} %pad_maximum_fusion.1.refs_13_.grads_ref.refs_0_), channel_id=1, source_target_pairs={{0,12},{1,13},{4,0},{5,1},{8,4},{9,5},{12,8},{13,9},{2,14},{3,15},... | collective-permute-start | bytes 786440 | tf_op jit(solution)/shard_map/ppermute | solution.py:539
  91.8 10.3 %collective-permute-start.22 = (bf16[16,64,128]{2,1,0:T(8,128)(2,1)S(1)}, bf16[16,64,128]{2,1,0:T(8,128)(2,1)S(1)}, u32[]{:S(2)}, u32[]{:S(2)}) collective-permute-start(bf16[16,64,128]{2,1,0:T(8,128)(2,1)S(1)} %pad_maximum_fusion.1.refs_13_.grads_ref.refs_0_), channel_id=1, source_target_pairs={{0,4},{1,5},{4,8},{5,9},{8,12},{9,13},{12,0},{13,1},{2,6},{3,7},{6... | collective-permute-start | bytes 786440 | tf_op jit(solution)/shard_map/ppermute | solution.py:539
  93.3 9.6 %collective-permute-start.21 = (bf16[16,64,128]{2,1,0:T(8,128)(2,1)S(1)}, bf16[16,64,128]{2,1,0:T(8,128)(2,1)S(1)}, u32[]{:S(2)}, u32[]{:S(2)}) collective-permute-start(bf16[16,64,128]{2,1,0:T(8,128)(2,1)S(1)} %pad_maximum_fusion.1.refs_13_.grads_ref.refs_0_), channel_id=1, source_target_pairs={{0,8},{1,9},{4,12},{5,13},{8,0},{9,1},{12,4},{13,5},{2,10},{3,11},... | collective-permute-start | bytes 786440 | tf_op jit(solution)/shard_map/ppermute | solution.py:539
  103.7 25.4 %all-to-all-start = ((bf16[128,16,128]{2,1,0:T(8,128)(2,1)}), bf16[128,16,128]{2,1,0:T(8,128)(2,1)S(1)}, u32[]{:S(2)}, u32[]{:S(2)}) async-start(bf16[128,16,128]{2,1,0:T(8,128)(2,1)} %get-tuple-element.32), calls=%async_computation | async-start | bytes 1048576 | tf_op jit(solution)/shard_map/all_to_all | solution.py:703
  130.1 18.0 %all-to-all-start.1 = ((bf16[128,16,128]{2,1,0:T(8,128)(2,1)}), bf16[128,16,128]{2,1,0:T(8,128)(2,1)S(1)}, u32[]{:S(2)}, u32[]{:S(2)}) async-start(bf16[128,16,128]{2,1,0:T(8,128)(2,1)} %get-tuple-element.38), calls=%async_computation.1 | async-start | bytes 1048576 | tf_op jit(solution)/shard_map/all_to_all | solution.py:715
  (11 other events, 53.6 us)
